TPU v7x, 256 devices: a whole 4x4x8 slice. The times are simulated.
256 devices in a mesh: rows: 8 (over z), cols: 32 (over y, x, core).
Axes of the slice: x: 4, y: 4, z: 8, core: 2. Of those that a mesh axis runs over, the one named last changes fastest.
Arguments:
- guidance: float32 [2, 3, 512, 4096], P(None, None, 'rows', 'cols'), may hold values from -6 to 6
- seam_weight: int32 [512, 4096], P('rows', 'cols'), may hold values from 1 to 64
- source_label: int32 [512, 4096], P('rows', 'cols'), may hold values from 0 to 3
Outputs:
- solution: float32 [3, 512, 4096], P(None, 'rows', 'cols')
- residual: float32 [3, 512, 4096], P(None, 'rows', 'cols')
All inputs are finite; a program needn't handle non-finite values.
Results may differ from a plain program's by a relative error of at most 0.0003.
Values sent between devices are 32-bit elements; how exact they have to be, the bound alone decides.
No kernel may reach another device: no remote copies, remote signals or barrier semaphores. Data moves between devices by JAX's collectives and lax.ppermute only.
A program may use at most 192 MiB of HBM per device.

v0:
```python
import jax
import jax.numpy as jnp
from jax import lax
from jax.sharding import PartitionSpec as P

LEVELS = 7
SWEEPS = 2
COARSE_SWEEPS = 48
CYCLES = 2


RELAX_WEIGHT = 0.8
SEAM_FACTOR = 0.25


def extended(cells, sides, width):
    for axis, dim in sides:
        count = lax.axis_size(axis)
        ends = count - 1
        head = lax.slice_in_dim(cells, 0, width, axis=dim)
        tail = lax.slice_in_dim(cells, cells.shape[dim] - width, cells.shape[dim], axis=dim)
        cells = jnp.concatenate(
            [
                lax.ppermute(tail, axis, [(i, (i + 1) % count) for i in range(ends)]),
                cells,
                lax.ppermute(head, axis, [((i + 1) % count, i) for i in range(ends)]),
            ],
            axis=dim,
        )
    return cells


def from_behind(array, axis, by):
    count = lax.axis_size(axis)
    pairs = [(i, i + by) for i in range(count) if 0 <= i + by < count]
    return lax.ppermute(array, axis, pairs)


def conductance(weight_here, weight_near, label_here, label_near):
    matching = jnp.where(label_near == label_here, 1.0, SEAM_FACTOR)
    return (weight_here + weight_near) / 64.0 * matching


def edge_maps(padded_weight, padded_label):
    weight_here = padded_weight[1:-1, 1:-1]
    label_here = padded_label[1:-1, 1:-1]
    upward = conductance(weight_here, padded_weight[:-2, 1:-1], label_here, padded_label[:-2, 1:-1])
    downward = conductance(weight_here, padded_weight[2:, 1:-1], label_here, padded_label[2:, 1:-1])
    leftward = conductance(
        weight_here, padded_weight[1:-1, :-2], label_here, padded_label[1:-1, :-2]
    )
    rightward = conductance(
        weight_here, padded_weight[1:-1, 2:], label_here, padded_label[1:-1, 2:]
    )
    return (upward, downward, leftward, rightward)


def fold_rows(values, offset):
    blocks = values.reshape(values.shape[0] // 2, 2, values.shape[1] // 2, 2)
    return 0.5 * (blocks[:, offset, :, 0] + blocks[:, offset, :, 1])


def fold_columns(values, offset):
    blocks = values.reshape(values.shape[0] // 2, 2, values.shape[1] // 2, 2)
    return 0.5 * (blocks[:, 0, :, offset] + blocks[:, 1, :, offset])


def coarsen(conductances):
    upward, downward, leftward, rightward = conductances
    return (
        fold_rows(upward, 0),
        fold_rows(downward, 1),
        fold_columns(leftward, 0),
        fold_columns(rightward, 1),
    )


def level_entry(conductances, level_index):
    factor = 0.5**level_index
    upward, downward, leftward, rightward = conductances
    return (conductances, factor * (upward + downward + leftward + rightward), factor)


def restrict(values):
    blocks = values.reshape(values.shape[0], values.shape[1] // 2, 2, values.shape[2] // 2, 2)
    return 0.25 * (
        blocks[:, :, 0, :, 0]
        + blocks[:, :, 0, :, 1]
        + blocks[:, :, 1, :, 0]
        + blocks[:, :, 1, :, 1]
    )


def prolong(values):
    channels, height, breadth = values.shape
    spread = jnp.broadcast_to(values[:, :, None, :, None], (channels, height, 2, breadth, 2))
    return spread.reshape(channels, 2 * height, 2 * breadth)


def stencil(centre, padded, conductances, factor):
    upward, downward, leftward, rightward = conductances
    flux_sum = upward * (centre - padded[:, :-2, 1:-1]) + downward * (centre - padded[:, 2:, 1:-1])
    flux_sum = (
        flux_sum
        + leftward * (centre - padded[:, 1:-1, :-2])
        + rightward * (centre - padded[:, 1:-1, 2:])
    )
    return factor * flux_sum


def whole_apply(values, conductances, factor):
    padded = jnp.pad(values, ((0, 0), (1, 1), (1, 1)))
    return stencil(values, padded, conductances, factor)


def spread_apply(values, conductances, factor):
    padded = extended(values, (("rows", 1), ("cols", 2)), 1)
    return stencil(values, padded, conductances, factor)


def relax(source_term, iterate, entry, apply_step):
    conductances, diagonal, factor = entry
    return (
        iterate
        + RELAX_WEIGHT * (source_term - apply_step(iterate, conductances, factor)) / diagonal
    )


def whole_cycle(source_term, hierarchy, level_index):
    entry = hierarchy[level_index]
    iterate = RELAX_WEIGHT * source_term / entry[1]
    if level_index == len(hierarchy) - 1:

        def coarse_step(number, current):
            return relax(source_term, current, entry, whole_apply)

        return lax.fori_loop(0, COARSE_SWEEPS - 1, coarse_step, iterate)
    iterate = relax(source_term, iterate, entry, whole_apply)
    residual_now = source_term - whole_apply(iterate, entry[0], entry[2])
    iterate = iterate + prolong(whole_cycle(restrict(residual_now), hierarchy, level_index + 1))
    for number in range(SWEEPS):
        iterate = relax(source_term, iterate, entry, whole_apply)
    return iterate


def spread_cycle(source_term, near_levels, far_levels, level_index):
    if level_index == len(near_levels):
        gathered = lax.all_gather(source_term, "cols", axis=2, tiled=True)
        gathered = lax.all_gather(gathered, "rows", axis=1, tiled=True)
        correction = whole_cycle(gathered, far_levels, 0)
        row_start = lax.axis_index("rows") * source_term.shape[1]
        column_start = lax.axis_index("cols") * source_term.shape[2]
        zero_index = jnp.zeros((), jnp.int32)
        return lax.dynamic_slice(
            correction, (zero_index, row_start, column_start), source_term.shape
        )
    entry = near_levels[level_index]
    iterate = RELAX_WEIGHT * source_term / entry[1]
    iterate = relax(source_term, iterate, entry, spread_apply)
    residual_now = source_term - spread_apply(iterate, entry[0], entry[2])
    iterate = iterate + prolong(
        spread_cycle(restrict(residual_now), near_levels, far_levels, level_index + 1)
    )
    for number in range(SWEEPS):
        iterate = relax(source_term, iterate, entry, spread_apply)
    return iterate


def local(guidance, seam_weight, source_label):
    merge_depth = 4
    stacked = jnp.stack([seam_weight, source_label])
    rim_cells = extended(stacked, (("rows", 1), ("cols", 2)), 1)
    conductances = edge_maps(rim_cells[0].astype(jnp.float32), rim_cells[1])
    near_levels = []
    for level_index in range(merge_depth):
        if level_index > 0:
            conductances = coarsen(conductances)
        near_levels.append(level_entry(conductances, level_index))
    upward, downward, leftward, rightward = coarsen(conductances)
    upward, downward, leftward, rightward = (
        lax.all_gather(upward, "cols", axis=1, tiled=True),
        lax.all_gather(downward, "cols", axis=1, tiled=True),
        lax.all_gather(leftward, "cols", axis=1, tiled=True),
        lax.all_gather(rightward, "cols", axis=1, tiled=True),
    )
    upward, downward, leftward, rightward = (
        lax.all_gather(upward, "rows", axis=0, tiled=True),
        lax.all_gather(downward, "rows", axis=0, tiled=True),
        lax.all_gather(leftward, "rows", axis=0, tiled=True),
        lax.all_gather(rightward, "rows", axis=0, tiled=True),
    )
    conductances = (upward, downward, leftward, rightward)
    far_levels = []
    for level_index in range(merge_depth, LEVELS):
        if level_index > merge_depth:
            conductances = coarsen(conductances)
        far_levels.append(level_entry(conductances, level_index))
    upward, downward, leftward, rightward = near_levels[0][0]
    down_guide = guidance[0]
    side_guide = guidance[1]
    above_row = from_behind(down_guide[:, -1:, :], "rows", 1)
    left_column = from_behind(side_guide[:, :, -1:], "cols", 1)
    above_rows = jnp.concatenate([above_row, down_guide[:, :-1, :]], axis=1)
    beside = jnp.concatenate([left_column, side_guide[:, :, :-1]], axis=2)
    source_term = (
        upward * above_rows - downward * down_guide + leftward * beside - rightward * side_guide
    )
    solution = jnp.zeros_like(source_term)
    for number in range(CYCLES):
        if number == 0:
            residual_now = source_term
        else:
            residual_now = source_term - spread_apply(solution, near_levels[0][0], 1.0)
        solution = solution + spread_cycle(residual_now, near_levels, far_levels, 0)
    residual = source_term - spread_apply(solution, near_levels[0][0], 1.0)
    return (solution, residual)


def solution(mesh):
    return jax.shard_map(
        local,
        mesh=mesh,
        in_specs=(P(None, None, "rows", "cols"), P("rows", "cols"), P("rows", "cols")),
        out_specs=(P(None, "rows", "cols"), P(None, "rows", "cols")),
        check_vma=False,
    )
```

profile of v0, /device:TPU:1, one launch (start us, length us, event | category | flops | bytes accessed | tf_op | source)
XLA Modules:
  0.0 1306.5 jit_solution(7786494908938102644)
XLA Ops:
  1.4 4.4 collective-permute-start
  8.0 4.2 collective-permute-start.4
  12.3 4.3 collective-permute-start.5
  43.5 3.9 fusion.45
  48.6 25.9 %all-gather.4 = f32[4,1,256,1]{3,2,1,0:T(8,128)S(1)} all-gather(f32[4,1,8,1]{3,2,1,0:T(8,128)S(1)} %fusion.695), channel_id=6, replica_groups=mesh['rows'=8,'cols'=32] {'cols'}, dimensions={2}, use_global_device_ids=true | all-gather | bytes 4224 | tf_op jit(solution)/shard_map/all_gather | solution.py:182
  74.7 21.8 %all-gather.5 = f32[32,1,256,1]{2,3,1,0:T(1,128)S(1)} all-gather(f32[4,1,256,1]{2,3,1,0:T(1,128)S(1)} %copy.158), channel_id=7, replica_groups=mesh['rows'=8,'cols'=32] {'rows'}, dimensions={0}, use_global_device_ids=true | all-gather | bytes 36864 | tf_op jit(solution)/shard_map/all_gather | solution.py:188
  97.7 29.5 %all-gather.2 = f32[4,1,256,1]{3,2,1,0:T(8,128)S(1)} all-gather(f32[4,1,8,1]{3,2,1,0:T(8,128)S(1)} %fusion.696), channel_id=4, replica_groups=mesh['rows'=8,'cols'=32] {'cols'}, dimensions={2}, use_global_device_ids=true | all-gather | bytes 4224 | tf_op jit(solution)/shard_map/all_gather | solution.py:181
  127.4 18.3 %all-gather.3 = f32[32,1,256,1]{2,3,1,0:T(1,128)S(1)} all-gather(f32[4,1,256,1]{2,3,1,0:T(1,128)S(1)} %copy.157), channel_id=5, replica_groups=mesh['rows'=8,'cols'=32] {'rows'}, dimensions={0}, use_global_device_ids=true | all-gather | bytes 36864 | tf_op jit(solution)/shard_map/all_gather | solution.py:187
  149.7 30.0 %all-gather.8 = f32[4,1,256,1]{3,2,1,0:T(8,128)S(1)} all-gather(f32[4,1,8,1]{3,2,1,0:T(8,128)S(1)} %fusion.693), channel_id=10, replica_groups=mesh['rows'=8,'cols'=32] {'cols'}, dimensions={2}, use_global_device_ids=true | all-gather | bytes 4224 | tf_op jit(solution)/shard_map/all_gather | solution.py:184
  180.9 18.1 %all-gather.9 = f32[32,1,256,1]{2,3,1,0:T(1,128)S(1)} all-gather(f32[4,1,256,1]{2,3,1,0:T(1,128)S(1)} %copy.160), channel_id=11, replica_groups=mesh['rows'=8,'cols'=32] {'rows'}, dimensions={0}, use_global_device_ids=true | all-gather | bytes 36864 | tf_op jit(solution)/shard_map/all_gather | solution.py:190
  199.0 29.5 %all-gather.6 = f32[4,1,256,1]{3,2,1,0:T(8,128)S(1)} all-gather(f32[4,1,8,1]{3,2,1,0:T(8,128)S(1)} %fusion.694), channel_id=8, replica_groups=mesh['rows'=8,'cols'=32] {'cols'}, dimensions={2}, use_global_device_ids=true | all-gather | bytes 4224 | tf_op jit(solution)/shard_map/all_gather | solution.py:183
  233.1 18.1 %all-gather.7 = f32[32,1,256,1]{2,3,1,0:T(1,128)S(1)} all-gather(f32[4,1,256,1]{2,3,1,0:T(1,128)S(1)} %copy.159), channel_id=9, replica_groups=mesh['rows'=8,'cols'=32] {'rows'}, dimensions={0}, use_global_device_ids=true | all-gather | bytes 36864 | tf_op jit(solution)/shard_map/all_gather | solution.py:189
  259.4 11.4 collective-permute-start.12
  272.8 4.1 collective-permute-done.13
  277.1 7.6 reshape.696
  284.7 8.0 multiply_reduce_fusion.6
  309.0 4.1 collective-permute-start.18
  317.8 4.0 collective-permute-start.20
  338.3 5.1 collective-permute-start.24
  365.8 4.8 collective-permute-start.30
  375.3 4.4 collective-permute-start.32
  393.0 6.1 collective-permute-start.36
  405.1 36.8 %all-gather = f32[3,4,1,256,1]{4,3,2,1,0:T(8,128)S(1)} all-gather(f32[3,4,1,8,1]{4,3,2,1,0:T(8,128)S(1)} %fusion.411), channel_id=2, replica_groups=mesh['rows'=8,'cols'=32] {'cols'}, dimensions={3}, use_global_device_ids=true | all-gather | bytes 12672 | tf_op jit(solution)/shard_map/all_gather | solution.py:148
  441.9 122.1 %all-gather.1 = f32[3,32,1,256,1]{4,3,2,1,0:T(8,128)} all-gather(f32[3,4,1,256,1]{4,3,2,1,0:T(8,128)S(1)} %all-gather), channel_id=3, replica_groups=mesh['rows'=8,'cols'=32] {'rows'}, dimensions={1}, use_global_device_ids=true | all-gather | bytes 110592 | tf_op jit(solution)/shard_map/all_gather | solution.py:149
  564.0 7.9 reduce.26
  572.2 7.6 reshape.704
  579.8 8.0 multiply_reduce_fusion.4
  590.5 4.5 while.24
  599.3 5.6 reshape.711
  684.4 4.1 collective-permute-done.57
  696.2 4.3 collective-permute-start.60
  702.4 4.5 collective-permute-done.61
  710.1 5.6 reshape.715
  723.3 4.1 collective-permute-start.64
  729.4 5.2 collective-permute-done.65
  747.7 5.9 collective-permute-done.69
  766.5 6.0 collective-permute-done.73
  785.5 6.0 collective-permute-done.77
  804.4 6.0 collective-permute-done.81
  810.5 7.6 reshape.716
  818.2 8.0 multiply_reduce_fusion.2
  839.0 5.4 collective-permute-done.85
  857.7 5.0 collective-permute-done.89
  878.7 4.6 collective-permute-done.93
  891.0 4.1 collective-permute-start.96
  897.0 4.3 collective-permute-done.97
  909.6 4.3 collective-permute-start.100
  915.8 4.0 collective-permute-done.101
  927.5 4.6 collective-permute-start.104
  938.1 36.8 %all-gather.10 = f32[3,4,1,256,1]{4,3,2,1,0:T(8,128)S(1)} all-gather(f32[3,4,1,8,1]{4,3,2,1,0:T(8,128)S(1)} %fusion.349), channel_id=12, replica_groups=mesh['rows'=8,'cols'=32] {'cols'}, dimensions={3}, use_global_device_ids=true | all-gather | bytes 12672 | tf_op jit(solution)/shard_map/all_gather | solution.py:148
  974.9 122.1 %all-gather.11 = f32[3,32,1,256,1]{4,3,2,1,0:T(8,128)} all-gather(f32[3,4,1,256,1]{4,3,2,1,0:T(8,128)S(1)} %all-gather.10), channel_id=13, replica_groups=mesh['rows'=8,'cols'=32] {'rows'}, dimensions={1}, use_global_device_ids=true | all-gather | bytes 110592 | tf_op jit(solution)/shard_map/all_gather | solution.py:149
  1096.9 7.9 reduce.58
  1105.1 7.8 reshape.720
  1113.0 8.0 multiply_reduce_fusion
  1123.6 4.5 while.25
  1132.5 5.6 reshape.723
  1217.3 4.1 collective-permute-done.125
  1229.1 4.3 collective-permute-start.128
  1235.4 4.5 collective-permute-done.129
  1243.0 5.6 reshape.727
  1256.3 4.1 collective-permute-start.132
  1262.3 5.2 collective-permute-done.133
  1280.6 5.9 collective-permute-done.137
  1299.4 6.0 collective-permute-done.141
  (728 shorter events, 515.1 us)
Async XLA Ops:
  1.4 15.3 %collective-permute-start = (s32[2,1,128]{2,1,0:T(1,128)S(1)}, s32[2,1,128]{2,1,0:T(1,128)S(1)}, u32[]{:S(2)}, u32[]{:S(2)}) collective-permute-start(s32[2,1,128]{2,1,0:T(1,128)S(1)} %get-tuple-element.322), channel_id=1, source_target_pairs={{0,32},{32,64},{64,96},{96,128},{128,160},{160,192},{192,224},{1,3... | collective-permute-start | bytes 3080 | tf_op jit(solution)/shard_map/ppermute | solution.py:24
  5.7 10.9 collective-permute-start.1
  8.0 30.5 %collective-permute-start.4 = (f32[3,1,128]{2,1,0:T(1,128)S(1)}, f32[3,1,128]{2,1,0:T(1,128)S(1)}, u32[]{:S(2)}, u32[]{:S(2)}) collective-permute-start(f32[3,1,128]{2,1,0:T(1,128)S(1)} %slice.2008), channel_id=1, source_target_pairs={{0,32},{32,64},{64,96},{96,128},{128,160},{160,192},{192,224},{1,3... | collective-permute-start | bytes 4616 | tf_op jit(solution)/shard_map/ppermute | solution.py:36
  12.3 26.3 %collective-permute-start.5 = (f32[3,64,1]{2,1,0:T(8,128)S(1)}, f32[3,64,1]{2,1,0:T(8,128)S(1)}, u32[]{:S(2)}, u32[]{:S(2)}) collective-permute-start(f32[3,64,1]{2,1,0:T(8,128)S(1)} %slice.2014), channel_id=1, source_target_pairs={{0,1},{1,2},{2,3},{3,4},{4,5},{5,6},{6,7},{7,8},{8,9},{9,10},{10,1... | collective-permute-start | bytes 2312 | tf_op jit(solution)/shard_map/ppermute | solution.py:36
  19.4 5.7 collective-permute-start.3
  38.7 190.0 %collective-permute-start.6 = (f32[3,1,128]{2,1,0:T(1,128)S(1)}, f32[3,1,128]{2,1,0:T(1,128)S(1)}, u32[]{:S(2)}, u32[]{:S(2)}) collective-permute-start(f32[3,1,128]{2,1,0:T(1,128)S(1)} %get-tuple-element.318), channel_id=1, source_target_pairs={{0,32},{32,64},{64,96},{96,128},{128,160},{160,192},{192,224},{1,3... | collective-permute-start | bytes 4616 | tf_op jit(solution)/shard_map/ppermute | solution.py:24
  42.2 186.4 %collective-permute-start.7 = (f32[3,1,128]{2,1,0:T(1,128)S(1)}, f32[3,1,128]{2,1,0:T(1,128)S(1)}, u32[]{:S(2)}, u32[]{:S(2)}) collective-permute-start(f32[3,1,128]{2,1,0:T(1,128)S(1)} %get-tuple-element.319), channel_id=1, source_target_pairs={{32,0},{64,32},{96,64},{128,96},{160,128},{192,160},{224,192},{33,... | collective-permute-start | bytes 4616 | tf_op jit(solution)/shard_map/ppermute | solution.py:26
  228.8 22.4 %collective-permute-start.8 = (f32[3,66,1]{2,1,0:T(8,128)S(1)}, f32[3,66,1]{2,1,0:T(8,128)S(1)}, u32[]{:S(2)}, u32[]{:S(2)}) collective-permute-start(f32[3,66,1]{2,1,0:T(8,128)S(1)} %get-tuple-element.294), channel_id=1, source_target_pairs={{0,1},{1,2},{2,3},{3,4},{4,5},{5,6},{6,7},{7,8},{8,9},{9,10},{10,1... | collective-permute-start | bytes 2384 | tf_op jit(solution)/shard_map/ppermute | solution.py:24
  231.1 20.1 %collective-permute-start.9 = (f32[3,66,1]{2,1,0:T(8,128)S(1)}, f32[3,66,1]{2,1,0:T(8,128)S(1)}, u32[]{:S(2)}, u32[]{:S(2)}) collective-permute-start(f32[3,66,1]{2,1,0:T(8,128)S(1)} %get-tuple-element.295), channel_id=1, source_target_pairs={{1,0},{2,1},{3,2},{4,3},{5,4},{6,5},{7,6},{8,7},{9,8},{10,9},{11,1... | collective-permute-start | bytes 2384 | tf_op jit(solution)/shard_map/ppermute | solution.py:26
  259.4 13.4 %collective-permute-start.12 = (f32[3,66,1]{2,1,0:T(8,128)S(1)}, f32[3,66,1]{2,1,0:T(8,128)S(1)}, u32[]{:S(2)}, u32[]{:S(2)}) collective-permute-start(f32[3,66,1]{2,1,0:T(8,128)S(1)} %get-tuple-element.292), channel_id=1, source_target_pairs={{0,1},{1,2},{2,3},{3,4},{4,5},{5,6},{6,7},{7,8},{8,9},{9,10},{10,1... | collective-permute-start | bytes 2384 | tf_op jit(solution)/shard_map/ppermute | solution.py:24
  270.8 6.1 collective-permute-start.13
  292.8 6.8 collective-permute-start.14
  300.3 7.7 collective-permute-start.16
  303.3 5.5 collective-permute-start.17
  309.0 8.2 collective-permute-start.18
  317.8 9.8 collective-permute-start.20
  321.8 5.8 collective-permute-start.21
  330.2 5.9 collective-permute-start.22
  338.3 7.0 collective-permute-start.24
  348.8 6.4 collective-permute-start.26
  356.6 6.0 collective-permute-start.28
  359.8 5.3 collective-permute-start.29
  365.8 6.2 collective-permute-start.30
  375.3 6.4 collective-permute-start.32
  393.0 8.2 collective-permute-start.36
  399.2 5.7 collective-permute-start.37
  612.4 5.6 collective-permute-start.40
  627.7 5.4 collective-permute-start.44
  648.2 5.3 collective-permute-start.49
  661.6 5.7 collective-permute-start.52
  665.0 5.3 collective-permute-start.53
  679.0 5.3 collective-permute-start.56
  682.4 6.1 collective-permute-start.57
  696.2 6.3 collective-permute-start.60
  700.5 6.4 collective-permute-start.61
  723.3 6.0 collective-permute-start.64
  727.4 7.1 collective-permute-start.65
  742.3 5.3 collective-permute-start.68
  745.7 7.8 collective-permute-start.69
  764.6 8.0 collective-permute-start.73
  783.5 8.0 collective-permute-start.77
  802.5 7.9 collective-permute-start.81
  837.0 7.4 collective-permute-start.85
  852.1 5.6 collective-permute-start.88
  855.6 7.1 collective-permute-start.89
  872.9 5.7 collective-permute-start.92
  876.7 6.6 collective-permute-start.93
  891.0 6.0 collective-permute-start.96
  895.0 6.3 collective-permute-start.97
  909.6 6.2 collective-permute-start.100
  913.9 6.0 collective-permute-start.101
  927.5 6.6 collective-permute-start.104
  932.1 5.7 collective-permute-start.105
  1145.2 5.6 collective-permute-start.108
  1194.4 5.5 collective-permute-start.120
  1211.8 5.5 collective-permute-start.124
  1215.4 6.1 collective-permute-start.125
  1229.1 6.3 collective-permute-start.128
  1233.4 6.4 collective-permute-start.129
  1256.3 6.0 collective-permute-start.132
  1260.3 7.1 collective-permute-start.133
  1275.2 5.3 collective-permute-start.136
  1278.7 7.8 collective-permute-start.137
  1297.5 8.0 collective-permute-start.141
  (81 other events, 390.9 us)
where the time goes:
time: 1330 us; the launch traced here: 1310 us
  blocking collectives  509 us (38%)
  starting transfers between devices  372 us (28%)
  waiting for transfers between devices  228 us (17%)
  local copies, waits for them, and re-layouts  110 us (8%)
  other arithmetic  82.7 us (6%)
    ppermute x70, starting transfers between devices, extended(): lax.ppermute(tail, axis, [(i, (i + 1) % count) for i in range(ends)])  247 us
    all_gather x2, blocking collectives, spread_cycle(): gathered = lax.all_gather(gathered, 'rows', axis=1, tiled=True)  244 us
    ppermute x70, waiting for transfers between devices, extended(): lax.ppermute(head, axis, [((i + 1) % count, i) for i in range(ends)])  228 us
    ppermute x70, starting transfers between devices, extended(): lax.ppermute(head, axis, [((i + 1) % count, i) for i in range(ends)])  117 us
    all_gather x2, blocking collectives, spread_cycle(): gathered = lax.all_gather(source_term, 'cols', axis=2, tiled=True)  73.6 us
    reshape x12, local copies, waits for them, and re-layouts, restrict(): values.reshape(values.shape[0], values.shape[1] // 2, 2, values.shape[2]...  37.6 us
    mul x12, other arithmetic, restrict(): 0.25 * (blocks[:, :, 0, :, 0] + blocks[:, :, 0, :, 1] + blocks[:, :, 1, :...  36.5 us
    all_gather x1, blocking collectives, local(): lax.all_gather(rightward, 'cols', axis=1, tiled=True)  30 us
  transfers between devices with their start and end apart: 142, of which 66 were waited for; matrix products, arithmetic and copies ran while one was open for 3% of the time, Pallas kernels for 0%

commit v1 on v0

v1 whole, which is shorter than its diff:
```python
import jax
import jax.numpy as jnp
from jax import lax
from jax.experimental import pallas as pl
from jax.experimental.pallas import tpu as pltpu
from jax.sharding import Mesh, PartitionSpec as P

F32 = jnp.float32
CHANNELS = 3
COARSE_SWEEPS = 48
RELAX_WEIGHT = 0.8
SEAM_FACTOR = 0.25
PAD = 8
LANES = 128
REACH = 56
SIDES = ("y", "x", "core")
CHIPS = ("z", "y", "x")
LOCAL_ROWS = (192, 96, 48)
UP, DOWN, LEFT, RIGHT, SCALE, INVERSE = range(6)


def lane_ids(rows):
    return lax.broadcasted_iota(jnp.int32, (rows, LANES), 1)


def beside(halves, width):
    count = len(halves)
    lane = lane_ids(halves[0].shape[0])
    ahead = [pltpu.roll(x, width, 1) for x in halves]
    behind = [pltpu.roll(x, LANES - width, 1) for x in halves]
    if count == 1:
        return ahead, behind
    left = [jnp.where(lane < width, ahead[h - 1], ahead[h]) for h in range(count)]
    right = [
        jnp.where(lane >= LANES - width, behind[(h + 1) % count], behind[h]) for h in range(count)
    ]
    return left, right


def pair_sum(x, width):
    low = (lane_ids(x.shape[0]) & width) == 0
    return x + jnp.where(low, pltpu.roll(x, LANES - width, 1), pltpu.roll(x, width, 1))


def low_of_pair(x, width):
    low = (lane_ids(x.shape[0]) & width) == 0
    return jnp.where(low, x, pltpu.roll(x, width, 1))


def high_of_pair(x, width):
    low = (lane_ids(x.shape[0]) & width) == 0
    return jnp.where(low, pltpu.roll(x, LANES - width, 1), x)


def exact_dot(x, chosen):
    return lax.dot_general(
        x,
        chosen,
        (((1,), (0,)), ((), ())),
        precision=lax.Precision.HIGHEST,
        preferred_element_type=F32,
    )


def chunks(low, high, size, body):
    count = (high - low) // size
    assert count * size == high - low

    def step(i, carry):
        body(pl.multiple_of(PAD + low + i * size, 8))
        return carry

    if count == 1:
        body(PAD + low)
    else:
        lax.fori_loop(0, count, step, 0)


def stencil(mode, target, field, base, maps, low, high, size, width=1, halves=2, first=0, extra=None):
    def body(start):
        at = pl.ds(start, size)
        span = range(first, first + halves)
        coef = [[maps[m, h, at, :] for h in span] for m in range(4)]
        for c in range(CHANNELS):
            here = [field[c, h, at, :] for h in span]
            above = [field[c, h, pl.ds(start - 1, size), :] for h in span]
            below = [field[c, h, pl.ds(start + 1, size), :] for h in span]
            left, right = beside(here, width)
            for i, h in enumerate(span):
                near = (above[i], below[i], left[i], right[i])
                if mode in ("difference", "scaled_difference", "final"):
                    near = [n - here[i] for n in near]
                total = coef[0][i] * near[0] + coef[1][i] * near[1]
                total = total + (coef[2][i] * near[2] + coef[3][i] * near[3])
                if mode == "first":
                    result = (2.0 - RELAX_WEIGHT) * here[i] + total
                elif mode == "relax":
                    result = (1.0 - RELAX_WEIGHT) * here[i] + base[c, h, at, :] + total
                elif mode == "relax_add":
                    result = (1.0 - RELAX_WEIGHT) * here[i] + base[c, h, at, :] + total
                    result = extra[c, h, at, :] + result
                elif mode == "residual":
                    result = base[c, h, at, :] - RELAX_WEIGHT * here[i] + total
                    result = maps[SCALE, h, at, :] * result
                elif mode == "difference":
                    result = base[c, h, at, :] + total
                else:
                    result = maps[SCALE, h, at, :] * (base[c, h, at, :] + total)
                target[c, h, at, :] = result

    chunks(low, high, size, body)


def scaled_maps(raw, factor):
    whole = raw[0] + raw[1] + raw[2] + raw[3]
    inside = whole > 0.0
    share = jnp.where(inside, RELAX_WEIGHT / jnp.where(inside, whole, 1.0), 0.0)
    return [r * share for r in raw], whole * (factor / RELAX_WEIGHT), share * (1.0 / factor)


def even_odd(ref, lead, start, count):
    return (
        ref[lead + (pl.ds(start, count, stride=2), slice(None))],
        ref[lead + (pl.ds(start + 1, count, stride=2), slice(None))],
    )


def stack_kernel(guidance, weight, label, whole, upper, lower):
    def put(a, x):
        whole[a] = x
        upper[a] = x[:REACH]
        lower[a] = x[64 - REACH :]

    for c in range(CHANNELS):
        put(c, guidance[0, c])
        put(CHANNELS + c, guidance[1, c])
    put(6, weight[...].astype(F32))
    put(7, label[...].astype(F32))


def pack_kernel(own, above, below, to_left, to_right):
    for a in range(8):
        top = jnp.concatenate([above[a], own[a, :32]], axis=0)
        bottom = jnp.concatenate([own[a, 32:], below[a]], axis=0)
        bottom = pltpu.roll(bottom, 64, 1)
        low = lane_ids(88) < 64
        to_left[a] = jnp.where(low, top, bottom)
        to_right[a] = jnp.where(low, bottom, top)


def local_down(level, field, base, work, maps, next_base, next_maps, first_rows, rest_rows, next_rows):
    width = 2**level
    low, high, size = first_rows
    stencil("first", field, base, base, maps, low, high, size, width)
    low, high, size = rest_rows
    stencil("scaled_difference", work, field, base, maps, low, high, size, width)
    if next_base is None:
        return

    low, high, size = next_rows

    def body(start):
        at = pl.ds(start, size)
        for h in range(2):
            inverse = 0.25 * next_maps[INVERSE, h, at, :]
            for c in range(CHANNELS):
                even, odd = even_odd(work, (c, h), 2 * start - PAD, size)
                next_base[c, h, at, :] = pair_sum(even + odd, width) * inverse

    chunks(low, high, size, body)


def own_row(x):
    lane = lax.broadcasted_iota(jnp.int32, (LANES, LANES), 0)
    place = lax.broadcasted_iota(jnp.int32, (LANES, LANES), 1)
    chosen = jnp.where(lane == 8 * (place & 15), 1.0, 0.0).astype(F32)
    count = x.shape[0] // 8
    spread = exact_dot(x, chosen)
    rows = []
    keep = (lane_ids(8) >> 4) == lax.broadcasted_iota(jnp.int32, (8, LANES), 0)
    for i in range(count):
        part = jnp.where(keep, spread[8 * i : 8 * i + 8], 0.0)
        rows.append(jnp.sum(part, axis=0, keepdims=True))
    return rows


def down_levels(fields, bases, work, maps, ranges):
    for level in range(3):
        local_down(
            level,
            fields[level],
            bases[level],
            work[level],
            maps[level],
            bases[level + 1] if level < 2 else None,
            maps[level + 1] if level < 2 else None,
            *ranges[level],
        )
    tiles = []
    for c in range(CHANNELS):
        even, odd = even_odd(work[2], (c, 0), PAD + 16, 8)
        tiles.append(0.25 * pair_sum(even + odd, 4))
    return tiles


FIRST_DOWN = (
    ((8, 184, 16), (8, 184, 16), (0, 96, 32)),
    ((0, 96, 32), (0, 96, 32), (0, 48, 24)),
    ((0, 48, 24), (0, 48, 24), None),
)
LATER_DOWN = (
    ((32, 160, 32), (32, 160, 32), (16, 80, 32)),
    ((16, 80, 32), (16, 80, 32), (8, 40, 32)),
    ((8, 40, 32), (8, 40, 32), None),
)
FIRST_UP = ((32, 160, 32), (8, 88, 16), (0, 48, 24))
LATER_UP = ((56, 136, 16), (24, 72, 24), (8, 40, 32))


def clear(ref, *bounds):
    for index in range(ref.shape[0]):
        for h in range(ref.shape[1]):
            for low, high in bounds:
                ref[index, h, low:high, :] = jnp.zeros((high - low, LANES), F32)


def setup_kernel(
    place, own, above, below, from_right, from_left,
    m0, m1, m2, source, f0, g1, f1, g2, f2, message,
    cells, raw0, raw1, raw2, w0, w1, w2,
):
    row_at, col_at = place[0], place[1]
    rows_of = lambda n, low: low + lax.broadcasted_iota(jnp.int32, (n, LANES), 0)
    edge = jnp.zeros((16, LANES), F32)
    not_top, not_bottom = row_at > 0, row_at < 7
    for a in range(8):
        for h in range(2):
            cells[a, h, 0:16, :] = edge
            cells[a, h, 192:208, :] = edge
        cells[a, 0, 16:72, :] = jnp.where(not_top, above[a], 0.0)
        cells[a, 0, 72:136, :] = own[a]
        cells[a, 0, 136:192, :] = jnp.where(not_bottom, below[a], 0.0)
        low = lane_ids(88) < 64
        inside = (low & (col_at < 31)) | (~low & (col_at > 0))
        top = jnp.where(low, from_right[a], from_left[a])
        bottom = pltpu.roll(jnp.where(low, from_left[a], from_right[a]), 64, 1)
        cells[a, 1, 16:104, :] = jnp.where(inside & (not_top | (rows_of(88, 8) >= 64)), top, 0.0)
        cells[a, 1, 104:192, :] = jnp.where(
            inside & (not_bottom | (rows_of(88, 96) < 128)), bottom, 0.0
        )
    for ref in (m0, raw0, source, f0, w0):
        clear(ref, (0, 16), (192, 208))
    for ref, rows in ((m1, 96), (raw1, 96), (g1, 96), (f1, 96), (w1, 96)):
        clear(ref, (0, 8), (rows + 8, rows + 16))
    for ref, rows in ((m2, 48), (raw2, 48), (g2, 48), (f2, 48), (w2, 48)):
        clear(ref, (0, 8), (rows + 8, rows + 16))

    def fine(start):
        size = 16
        at = pl.ds(start, size)
        up_at, down_at = pl.ds(start - 1, size), pl.ds(start + 1, size)
        weights = [cells[6, h, at, :] for h in range(2)]
        labels = [cells[7, h, at, :] for h in range(2)]
        weight_sides = beside(weights, 1)
        label_sides = beside(labels, 1)
        coef = []
        for h in range(2):
            near_weights = (
                cells[6, h, up_at, :], cells[6, h, down_at, :], weight_sides[0][h], weight_sides[1][h],
            )
            near_labels = (
                cells[7, h, up_at, :], cells[7, h, down_at, :], label_sides[0][h], label_sides[1][h],
            )
            raw = []
            for m in range(4):
                matching = jnp.where(near_labels[m] == labels[h], 1.0 / 64.0, SEAM_FACTOR / 64.0)
                value = (weights[h] + near_weights[m]) * matching
                value = jnp.where(weights[h] > 0.0, value, 0.0)
                raw.append(value)
                raw0[m, h, at, :] = value
            scaled, scale, _ = scaled_maps(raw, 1.0)
            for m in range(4):
                m0[m, h, at, :] = scaled[m]
            m0[SCALE, h, at, :] = scale
            coef.append(scaled)
        for c in range(CHANNELS):
            second = [cells[CHANNELS + c, h, at, :] for h in range(2)]
            left = beside(second, 1)[0]
            for h in range(2):
                flux = coef[h][UP] * cells[c, h, up_at, :] - coef[h][DOWN] * cells[c, h, at, :]
                flux = flux + coef[h][LEFT] * left[h] - coef[h][RIGHT] * second[h]
                source[c, h, at, :] = flux

    chunks(8, 184, 16, fine)

    def coarser(raw, width, start, size, h):
        parts = []
        for m in range(4):
            even, odd = even_odd(raw, (m, h), start, size)
            if m == UP:
                parts.append(0.5 * pair_sum(even, width))
            elif m == DOWN:
                parts.append(0.5 * pair_sum(odd, width))
            elif m == LEFT:
                parts.append(0.5 * low_of_pair(even + odd, width))
            else:
                parts.append(0.5 * high_of_pair(even + odd, width))
        return parts

    for level, fine_raw, raw, maps, rows in ((1, raw0, raw1, m1, 96), (2, raw1, raw2, m2, 48)):

        def coarse(start, level=level, fine_raw=fine_raw, raw=raw, maps=maps):
            size = 16
            at = pl.ds(start, size)
            for h in range(2):
                parts = coarser(fine_raw, 2 ** (level - 1), 2 * start - PAD, size, h)
                scaled, scale, inverse = scaled_maps(parts, 0.5**level)
                for m in range(4):
                    raw[m, h, at, :] = parts[m]
                    maps[m, h, at, :] = scaled[m]
                maps[SCALE, h, at, :] = scale
                maps[INVERSE, h, at, :] = inverse

        chunks(0, rows, 16, coarse)
    tiles = down_levels((f0, f1, f2), (source, g1, g2), (w0, w1, w2), (m0, m1, m2), FIRST_DOWN)
    tiles = tiles + coarser(raw2, 4, PAD + 16, 8, 0)
    rows = own_row(jnp.concatenate(tiles, axis=0))
    for i in range(7):
        message[i : i + 1, :] = rows[i]
    message[7:8, :] = jnp.zeros((1, LANES), F32)


def unpack(place, mine, other, count, stride, ordered, put):
    core = place[2]
    for f in range(count):
        own = mine[pl.ds(f, 128, stride=stride), :]
        theirs = other[pl.ds(f, 128, stride=stride), :]
        ordered[f, pl.ds(0, 128, stride=2), :] = jnp.where(core == 0, own, theirs)
        ordered[f, pl.ds(1, 128, stride=2), :] = jnp.where(core == 0, theirs, own)
    sub = lax.broadcasted_iota(jnp.int32, (8, LANES), 0)
    part = lane_ids(8) >> 4

    def body(z, carry):
        for f in range(count):
            for group in range(4):
                x = ordered[f, pl.ds(pl.multiple_of(z * 32 + 8 * group, 8), 8), :]
                for k in (4, 2, 1):
                    same = (sub & k) == (part & k)
                    ahead = pltpu.roll(pltpu.roll(x, 8 - k, 0), 16 * k, 1)
                    if k == 4:
                        moved = ahead
                    else:
                        behind = pltpu.roll(pltpu.roll(x, k, 0), LANES - 16 * k, 1)
                        moved = jnp.where((sub & k) == 0, ahead, behind)
                    x = jnp.where(same, x, moved)
                put(f, pl.multiple_of(PAD + 8 * z, 8), group, x)
        return carry

    lax.fori_loop(0, 8, body, 0)


def halving(kind):
    lane = lax.broadcasted_iota(jnp.int32, (2 * LANES, LANES), 0)
    place = lax.broadcasted_iota(jnp.int32, (2 * LANES, LANES), 1)
    if kind == "sum":
        hit = (lane >> 1) == place
    elif kind == "low":
        hit = lane == 2 * place
    else:
        hit = lane == 2 * place + 1
    return jnp.where(hit, 1.0, 0.0).astype(F32)


def doubling():
    place = lax.broadcasted_iota(jnp.int32, (LANES, 2 * LANES), 0)
    lane = lax.broadcasted_iota(jnp.int32, (LANES, 2 * LANES), 1)
    return jnp.where((lane >> 1) == place, 1.0, 0.0).astype(F32)


def folded(halves, matrix):
    if len(halves) == 1:
        return [exact_dot(halves[0], matrix[:LANES])]
    return [
        exact_dot(jnp.concatenate(halves[i : i + 2], axis=1), matrix)
        for i in range(0, len(halves), 2)
    ]


WHOLE = {3: (4, 64, 1), 4: (2, 32, 0), 5: (1, 16, 0), 6: (1, 8, 0)}


def whole_maps(level, raw, maps):
    halves, rows, first = WHOLE[level]
    size = min(rows, 16)

    def body(start):
        at = pl.ds(start, size)
        lane = lane_ids(size)
        for i in range(halves):
            scaled, scale, inverse = scaled_maps(
                [raw[m, first + i, at, :] for m in range(4)], 0.5**level
            )
            if i == 0:
                scaled[LEFT] = jnp.where(lane == 0, 0.0, scaled[LEFT])
            if i == halves - 1:
                last = 63 if level == 6 else LANES - 1
                scaled[RIGHT] = jnp.where(lane == last, 0.0, scaled[RIGHT])
            for m in range(4):
                maps[m, first + i, at, :] = scaled[m]
            maps[SCALE, first + i, at, :] = scale
            maps[INVERSE, first + i, at, :] = inverse

    chunks(0, rows, size, body)


def coarsen_whole(level, raw, next_raw):
    halves, rows, first = WHOLE[level]
    next_halves, next_rows, next_first = WHOLE[level + 1]
    for m in range(4):
        parts = []
        for h in range(halves):
            even, odd = even_odd(raw, (m, first + h), PAD, next_rows)
            parts.append(even if m == UP else odd if m == DOWN else even + odd)
        kind = "sum" if m in (UP, DOWN) else "low" if m == LEFT else "high"
        for h, x in enumerate(folded(parts, halving(kind))):
            next_raw[m, next_first + h, PAD : PAD + next_rows, :] = 0.5 * x


def coarse_solve(base, maps):
    coef = [maps[m, 0, PAD : PAD + 8, :] for m in range(4)]
    row = lax.broadcasted_iota(jnp.int32, (8, LANES), 0)
    coef[UP] = jnp.where(row == 0, 0.0, coef[UP])
    coef[DOWN] = jnp.where(row == 7, 0.0, coef[DOWN])
    right_side = [base[c, 0, PAD : PAD + 8, :] for c in range(CHANNELS)]

    def step(number, values):
        out = []
        for c in range(CHANNELS):
            v = values[c]
            near = coef[UP] * pltpu.roll(v, 1, 0) + coef[DOWN] * pltpu.roll(v, 7, 0)
            side = coef[LEFT] * pltpu.roll(v, 1, 1) + coef[RIGHT] * pltpu.roll(v, LANES - 1, 1)
            out.append(((1.0 - RELAX_WEIGHT) * v + right_side[c]) + (near + side))
        return tuple(out)

    return lax.fori_loop(0, COARSE_SWEEPS - 1, step, tuple(right_side), unroll=True)


def whole_cycle(level, bases, fields, others, maps):
    halves, rows, first = WHOLE[level]
    base, field, other, level_maps = bases[level], fields[level], others[level], maps[level]
    size = {3: 16, 4: 32, 5: 16}[level]
    stencil("first", field, base, base, level_maps, 0, rows, size, 1, halves, first)
    stencil("residual", other, field, base, level_maps, 0, rows, size, 1, halves, first)
    next_halves, next_rows, next_first = WHOLE[level + 1]
    summed = []
    for h in range(halves):
        parts = []
        for c in range(CHANNELS):
            even, odd = even_odd(other, (c, first + h), PAD, next_rows)
            parts.append(even + odd)
        summed.append(jnp.concatenate(parts, axis=0))
    for h, x in enumerate(folded(summed, halving("sum"))):
        inverse = 0.25 * maps[level + 1][INVERSE, next_first + h, PAD : PAD + next_rows, :]
        for c in range(CHANNELS):
            part = x[c * next_rows : (c + 1) * next_rows]
            bases[level + 1][c, next_first + h, PAD : PAD + next_rows, :] = part * inverse
    if level == 5:
        coarse = coarse_solve(bases[6], maps[6])
        coarse = [jnp.concatenate(coarse, axis=0)]
    else:
        whole_cycle(level + 1, bases, fields, others, maps)
        coarse = [
            jnp.concatenate(
                [
                    fields[level + 1][c, next_first + h, PAD : PAD + next_rows, :]
                    for c in range(CHANNELS)
                ],
                axis=0,
            )
            for h in range(next_halves)
        ]
    for m, x in enumerate(coarse):
        wide = exact_dot(x, doubling())
        for i in range(min(halves, 2)):
            h = first + 2 * m + i
            for c in range(CHANNELS):
                part = wide[c * next_rows : (c + 1) * next_rows, LANES * i : LANES * (i + 1)]
                for offset in range(2):
                    at = pl.ds(PAD + offset, next_rows, stride=2)
                    field[c, h, at, :] = field[c, h, at, :] + part
    if level > 3:
        stencil("relax", other, field, base, level_maps, 0, rows, size, 1, halves, first)
        stencil("relax", field, other, base, level_maps, 0, rows, size, 1, halves, first)


def window(ref, index, place):
    group = lax.shift_right_logical(place[1], 3)
    offset = 16 * (place[1] & 7)
    at = pl.ds(pl.multiple_of(8 * place[0], 8), 24)
    lane = lane_ids(24)
    turn = lax.rem(LANES - offset, LANES)
    before, here, after = [pltpu.roll(ref[index, group + i, at, :], turn, 1) for i in range(3)]
    low = lane < 64
    fits = lane + offset < LANES
    return jnp.where(low, jnp.where(fits, here, after), jnp.where(fits, before, here))


def spread_matrix():
    place = lax.broadcasted_iota(jnp.int32, (LANES, 2 * LANES), 0)
    lane = lax.broadcasted_iota(jnp.int32, (LANES, 2 * LANES), 1)
    source = lane >> 3
    source = jnp.where(lane >= 192, source + 96, source)
    return jnp.where(place == source, 1.0, 0.0).astype(F32)


def correct_level_two(place, bases, fields, maps, f2, near_maps, near_base, near_a, near_b):
    for m in range(4):
        near_maps[m, 0, PAD : PAD + 24, :] = window(maps[3], m, place)
    edge = jnp.zeros((PAD, LANES), F32)
    for c in range(CHANNELS):
        near_base[c, 0, PAD : PAD + 24, :] = window(bases[3], c, place)
        near_a[c, 0, PAD : PAD + 24, :] = window(fields[3], c, place)
        for ref in (near_a, near_b):
            ref[c, 0, 0:PAD, :] = edge
            ref[c, 0, PAD + 24 : PAD + 32, :] = edge
    stencil("relax", near_b, near_a, near_base, near_maps, 0, 24, 24, 1, 1)
    stencil("relax", near_a, near_b, near_base, near_maps, 0, 24, 24, 1, 1)
    flat = jnp.concatenate([near_a[c, 0, PAD : PAD + 24, :] for c in range(CHANNELS)], axis=0)
    wide = exact_dot(flat, spread_matrix())
    for c in range(CHANNELS):
        for h in range(2):
            part = wide[24 * c : 24 * c + 24, LANES * h : LANES * h + LANES]
            for offset in range(2):
                at = pl.ds(PAD + offset, 24, stride=2)
                f2[c, h, at, :] = f2[c, h, at, :] + part


def add_rows(field, coarse, low, high, size):
    def body(start):
        for c in range(CHANNELS):
            for h in range(2):
                part = coarse[c, h, pl.ds(start, size), :]
                for offset in range(2):
                    at = pl.ds(2 * start - PAD + offset, size, stride=2)
                    field[c, h, at, :] = field[c, h, at, :] + part

    chunks(low, high, size, body)


def up_levels(ranges, fields, bases, works, maps, extra):
    low, high, size = ranges[2]
    stencil("relax", works[2], fields[2], bases[2], maps[2], low, high, size, 4)
    stencil("relax", fields[2], works[2], bases[2], maps[2], low, high, size, 4)
    add_rows(fields[1], fields[2], 0, 48, 24)
    low, high, size = ranges[1]
    stencil("relax", works[1], fields[1], bases[1], maps[1], low, high, size, 2)
    stencil("relax", fields[1], works[1], bases[1], maps[1], low, high, size, 2)
    add_rows(fields[0], fields[1], 0, 96, 24)
    low, high, size = ranges[0]
    stencil("relax", works[0], fields[0], bases[0], maps[0], low, high, size, 1)
    if extra is None:
        stencil("relax", fields[0], works[0], bases[0], maps[0], low, high, size, 1)
    else:
        stencil(
            "relax_add", fields[0], works[0], bases[0], maps[0], low, high, size, 1, extra=extra
        )


def copy_field(source, target):
    count, halves, rows, _ = source.shape
    for c in range(count):
        for h in range(halves):
            target[c, h] = source[c, h]


def middle_kernel(
    place, mine, other, m0, m1, m2, source, f0, g1, f1, g2, f2,
    m3, m4, m5, m6, solution, n0, h0, k1, h1, k2, h2, message,
    ordered, raw3, raw4, raw5, raw6, b3, v3, o3, b4, v4, o4, b5, v5, o5, b6,
    w0, w1, w2, near_maps, near_base, near_a, near_b,
):
    for ref in (m3, raw3, b3, v3, o3):
        rows = ref.shape[2]
        clear(ref, (0, PAD), (rows - PAD, rows))
        for index in range(ref.shape[0]):
            for h in (0, 5):
                ref[index, h] = jnp.zeros((rows, LANES), F32)
    for ref in (b4, v4, o4, b5, v5, o5):
        rows = ref.shape[2]
        clear(ref, (0, PAD), (rows - PAD, rows))
    for ref in (w0, w1, w2, n0):
        rows = ref.shape[2]
        clear(ref, (0, rows))

    def put(f, start, group, tile):
        if f < CHANNELS:
            b3[f, 1 + group, pl.ds(start, 8), :] = tile
        else:
            raw3[f - CHANNELS, 1 + group, pl.ds(start, 8), :] = tile

    unpack(place, mine, other, 7, 8, ordered, put)
    raws = {3: raw3, 4: raw4, 5: raw5, 6: raw6}
    maps = {3: m3, 4: m4, 5: m5, 6: m6}
    whole_maps(3, raw3, m3)
    for level in (3, 4, 5):
        coarsen_whole(level, raws[level], raws[level + 1])
        whole_maps(level + 1, raws[level + 1], maps[level + 1])
    scale_base(b3, m3)
    whole_cycle(
        3, {3: b3, 4: b4, 5: b5, 6: b6}, {3: v3, 4: v4, 5: v5}, {3: o3, 4: o4, 5: o5}, maps
    )
    copy_field(f0, solution)
    copy_field(f1, h1)
    copy_field(f2, h2)
    correct_level_two(
        place, {3: b3}, {3: v3}, maps, h2, near_maps, near_base, near_a, near_b
    )
    local_maps = (m0, m1, m2)
    up_levels(FIRST_UP, (solution, h1, h2), (source, g1, g2), (w0, w1, w2), local_maps, None)
    stencil("difference", n0, solution, source, m0, 32, 160, 32, 1)
    for ref in (h0, k1, k2):
        rows = ref.shape[2]
        clear(ref, (0, rows))
    tiles = down_levels((h0, h1, h2), (n0, k1, k2), (w0, w1, w2), local_maps, LATER_DOWN)
    rows = own_row(jnp.concatenate(tiles, axis=0))
    for i in range(CHANNELS):
        message[i : i + 1, :] = rows[i]


def scale_base(base, maps):
    halves, rows, first = WHOLE[3]

    def body(start):
        at = pl.ds(start, 16)
        for i in range(halves):
            inverse = maps[INVERSE, first + i, at, :]
            for c in range(CHANNELS):
                base[c, first + i, at, :] = base[c, first + i, at, :] * inverse

    chunks(0, rows, 16, body)


def last_kernel(
    place, mine, other, m0, m1, m2, source, m3, m4, m5, m6, before, n0, f0, k1, f1, k2, f2,
    solution, residual,
    ordered, b3, v3, o3, b4, v4, o4, b5, v5, o5, b6,
    h0, h1, h2, w0, w1, w2, near_maps, near_base, near_a, near_b,
):
    for ref in (b3, v3, o3):
        rows = ref.shape[2]
        clear(ref, (0, PAD), (rows - PAD, rows))
        for index in range(ref.shape[0]):
            for h in (0, 5):
                ref[index, h] = jnp.zeros((rows, LANES), F32)
    for ref in (b4, v4, o4, b5, v5, o5):
        rows = ref.shape[2]
        clear(ref, (0, PAD), (rows - PAD, rows))
    for ref in (w0, w1, w2):
        rows = ref.shape[2]
        clear(ref, (0, rows))

    def put(f, start, group, tile):
        b3[f, 1 + group, pl.ds(start, 8), :] = tile

    unpack(place, mine, other, CHANNELS, CHANNELS, ordered, put)
    maps = {3: m3, 4: m4, 5: m5, 6: m6}
    scale_base(b3, m3)
    whole_cycle(
        3, {3: b3, 4: b4, 5: b5, 6: b6}, {3: v3, 4: v4, 5: v5}, {3: o3, 4: o4, 5: o5}, maps
    )
    copy_field(f0, h0)
    copy_field(f1, h1)
    copy_field(f2, h2)
    correct_level_two(
        place, {3: b3}, {3: v3}, maps, h2, near_maps, near_base, near_a, near_b
    )
    local_maps = (m0, m1, m2)
    up_levels(LATER_UP, (h0, h1, h2), (n0, k1, k2), (w0, w1, w2), local_maps, before)
    stencil("final", w0, h0, source, m0, 64, 128, 32, 1)
    for c in range(CHANNELS):
        solution[c] = h0[c, 0, PAD + 64 : PAD + 128, :]
        residual[c] = w0[c, 0, PAD + 64 : PAD + 128, :]


def shape(*dims):
    return jax.ShapeDtypeStruct(dims, F32)


def field_shape(level, count):
    return (count, 2, LOCAL_ROWS[level] + 2 * PAD, LANES)


def whole_shape(level, count):
    halves, rows, first = WHOLE[level]
    return (count, halves + 2 * first, rows + 2 * PAD, LANES)


def call(kernel, outs, scratch, *args):
    in_specs = [pl.BlockSpec(memory_space=pltpu.VMEM) for _ in args]
    if args[0].dtype == jnp.int32 and args[0].ndim == 1:
        in_specs[0] = pl.BlockSpec(memory_space=pltpu.SMEM)
    return pl.pallas_call(
        kernel,
        out_shape=[shape(*o) for o in outs],
        in_specs=in_specs,
        out_specs=[pl.BlockSpec(memory_space=pltpu.VMEM) for _ in outs],
        scratch_shapes=[pltpu.VMEM(s, F32) for s in scratch],
        compiler_params=pltpu.CompilerParams(vmem_limit_bytes=48 * 1024 * 1024),
    )(*args)


def ring(count, step):
    return [(i, (i + step) % count) for i in range(count)]


def gathered(message):
    rows = message.shape[0]
    sent = jnp.broadcast_to(message[None], (128, rows, LANES))
    mine = lax.all_to_all(sent, CHIPS, 0, 0, tiled=True)
    mine = mine.reshape(128 * rows, LANES)
    return mine, lax.ppermute(mine, "core", ring(2, 1))


def local(guidance, seam_weight, source_label):
    place = jnp.stack(
        [lax.axis_index("z"), lax.axis_index(SIDES), lax.axis_index("core")]
    ).astype(jnp.int32)
    own, upper, lower = call(
        stack_kernel,
        [(8, 64, LANES), (8, REACH, LANES), (8, REACH, LANES)],
        [],
        guidance,
        seam_weight,
        source_label,
    )
    above = lax.ppermute(lower, "z", ring(8, 1))
    below = lax.ppermute(upper, "z", ring(8, -1))
    to_left, to_right = call(
        pack_kernel, [(8, 88, LANES)] * 2, [], own, above, below
    )
    from_right = lax.ppermute(to_left, SIDES, ring(32, -1))
    from_left = lax.ppermute(to_right, SIDES, ring(32, 1))
    fields = [field_shape(level, CHANNELS) for level in range(3)]
    maps = [field_shape(0, 5), field_shape(1, 6), field_shape(2, 6)]
    raws = [field_shape(level, 4) for level in range(3)]
    m0, m1, m2, source, f0, g1, f1, g2, f2, message = call(
        setup_kernel,
        maps + [fields[0], fields[0], fields[1], fields[1], fields[2], fields[2], (8, LANES)],
        [field_shape(0, 8)] + raws + fields,
        place, own, above, below, from_right, from_left,
    )
    mine, other = gathered(message)
    wholes = [whole_shape(level, CHANNELS) for level in (3, 4, 5) for _ in range(3)]
    wholes = wholes + [whole_shape(6, CHANNELS)]
    near = [(4, 1, 40, LANES)] + [(CHANNELS, 1, 40, LANES)] * 3
    m3, m4, m5, m6, solution, n0, h0, k1, h1, k2, h2, message = call(
        middle_kernel,
        [whole_shape(level, 6) for level in (3, 4, 5, 6)]
        + [fields[0]] * 3 + [fields[1]] * 2 + [fields[2]] * 2 + [(CHANNELS, LANES)],
        [(7, 256, LANES)] + [whole_shape(level, 4) for level in (3, 4, 5, 6)]
        + wholes + fields + near,
        place, mine, other, m0, m1, m2, source, f0, g1, f1, g2, f2,
    )
    mine, other = gathered(message)
    outs = call(
        last_kernel,
        [(CHANNELS, 64, LANES)] * 2,
        [(CHANNELS, 256, LANES)] + wholes + fields + fields + near,
        place, mine, other, m0, m1, m2, source, m3, m4, m5, m6,
        solution, n0, h0, k1, h1, k2, h2,
    )
    return tuple(outs)


def solution(mesh):
    fine = Mesh(mesh.devices.reshape(8, 4, 4, 2), ("z", "y", "x", "core"))
    return jax.shard_map(
        local,
        mesh=fine,
        in_specs=(P(None, None, "z", SIDES), P("z", SIDES), P("z", SIDES)),
        out_specs=(P(None, "z", SIDES), P(None, "z", SIDES)),
        check_vma=False,
    )
```

time: 1330 us -> 140 us (0.11); the launches traced: 1310 us -> 139 us
  blocking collectives: 509 us -> 52.9 us
  starting transfers between devices: 372 us -> 14.6 us
  waiting for transfers between devices: 228 us -> 12.8 us
  local copies, waits for them, and re-layouts: 110 us -> 17.7 us
  other arithmetic: 82.7 us -> 0.08 us
  Pallas kernels: 0 us -> 40.3 us
    all_gather x12 -> x0, blocking collectives: 509 us -> none  [the longest x2 244 us: spread_cycle(): gathered = lax.all_gather(gathered, 'rows', axis=1, tiled=True)]
    ppermute x142 -> x6, starting transfers between devices: 372 us -> 14.6 us  [the longest x2 5.51 us: gathered(): return (mine, lax.ppermute(mine, 'core', ring(2, 1)))]
    ppermute x142 -> x6, waiting for transfers between devices: 228 us -> 12.8 us  [the longest x1 5.24 us: local(): above = lax.ppermute(lower, 'z', ring(8, 1))]
    reshape x32 -> x1, local copies, waits for them, and re-layouts: 86.3 us -> 1.04 us  [gathered(): mine = mine.reshape(128 * rows, LANES)]
    all_to_all x0 -> x2, blocking collectives: none -> 52.9 us  [gathered(): mine = lax.all_to_all(sent, CHIPS, 0, 0, tiled=True)]
    mul x37 -> x0, other arithmetic: 48.2 us -> none  [the longest x12 36.5 us: restrict(): 0.25 * (blocks[:, :, 0, :, 0] + blocks[:, :, 0, :, 1] + blocks[:, :, 1, :...]
    pallas_call x0 -> x5, Pallas kernels: none -> 40.3 us  [call(): pl.pallas_call(kernel, out_shape=[shape(*o) for o in outs], in_specs=in_s...]
    unnamed x10 -> x46, local copies, waits for them, and re-layouts: 0.03 us -> 16.6 us
  transfers between devices with their start and end apart: 142 -> 6, of which waited for: 66 -> 4; matrix products, arithmetic and copies ran while one was open for 3% -> 0% of each run, Pallas kernels for 0% -> 0%
where the time goes in v1:
time: 140 us; the launch traced here: 139 us
  blocking collectives  52.9 us (38%)
  Pallas kernels  40.3 us (29%)
  local copies, waits for them, and re-layouts  17.7 us (13%)
  starting transfers between devices  14.6 us (10%)
  waiting for transfers between devices  12.8 us (9%)
    all_to_all x2, blocking collectives, gathered(): mine = lax.all_to_all(sent, CHIPS, 0, 0, tiled=True)  52.9 us
    pallas_call x5, Pallas kernels, call(): pl.pallas_call(kernel, out_shape=[shape(*o) for o in outs], in_specs=in_s...  40.3 us
    unnamed x46, local copies, waits for them, and re-layouts  16.6 us
    ppermute x2, starting transfers between devices, gathered(): return (mine, lax.ppermute(mine, 'core', ring(2, 1)))  5.51 us
    ppermute x1, waiting for transfers between devices, local(): above = lax.ppermute(lower, 'z', ring(8, 1))  5.24 us
    ppermute x1, waiting for transfers between devices, local(): from_right = lax.ppermute(to_left, SIDES, ring(32, -1))  4.94 us
    ppermute x1, starting transfers between devices, local(): below = lax.ppermute(upper, 'z', ring(8, -1))  4.03 us
  transfers between devices with their start and end apart: 6, of which 4 were waited for; matrix products, arithmetic and copies ran while one was open for 0% of the time, Pallas kernels for 0%

profile of v1, /device:TPU:1, one launch (start us, length us, event | category | flops | bytes accessed | tf_op | source)
XLA Modules:
  0.0 139.1 jit_solution(15792248400533765490)
XLA Ops:
  0.6 0.0 copy-start.12
  0.6 0.9 copy-done.12
  1.6 0.0 copy-start.21
  1.6 0.8 copy-done.21
  2.3 0.0 copy-start.22
  2.3 0.8 copy-done.22
  3.1 2.5 %collective-permute-start = (f32[8,56,128]{2,1,0:T(8,128)S(1)}, f32[8,56,128]{2,1,0:T(8,128)S(1)}, u32[]{:S(2)}, u32[]{:S(2)}) collective-permute-start(f32[8,56,128]{2,1,0:T(8,128)S(1)} %get-tuple-element.30), channel_id=1, source_target_pairs={{0,32},{32,64},{64,96},{96,128},{128,160},{160,192},{192,224},{224... | collective-permute-start | bytes 688136 | tf_op jit(solution)/shard_map/ppermute | solution.py:736
  5.7 4.0 %collective-permute-start.1 = (f32[8,56,128]{2,1,0:T(8,128)S(1)}, f32[8,56,128]{2,1,0:T(8,128)S(1)}, u32[]{:S(2)}, u32[]{:S(2)}) collective-permute-start(f32[8,56,128]{2,1,0:T(8,128)S(1)} %get-tuple-element.31), channel_id=1, source_target_pairs={{0,224},{32,0},{64,32},{96,64},{128,96},{160,128},{192,160},{224,1... | collective-permute-start | bytes 688136 | tf_op jit(solution)/shard_map/ppermute | solution.py:737
  9.7 5.2 %collective-permute-done.above = f32[8,56,128]{2,1,0:T(8,128)S(1)} collective-permute-done((f32[8,56,128]{2,1,0:T(8,128)S(1)}, f32[8,56,128]{2,1,0:T(8,128)S(1)}, u32[]{:S(2)}, u32[]{:S(2)}) %collective-permute-start) | collective-permute-done | bytes 229408 | tf_op jit(solution)/shard_map/ppermute | solution.py:736
  14.9 0.0 collective-permute-done.1.below
  14.9 0.2 shard_map.51
  15.1 1.3 collective-permute-start.2
  16.4 1.2 collective-permute-start.3
  17.6 0.1 pad_add_fusion.place
  17.7 4.9 %collective-permute-done.2.from_right = f32[8,88,128]{2,1,0:T(8,128)S(1)} collective-permute-done((f32[8,88,128]{2,1,0:T(8,128)S(1)}, f32[8,88,128]{2,1,0:T(8,128)S(1)}, u32[]{:S(2)}, u32[]{:S(2)}) %collective-permute-start.2) | collective-permute-done | bytes 360480 | tf_op jit(solution)/shard_map/ppermute | solution.py:741
  22.6 0.0 collective-permute-done.3.from_left
  22.6 7.4 %shard_map.52 = (f32[5,2,208,128]{3,2,1,0:T(8,128)S(1)}, f32[6,2,112,128]{3,2,1,0:T(8,128)S(1)}, f32[6,2,64,128]{3,2,1,0:T(8,128)S(1)}, f32[3,2,208,128]{3,2,1,0...) custom-call(s32[3]{0:T(128)S(1)} %pad_add_fusion.place, ...), custom_call_target="tpu_custom_call" | custom-call | tf_op jit(solution)/shard_map/pallas_call | solution.py:702
  30.0 0.0 copy-start
  30.0 1.0 copy-done
  31.0 0.0 copy-start.1
  31.0 0.8 copy-done.1
  31.8 0.0 copy-start.3
  31.8 0.8 copy-done.3
  32.7 0.0 copy-start.7
  32.7 32.7 %all_to_all.10 = f32[128,8,128]{2,1,0:T(8,128)S(1)} all-to-all(f32[128,8,128]{2,1,0:T(8,128)S(1)} %broadcast_in_dim.4), channel_id=1, replica_groups=mesh['z'=8,'y'=4,'x'=4,'core'=2] {'z','y','x'}, dimensions={0} | all-to-all | bytes 1048576 | tf_op jit(solution)/shard_map/all_to_all | solution.py:719
  65.4 3.3 %collective-permute-start.4 = (f32[1024,128]{1,0:T(8,128)S(1)}, f32[1024,128]{1,0:T(8,128)S(1)}, u32[]{:S(2)}, u32[]{:S(2)}) collective-permute-start(f32[1024,128]{1,0:T(8,128)S(1)} %bitcast.4), channel_id=1, source_target_pairs={{0,1},{1,0},{2,3},{3,2},{4,5},{5,4},{6,7},{7,6},{8,9},{9,8},{10,11... | collective-permute-start | bytes 1572872 | tf_op jit(solution)/shard_map/ppermute | solution.py:721
  68.7 1.5 %collective-permute-done.4.other = f32[1024,128]{1,0:T(8,128)S(1)} collective-permute-done((f32[1024,128]{1,0:T(8,128)S(1)}, f32[1024,128]{1,0:T(8,128)S(1)}, u32[]{:S(2)}, u32[]{:S(2)}) %collective-permute-start.4) | collective-permute-done | bytes 524320 | tf_op jit(solution)/shard_map/ppermute | solution.py:721
  70.2 0.0 copy-done.7
  70.2 19.4 %shard_map.53 = (f32[6,6,80,128]{3,2,1,0:T(8,128)}, f32[6,2,48,128]{3,2,1,0:T(8,128)S(1)}, f32[6,1,32,128]{3,2,1,0:T(8,128)S(1)}, f32[6,1,24,128]{3,2,1,0:T(8,12...) custom-call(s32[3]{0:T(128)S(1)} %pad_add_fusion.place, ...), custom_call_target="tpu_custom_call" | custom-call | tf_op jit(solution)/shard_map/pallas_call | solution.py:702
  89.6 0.0 copy-start.5
  89.6 0.8 copy-done.5
  90.4 0.0 copy-start.8
  90.4 0.7 copy-done.8
  91.2 0.0 copy-start.10
  91.2 0.7 copy-done.10
  91.9 0.0 copy-start.15
  91.9 0.7 copy-done.15
  92.6 0.0 copy-start.17
  92.6 0.6 copy-done.17
  93.2 0.0 copy-start.19
  93.2 0.6 copy-done.19
  93.8 0.0 copy-start.13
  93.8 0.0 copy-start.2
  93.9 0.6 copy-done.13
  94.5 20.2 %all_to_all.11 = f32[128,3,128]{2,1,0:T(4,128)} all-to-all(f32[128,3,128]{2,1,0:T(4,128)S(1)} %broadcast_in_dim.5), channel_id=1, replica_groups=mesh['z'=8,'y'=4,'x'=4,'core'=2] {'z','y','x'}, dimensions={0} | all-to-all | bytes 393216 | tf_op jit(solution)/shard_map/all_to_all | solution.py:719
  114.7 1.0 reshape.13.mine
  115.8 2.2 %collective-permute-start.5 = (f32[384,128]{1,0:T(8,128)S(1)}, f32[384,128]{1,0:T(8,128)S(1)}, u32[]{:S(2)}, u32[]{:S(2)}) collective-permute-start(f32[384,128]{1,0:T(8,128)S(1)} %reshape.13.mine), channel_id=1, source_target_pairs={{0,1},{1,0},{2,3},{3,2},{4,5},{5,4},{6,7},{7,6},{8,9},{9,8},{10,11... | collective-permute-start | bytes 589832 | tf_op jit(solution)/shard_map/ppermute | solution.py:721
  118.0 1.1 collective-permute-done.5.other
  119.0 0.0 copy-done.4
  119.0 0.0 copy-done.2
  119.0 1.1 copy-done.6
  120.1 0.0 copy-start.9
  120.1 1.0 copy-done.9
  121.1 0.0 copy-start.11
  121.1 1.0 copy-done.11
  122.1 0.0 copy-start.14
  122.1 0.9 copy-done.14
  123.0 0.0 copy-start.16
  123.0 0.9 copy-done.16
  123.9 0.0 copy-start.18
  123.9 0.9 copy-done.18
  124.8 0.0 copy-start.20
  124.8 0.9 copy-done.20
  125.7 13.4 %shard_map.54 = (f32[3,64,128]{2,1,0:T(8,128)}, f32[3,64,128]{2,1,0:T(8,128)}) custom-call(s32[3]{0:T(128)S(1)} %pad_add_fusion.place, f32[384,128]{1,0:T(8,128)S(1)} %reshape.13.mine, f32[384,128]{1,0:T(8,128)S(1)} %collective-permute-done.5.other, f32[5,2,208,128]{3,2,1,0:T(8,128)} %copy-done, f32[6,2,112,128]{3,2,1,0:T(8,128)S(1)} %copy-done.2, ...), custom_call_target="tpu_custom_call" | custom-call | tf_op jit(solution)/shard_map/pallas_call | solution.py:702
  (5 shorter events, 0.1 us)
Async XLA Ops:
  0.6 0.9 copy-start.12
  1.6 0.8 copy-start.21
  2.3 0.8 copy-start.22
  3.1 11.8 %collective-permute-start = (f32[8,56,128]{2,1,0:T(8,128)S(1)}, f32[8,56,128]{2,1,0:T(8,128)S(1)}, u32[]{:S(2)}, u32[]{:S(2)}) collective-permute-start(f32[8,56,128]{2,1,0:T(8,128)S(1)} %get-tuple-element.30), channel_id=1, source_target_pairs={{0,32},{32,64},{64,96},{96,128},{128,160},{160,192},{192,224},{224... | collective-permute-start | bytes 688136 | tf_op jit(solution)/shard_map/ppermute | solution.py:736
  5.7 9.3 %collective-permute-start.1 = (f32[8,56,128]{2,1,0:T(8,128)S(1)}, f32[8,56,128]{2,1,0:T(8,128)S(1)}, u32[]{:S(2)}, u32[]{:S(2)}) collective-permute-start(f32[8,56,128]{2,1,0:T(8,128)S(1)} %get-tuple-element.31), channel_id=1, source_target_pairs={{0,224},{32,0},{64,32},{96,64},{128,96},{160,128},{192,160},{224,1... | collective-permute-start | bytes 688136 | tf_op jit(solution)/shard_map/ppermute | solution.py:737
  15.1 7.5 %collective-permute-start.2 = (f32[8,88,128]{2,1,0:T(8,128)S(1)}, f32[8,88,128]{2,1,0:T(8,128)S(1)}, u32[]{:S(2)}, u32[]{:S(2)}) collective-permute-start(f32[8,88,128]{2,1,0:T(8,128)S(1)} %get-tuple-element.32), channel_id=1, source_target_pairs={{0,31},{1,0},{2,1},{3,2},{4,3},{5,4},{6,5},{7,6},{8,7},{9,8},{10,9... | collective-permute-start | bytes 1081352 | tf_op jit(solution)/shard_map/ppermute | solution.py:741
  16.4 6.2 %collective-permute-start.3 = (f32[8,88,128]{2,1,0:T(8,128)S(1)}, f32[8,88,128]{2,1,0:T(8,128)S(1)}, u32[]{:S(2)}, u32[]{:S(2)}) collective-permute-start(f32[8,88,128]{2,1,0:T(8,128)S(1)} %get-tuple-element.33), channel_id=1, source_target_pairs={{0,1},{1,2},{2,3},{3,4},{4,5},{5,6},{6,7},{7,8},{8,9},{9,10},{10,1... | collective-permute-start | bytes 1081352 | tf_op jit(solution)/shard_map/ppermute | solution.py:742
  30.0 1.0 copy-start
  31.0 0.8 copy-start.1
  31.8 0.8 copy-start.3
  32.7 37.6 %copy-start.7 = (f32[3,2,208,128]{3,2,1,0:T(8,128)}, f32[3,2,208,128]{3,2,1,0:T(8,128)S(1)}, u32[]{:S(2)}) copy-start(f32[3,2,208,128]{3,2,1,0:T(8,128)S(1)} %get-tuple-element.39.f0) | copy-start | bytes 1916932
  65.4 4.9 %collective-permute-start.4 = (f32[1024,128]{1,0:T(8,128)S(1)}, f32[1024,128]{1,0:T(8,128)S(1)}, u32[]{:S(2)}, u32[]{:S(2)}) collective-permute-start(f32[1024,128]{1,0:T(8,128)S(1)} %bitcast.4), channel_id=1, source_target_pairs={{0,1},{1,0},{2,3},{3,2},{4,5},{5,4},{6,7},{7,6},{8,9},{9,8},{10,11... | collective-permute-start | bytes 1572872 | tf_op jit(solution)/shard_map/ppermute | solution.py:721
  70.2 48.8 %copy-start.4 = (f32[3,2,208,128]{3,2,1,0:T(8,128)S(1)}, f32[3,2,208,128]{3,2,1,0:T(8,128)}, u32[]{:S(2)}) copy-start(f32[3,2,208,128]{3,2,1,0:T(8,128)} %copy-done.3) | copy-start | bytes 1916932
  89.6 0.8 copy-start.5
  90.4 0.7 copy-start.8
  91.2 0.7 copy-start.10
  91.9 0.7 copy-start.15
  92.6 0.6 copy-start.17
  93.2 0.6 copy-start.19
  93.8 0.7 copy-start.13
  93.8 25.2 %copy-start.2 = (f32[6,2,112,128]{3,2,1,0:T(8,128)S(1)}, f32[6,2,112,128]{3,2,1,0:T(8,128)}, u32[]{:S(2)}) copy-start(f32[6,2,112,128]{3,2,1,0:T(8,128)} %copy-done.1) | copy-start | bytes 2064388
  115.8 3.3 %collective-permute-start.5 = (f32[384,128]{1,0:T(8,128)S(1)}, f32[384,128]{1,0:T(8,128)S(1)}, u32[]{:S(2)}, u32[]{:S(2)}) collective-permute-start(f32[384,128]{1,0:T(8,128)S(1)} %reshape.13.mine), channel_id=1, source_target_pairs={{0,1},{1,0},{2,3},{3,2},{4,5},{5,4},{6,7},{7,6},{8,9},{9,8},{10,11... | collective-permute-start | bytes 589832 | tf_op jit(solution)/shard_map/ppermute | solution.py:721
  119.0 1.1 copy-start.6
  120.1 1.0 copy-start.9
  121.1 1.0 copy-start.11
  122.1 0.9 copy-start.14
  123.0 0.9 copy-start.16
  123.9 0.9 copy-start.18
  124.8 0.9 copy-start.20

commit v2 on v1

--- a/solution.py
+++ b/solution.py
@@ -125,7 +125,20 @@
     )
 
 
-def stack_kernel(guidance, weight, label, whole, upper, lower):
+def stack_kernel(
+    guidance_in, weight_in, label_in, whole, upper, lower, guidance, weight, label, arrived
+):
+    copies = [
+        pltpu.make_async_copy(source, target, arrived.at[i])
+        for i, (source, target) in enumerate(
+            ((guidance_in, guidance), (weight_in, weight), (label_in, label))
+        )
+    ]
+    for copy in copies:
+        copy.start()
+    for copy in copies:
+        copy.wait()
+
     def put(a, x):
         whole[a] = x
         upper[a] = x[:REACH]
@@ -204,17 +217,17 @@
 
 
 FIRST_DOWN = (
-    ((8, 184, 16), (8, 184, 16), (0, 96, 32)),
-    ((0, 96, 32), (0, 96, 32), (0, 48, 24)),
-    ((0, 48, 24), (0, 48, 24), None),
+    ((8, 184, 176), (8, 184, 176), (0, 96, 96)),
+    ((0, 96, 96), (0, 96, 96), (0, 48, 48)),
+    ((0, 48, 48), (0, 48, 48), None),
 )
 LATER_DOWN = (
-    ((32, 160, 32), (32, 160, 32), (16, 80, 32)),
-    ((16, 80, 32), (16, 80, 32), (8, 40, 32)),
+    ((32, 160, 128), (32, 160, 128), (16, 80, 64)),
+    ((16, 80, 64), (16, 80, 64), (8, 40, 32)),
     ((8, 40, 32), (8, 40, 32), None),
 )
-FIRST_UP = ((32, 160, 32), (8, 88, 16), (0, 48, 24))
-LATER_UP = ((56, 136, 16), (24, 72, 24), (8, 40, 32))
+FIRST_UP = ((32, 160, 128), (8, 88, 80), (0, 48, 48))
+LATER_UP = ((56, 136, 80), (24, 72, 48), (8, 40, 32))
 
 
 def clear(ref, *bounds):
@@ -256,7 +269,7 @@
         clear(ref, (0, 8), (rows + 8, rows + 16))
 
     def fine(start):
-        size = 16
+        size = 176
         at = pl.ds(start, size)
         up_at, down_at = pl.ds(start - 1, size), pl.ds(start + 1, size)
         weights = [cells[6, h, at, :] for h in range(2)]
@@ -291,7 +304,7 @@
                 flux = flux + coef[h][LEFT] * left[h] - coef[h][RIGHT] * second[h]
                 source[c, h, at, :] = flux
 
-    chunks(8, 184, 16, fine)
+    chunks(8, 184, 176, fine)
 
     def coarser(raw, width, start, size, h):
         parts = []
@@ -309,8 +322,8 @@
 
     for level, fine_raw, raw, maps, rows in ((1, raw0, raw1, m1, 96), (2, raw1, raw2, m2, 48)):
 
-        def coarse(start, level=level, fine_raw=fine_raw, raw=raw, maps=maps):
-            size = 16
+        def coarse(start, level=level, fine_raw=fine_raw, raw=raw, maps=maps, rows=rows):
+            size = rows
             at = pl.ds(start, size)
             for h in range(2):
                 parts = coarser(fine_raw, 2 ** (level - 1), 2 * start - PAD, size, h)
@@ -321,13 +334,16 @@
                 maps[SCALE, h, at, :] = scale
                 maps[INVERSE, h, at, :] = inverse
 
-        chunks(0, rows, 16, coarse)
+        chunks(0, rows, rows, coarse)
     tiles = down_levels((f0, f1, f2), (source, g1, g2), (w0, w1, w2), (m0, m1, m2), FIRST_DOWN)
-    tiles = tiles + coarser(raw2, 4, PAD + 16, 8, 0)
-    rows = own_row(jnp.concatenate(tiles, axis=0))
-    for i in range(7):
+    upward, downward, leftward, rightward = coarser(raw2, 4, PAD + 16, 8, 0)
+    row = lax.broadcasted_iota(jnp.int32, (8, LANES), 0)
+    cell = lane_ids(8) >> 3
+    turned = pltpu.roll(pltpu.roll(rightward, LANES - 8, 1), 7, 0)
+    ends = jnp.where(row == 7, downward, jnp.where(cell == 15, rightward, turned))
+    rows = own_row(jnp.concatenate(tiles + [upward, leftward, ends], axis=0))
+    for i in range(6):
         message[i : i + 1, :] = rows[i]
-    message[7:8, :] = jnp.zeros((1, LANES), F32)
 
 
 def unpack(place, mine, other, count, stride, ordered, put):
@@ -340,10 +356,10 @@
     sub = lax.broadcasted_iota(jnp.int32, (8, LANES), 0)
     part = lane_ids(8) >> 4
 
-    def body(z, carry):
+    for z in range(8):
         for f in range(count):
             for group in range(4):
-                x = ordered[f, pl.ds(pl.multiple_of(z * 32 + 8 * group, 8), 8), :]
+                x = ordered[f, pl.ds(z * 32 + 8 * group, 8), :]
                 for k in (4, 2, 1):
                     same = (sub & k) == (part & k)
                     ahead = pltpu.roll(pltpu.roll(x, 8 - k, 0), 16 * k, 1)
@@ -353,10 +369,7 @@
                         behind = pltpu.roll(pltpu.roll(x, k, 0), LANES - 16 * k, 1)
                         moved = jnp.where((sub & k) == 0, ahead, behind)
                     x = jnp.where(same, x, moved)
-                put(f, pl.multiple_of(PAD + 8 * z, 8), group, x)
-        return carry
-
-    lax.fori_loop(0, 8, body, 0)
+                put(f, PAD + 8 * z, group, x)
 
 
 def halving(kind):
@@ -391,7 +404,7 @@
 
 def whole_maps(level, raw, maps):
     halves, rows, first = WHOLE[level]
-    size = min(rows, 16)
+    size = rows
 
     def body(start):
         at = pl.ds(start, size)
@@ -426,29 +439,78 @@
             next_raw[m, next_first + h, PAD : PAD + next_rows, :] = 0.5 * x
 
 
-def coarse_solve(base, maps):
+def one_sweep(maps):
     coef = [maps[m, 0, PAD : PAD + 8, :] for m in range(4)]
     row = lax.broadcasted_iota(jnp.int32, (8, LANES), 0)
     coef[UP] = jnp.where(row == 0, 0.0, coef[UP])
     coef[DOWN] = jnp.where(row == 7, 0.0, coef[DOWN])
+    steps = ((-1, 0), (1, 0), (0, -1), (0, 1))
+    return dict(zip(steps, coef))
+
+
+def moved(x, rows, columns):
+    if rows:
+        x = pltpu.roll(x, (-rows) % 8, 0)
+    if columns:
+        x = pltpu.roll(x, (-columns) % LANES, 1)
+    return x
+
+
+DIAMOND = [(a, b) for a in range(-4, 5) for b in range(-4, 5) if abs(a) + abs(b) <= 4]
+
+
+def four_sweeps(maps, product):
+    sweep = one_sweep(maps)
+    whole = dict(sweep)
+    whole[0, 0] = jnp.full((8, LANES), 1.0 - RELAX_WEIGHT, F32)
+    for _ in range(3):
+        grown = {at: (1.0 - RELAX_WEIGHT) * x for at, x in whole.items()}
+        for step, coef in sweep.items():
+            for at, x in whole.items():
+                place = (at[0] + step[0], at[1] + step[1])
+                term = coef * moved(x, *step)
+                grown[place] = grown[place] + term if place in grown else term
+        whole = grown
+    for i, at in enumerate(DIAMOND):
+        product[i] = moved(whole[at], -at[0], 0)
+
+
+def coarse_solve(base, maps, product):
+    sweep = one_sweep(maps)
     right_side = [base[c, 0, PAD : PAD + 8, :] for c in range(CHANNELS)]
-
-    def step(number, values):
-        out = []
+    first = right_side
+    for _ in range(3):
+        first = [
+            (1.0 - RELAX_WEIGHT) * v + g + sum(coef * moved(v, *at) for at, coef in sweep.items())
+            for v, g in zip(first, right_side)
+        ]
+    values = first
+    for _ in range(COARSE_SWEEPS // 4 - 1):
+        lanes = [[moved(v, 0, b) for b in range(-4, 5)] for v in values]
+        totals = [list() for _ in range(CHANNELS)]
+        for a in range(-4, 5):
+            sums = [None] * CHANNELS
+            for i, at in enumerate(DIAMOND):
+                if at[0] == a:
+                    coef = product[i]
+                    for c in range(CHANNELS):
+                        term = coef * lanes[c][at[1] + 4]
+                        sums[c] = term if sums[c] is None else sums[c] + term
+            for c in range(CHANNELS):
+                totals[c].append(moved(sums[c], a, 0))
+        values = []
         for c in range(CHANNELS):
-            v = values[c]
-            near = coef[UP] * pltpu.roll(v, 1, 0) + coef[DOWN] * pltpu.roll(v, 7, 0)
-            side = coef[LEFT] * pltpu.roll(v, 1, 1) + coef[RIGHT] * pltpu.roll(v, LANES - 1, 1)
-            out.append(((1.0 - RELAX_WEIGHT) * v + right_side[c]) + (near + side))
-        return tuple(out)
-
-    return lax.fori_loop(0, COARSE_SWEEPS - 1, step, tuple(right_side), unroll=True)
-
-
-def whole_cycle(level, bases, fields, others, maps):
+            t = totals[c]
+            even = (t[0] + t[1]) + (t[2] + t[3])
+            odd = (t[5] + t[6]) + (t[7] + t[8])
+            values.append((first[c] + t[4]) + (even + odd))
+    return values
+
+
+def whole_cycle(level, bases, fields, others, maps, product):
     halves, rows, first = WHOLE[level]
     base, field, other, level_maps = bases[level], fields[level], others[level], maps[level]
-    size = {3: 16, 4: 32, 5: 16}[level]
+    size = rows
     stencil("first", field, base, base, level_maps, 0, rows, size, 1, halves, first)
     stencil("residual", other, field, base, level_maps, 0, rows, size, 1, halves, first)
     next_halves, next_rows, next_first = WHOLE[level + 1]
@@ -465,10 +527,10 @@
             part = x[c * next_rows : (c + 1) * next_rows]
             bases[level + 1][c, next_first + h, PAD : PAD + next_rows, :] = part * inverse
     if level == 5:
-        coarse = coarse_solve(bases[6], maps[6])
+        coarse = coarse_solve(bases[6], maps[6], product)
         coarse = [jnp.concatenate(coarse, axis=0)]
     else:
-        whole_cycle(level + 1, bases, fields, others, maps)
+        whole_cycle(level + 1, bases, fields, others, maps, product)
         coarse = [
             jnp.concatenate(
                 [
@@ -551,11 +613,11 @@
     low, high, size = ranges[2]
     stencil("relax", works[2], fields[2], bases[2], maps[2], low, high, size, 4)
     stencil("relax", fields[2], works[2], bases[2], maps[2], low, high, size, 4)
-    add_rows(fields[1], fields[2], 0, 48, 24)
+    add_rows(fields[1], fields[2], 0, 48, 48)
     low, high, size = ranges[1]
     stencil("relax", works[1], fields[1], bases[1], maps[1], low, high, size, 2)
     stencil("relax", fields[1], works[1], bases[1], maps[1], low, high, size, 2)
-    add_rows(fields[0], fields[1], 0, 96, 24)
+    add_rows(fields[0], fields[1], 0, 96, 96)
     low, high, size = ranges[0]
     stencil("relax", works[0], fields[0], bases[0], maps[0], low, high, size, 1)
     if extra is None:
@@ -573,9 +635,25 @@
             target[c, h] = source[c, h]
 
 
+def complete_maps(raw):
+    size = 64
+    at = pl.ds(PAD, size)
+    lane = lane_ids(size)
+    row = lax.broadcasted_iota(jnp.int32, (size, LANES), 0)
+    ends = [raw[RIGHT, h, at, :] for h in range(1, 5)]
+    shifted = beside([raw[LEFT, h, at, :] for h in range(1, 5)], 1)[1]
+    last = ends[3]
+    last = jnp.where((row & 7) == 7, pltpu.roll(pltpu.roll(last, 1, 1), 1, 0), last)
+    shifted[3] = jnp.where(lane == LANES - 1, last, shifted[3])
+    for i in range(4):
+        below = raw[UP, 1 + i, pl.ds(PAD + 1, size), :]
+        raw[DOWN, 1 + i, at, :] = jnp.where(row == size - 1, ends[i], below)
+        raw[RIGHT, 1 + i, at, :] = shifted[i]
+
+
 def middle_kernel(
     place, mine, other, m0, m1, m2, source, f0, g1, f1, g2, f2,
-    m3, m4, m5, m6, solution, n0, h0, k1, h1, k2, h2, message,
+    m3, m4, m5, m6, product, solution, n0, h0, k1, h1, k2, h2, message,
     ordered, raw3, raw4, raw5, raw6, b3, v3, o3, b4, v4, o4, b5, v5, o5, b6,
     w0, w1, w2, near_maps, near_base, near_a, near_b,
 ):
@@ -596,18 +674,22 @@
         if f < CHANNELS:
             b3[f, 1 + group, pl.ds(start, 8), :] = tile
         else:
-            raw3[f - CHANNELS, 1 + group, pl.ds(start, 8), :] = tile
-
-    unpack(place, mine, other, 7, 8, ordered, put)
+            slot = (UP, LEFT, RIGHT)[f - CHANNELS]
+            raw3[slot, 1 + group, pl.ds(start, 8), :] = tile
+
+    unpack(place, mine, other, 6, 6, ordered, put)
+    complete_maps(raw3)
     raws = {3: raw3, 4: raw4, 5: raw5, 6: raw6}
     maps = {3: m3, 4: m4, 5: m5, 6: m6}
     whole_maps(3, raw3, m3)
     for level in (3, 4, 5):
         coarsen_whole(level, raws[level], raws[level + 1])
         whole_maps(level + 1, raws[level + 1], maps[level + 1])
+    four_sweeps(m6, product)
     scale_base(b3, m3)
     whole_cycle(
-        3, {3: b3, 4: b4, 5: b5, 6: b6}, {3: v3, 4: v4, 5: v5}, {3: o3, 4: o4, 5: o5}, maps
+        3, {3: b3, 4: b4, 5: b5, 6: b6}, {3: v3, 4: v4, 5: v5}, {3: o3, 4: o4, 5: o5}, maps,
+        product,
     )
     copy_field(f0, solution)
     copy_field(f1, h1)
@@ -617,7 +699,7 @@
     )
     local_maps = (m0, m1, m2)
     up_levels(FIRST_UP, (solution, h1, h2), (source, g1, g2), (w0, w1, w2), local_maps, None)
-    stencil("difference", n0, solution, source, m0, 32, 160, 32, 1)
+    stencil("difference", n0, solution, source, m0, 32, 160, 128, 1)
     for ref in (h0, k1, k2):
         rows = ref.shape[2]
         clear(ref, (0, rows))
@@ -631,17 +713,17 @@
     halves, rows, first = WHOLE[3]
 
     def body(start):
-        at = pl.ds(start, 16)
+        at = pl.ds(start, rows)
         for i in range(halves):
             inverse = maps[INVERSE, first + i, at, :]
             for c in range(CHANNELS):
                 base[c, first + i, at, :] = base[c, first + i, at, :] * inverse
 
-    chunks(0, rows, 16, body)
+    chunks(0, rows, rows, body)
 
 
 def last_kernel(
-    place, mine, other, m0, m1, m2, source, m3, m4, m5, m6, before, n0, f0, k1, f1, k2, f2,
+    place, mine, other, m0, m1, m2, source, m3, m4, m5, m6, product, before, n0, f0, k1, f1, k2, f2,
     solution, residual,
     ordered, b3, v3, o3, b4, v4, o4, b5, v5, o5, b6,
     h0, h1, h2, w0, w1, w2, near_maps, near_base, near_a, near_b,
@@ -666,7 +748,8 @@
     maps = {3: m3, 4: m4, 5: m5, 6: m6}
     scale_base(b3, m3)
     whole_cycle(
-        3, {3: b3, 4: b4, 5: b5, 6: b6}, {3: v3, 4: v4, 5: v5}, {3: o3, 4: o4, 5: o5}, maps
+        3, {3: b3, 4: b4, 5: b5, 6: b6}, {3: v3, 4: v4, 5: v5}, {3: o3, 4: o4, 5: o5}, maps,
+        product,
     )
     copy_field(f0, h0)
     copy_field(f1, h1)
@@ -676,7 +759,7 @@
     )
     local_maps = (m0, m1, m2)
     up_levels(LATER_UP, (h0, h1, h2), (n0, k1, k2), (w0, w1, w2), local_maps, before)
-    stencil("final", w0, h0, source, m0, 64, 128, 32, 1)
+    stencil("final", w0, h0, source, m0, 64, 128, 64, 1)
     for c in range(CHANNELS):
         solution[c] = h0[c, 0, PAD + 64 : PAD + 128, :]
         residual[c] = w0[c, 0, PAD + 64 : PAD + 128, :]
@@ -705,7 +788,7 @@
         in_specs=in_specs,
         out_specs=[pl.BlockSpec(memory_space=pltpu.VMEM) for _ in outs],
         scratch_shapes=[pltpu.VMEM(s, F32) for s in scratch],
-        compiler_params=pltpu.CompilerParams(vmem_limit_bytes=48 * 1024 * 1024),
+        compiler_params=pltpu.CompilerParams(vmem_limit_bytes=14 * 1024 * 1024),
     )(*args)
 
 
@@ -715,7 +798,7 @@
 
 def gathered(message):
     rows = message.shape[0]
-    sent = jnp.broadcast_to(message[None], (128, rows, LANES))
+    sent = jnp.broadcast_to(message.reshape(1, 1, rows * LANES), (128, 1, rows * LANES))
     mine = lax.all_to_all(sent, CHIPS, 0, 0, tiled=True)
     mine = mine.reshape(128 * rows, LANES)
     return mine, lax.ppermute(mine, "core", ring(2, 1))
@@ -725,14 +808,19 @@
     place = jnp.stack(
         [lax.axis_index("z"), lax.axis_index(SIDES), lax.axis_index("core")]
     ).astype(jnp.int32)
-    own, upper, lower = call(
+    own, upper, lower = pl.pallas_call(
         stack_kernel,
-        [(8, 64, LANES), (8, REACH, LANES), (8, REACH, LANES)],
-        [],
-        guidance,
-        seam_weight,
-        source_label,
-    )
+        out_shape=[shape(8, 64, LANES), shape(8, REACH, LANES), shape(8, REACH, LANES)],
+        in_specs=[pl.BlockSpec(memory_space=pltpu.HBM)] * 3,
+        out_specs=[pl.BlockSpec(memory_space=pltpu.VMEM)] * 3,
+        scratch_shapes=[
+            pltpu.VMEM((2, CHANNELS, 64, LANES), F32),
+            pltpu.VMEM((64, LANES), jnp.int32),
+            pltpu.VMEM((64, LANES), jnp.int32),
+            pltpu.SemaphoreType.DMA((3,)),
+        ],
+        compiler_params=pltpu.CompilerParams(vmem_limit_bytes=58 * 1024 * 1024),
+    )(guidance, seam_weight, source_label)
     above = lax.ppermute(lower, "z", ring(8, 1))
     below = lax.ppermute(upper, "z", ring(8, -1))
     to_left, to_right = call(
@@ -745,7 +833,7 @@
     raws = [field_shape(level, 4) for level in range(3)]
     m0, m1, m2, source, f0, g1, f1, g2, f2, message = call(
         setup_kernel,
-        maps + [fields[0], fields[0], fields[1], fields[1], fields[2], fields[2], (8, LANES)],
+        maps + [fields[0], fields[0], fields[1], fields[1], fields[2], fields[2], (6, LANES)],
         [field_shape(0, 8)] + raws + fields,
         place, own, above, below, from_right, from_left,
     )
@@ -753,11 +841,11 @@
     wholes = [whole_shape(level, CHANNELS) for level in (3, 4, 5) for _ in range(3)]
     wholes = wholes + [whole_shape(6, CHANNELS)]
     near = [(4, 1, 40, LANES)] + [(CHANNELS, 1, 40, LANES)] * 3
-    m3, m4, m5, m6, solution, n0, h0, k1, h1, k2, h2, message = call(
+    m3, m4, m5, m6, product, solution, n0, h0, k1, h1, k2, h2, message = call(
         middle_kernel,
         [whole_shape(level, 6) for level in (3, 4, 5, 6)]
-        + [fields[0]] * 3 + [fields[1]] * 2 + [fields[2]] * 2 + [(CHANNELS, LANES)],
-        [(7, 256, LANES)] + [whole_shape(level, 4) for level in (3, 4, 5, 6)]
+        + [(len(DIAMOND), 8, LANES)] + [fields[0]] * 3 + [fields[1]] * 2 + [fields[2]] * 2 + [(CHANNELS, LANES)],
+        [(6, 256, LANES)] + [whole_shape(level, 4) for level in (3, 4, 5, 6)]
         + wholes + fields + near,
         place, mine, other, m0, m1, m2, source, f0, g1, f1, g2, f2,
     )
@@ -766,7 +854,7 @@
         last_kernel,
         [(CHANNELS, 64, LANES)] * 2,
         [(CHANNELS, 256, LANES)] + wholes + fields + fields + near,
-        place, mine, other, m0, m1, m2, source, m3, m4, m5, m6,
+        place, mine, other, m0, m1, m2, source, m3, m4, m5, m6, product,
         solution, n0, h0, k1, h1, k2, h2,
     )
     return tuple(outs)

time: 140 us -> 100 us (0.71)
  Pallas kernels: 40.3 us -> 21.9 us
  local copies, waits for them, and re-layouts: 17.7 us -> 2.21 us
  blocking collectives: 52.9 us -> 48.4 us
    pallas_call x5 -> x4, Pallas kernels: 40.3 us -> 20.1 us  [call(): pl.pallas_call(kernel, out_shape=[shape(*o) for o in outs], in_specs=in_s...]
    unnamed x46 -> x4, local copies, waits for them, and re-layouts: 16.6 us -> 1.9 us
    all_to_all x2, blocking collectives: 52.9 us -> 48.4 us  [gathered(): mine = lax.all_to_all(sent, CHIPS, 0, 0, tiled=True)]
    pallas_call x0 -> x1, Pallas kernels: none -> 1.86 us  [local(): pl.pallas_call(stack_kernel, out_shape=[shape(8, 64, LANES), shape(8, REA...]
where the time goes in v2:
time: 100 us
  blocking collectives  48.4 us (48%)
  Pallas kernels  21.9 us (22%)
  starting transfers between devices  14.1 us (14%)
  waiting for transfers between devices  12.8 us (13%)
  local copies, waits for them, and re-layouts  2.21 us (2%)
    all_to_all x2, blocking collectives, gathered(): mine = lax.all_to_all(sent, CHIPS, 0, 0, tiled=True)  48.4 us
    pallas_call x4, Pallas kernels, call(): pl.pallas_call(kernel, out_shape=[shape(*o) for o in outs], in_specs=in_s...  20.1 us
    ppermute x1, waiting for transfers between devices, local(): above = lax.ppermute(lower, 'z', ring(8, 1))  5.45 us
    ppermute x2, starting transfers between devices, gathered(): return (mine, lax.ppermute(mine, 'core', ring(2, 1)))  5.05 us
    ppermute x1, waiting for transfers between devices, local(): from_right = lax.ppermute(to_left, SIDES, ring(32, -1))  4.94 us
    ppermute x1, starting transfers between devices, local(): below = lax.ppermute(upper, 'z', ring(8, -1))  4.03 us
    ppermute x1, starting transfers between devices, local(): above = lax.ppermute(lower, 'z', ring(8, 1))  2.54 us
    ppermute x2, waiting for transfers between devices, gathered(): return (mine, lax.ppermute(mine, 'core', ring(2, 1)))  2.42 us
  transfers between devices with their start and end apart: 6, of which 4 were waited for; matrix products, arithmetic and copies ran while one was open for 0% of the time, Pallas kernels for 0%

profile of v2, /device:TPU:1, one launch (start us, length us, event | category | flops | bytes accessed | tf_op | source)
XLA Modules:
  0.0 100.2 jit_solution(4289965799022206827)
XLA Ops:
  0.6 1.9 %shard_map.50 = (f32[8,64,128]{2,1,0:T(8,128)}, f32[8,56,128]{2,1,0:T(8,128)}, f32[8,56,128]{2,1,0:T(8,128)}) custom-call(f32[2,3,64,128]{3,2,1,0:T(8,128)} %guidance_in.1, s32[64,128]{1,0:T(8,128)} %weight_in.1, s32[64,128]{1,0:T(8,128)} %label_in.1), custom_call_target="tpu_custom_call" | custom-call | tf_op jit(solution)/shard_map/pallas_call | solution.py:811
  2.5 2.5 %collective-permute-start = (f32[8,56,128]{2,1,0:T(8,128)}, f32[8,56,128]{2,1,0:T(8,128)S(1)}, u32[]{:S(2)}, u32[]{:S(2)}) collective-permute-start(f32[8,56,128]{2,1,0:T(8,128)} %get-tuple-element.31), channel_id=1, source_target_pairs={{0,32},{32,64},{64,96},{96,128},{128,160},{160,192},{192,224},{224... | collective-permute-start | bytes 688136 | tf_op jit(solution)/shard_map/ppermute | solution.py:824
  5.0 4.0 %collective-permute-start.1 = (f32[8,56,128]{2,1,0:T(8,128)}, f32[8,56,128]{2,1,0:T(8,128)S(1)}, u32[]{:S(2)}, u32[]{:S(2)}) collective-permute-start(f32[8,56,128]{2,1,0:T(8,128)} %get-tuple-element.32), channel_id=1, source_target_pairs={{0,224},{32,0},{64,32},{96,64},{128,96},{160,128},{192,160},{224,1... | collective-permute-start | bytes 688136 | tf_op jit(solution)/shard_map/ppermute | solution.py:825
  9.1 5.5 %collective-permute-done.above = f32[8,56,128]{2,1,0:T(8,128)S(1)} collective-permute-done((f32[8,56,128]{2,1,0:T(8,128)}, f32[8,56,128]{2,1,0:T(8,128)S(1)}, u32[]{:S(2)}, u32[]{:S(2)}) %collective-permute-start) | collective-permute-done | bytes 229408 | tf_op jit(solution)/shard_map/ppermute | solution.py:824
  14.5 0.0 collective-permute-done.1.below
  14.5 0.0 copy-start
  14.5 0.9 copy-done
  15.5 0.2 shard_map.51
  15.6 1.3 %collective-permute-start.2 = (f32[8,88,128]{2,1,0:T(8,128)S(1)}, f32[8,88,128]{2,1,0:T(8,128)S(1)}, u32[]{:S(2)}, u32[]{:S(2)}) collective-permute-start(f32[8,88,128]{2,1,0:T(8,128)S(1)} %get-tuple-element.33), channel_id=1, source_target_pairs={{0,31},{1,0},{2,1},{3,2},{4,3},{5,4},{6,5},{7,6},{8,7},{9,8},{10,9... | collective-permute-start | bytes 1081352 | tf_op jit(solution)/shard_map/ppermute | solution.py:829
  16.9 1.2 %collective-permute-start.3 = (f32[8,88,128]{2,1,0:T(8,128)S(1)}, f32[8,88,128]{2,1,0:T(8,128)S(1)}, u32[]{:S(2)}, u32[]{:S(2)}) collective-permute-start(f32[8,88,128]{2,1,0:T(8,128)S(1)} %get-tuple-element.34), channel_id=1, source_target_pairs={{0,1},{1,2},{2,3},{3,4},{4,5},{5,6},{6,7},{7,8},{8,9},{9,10},{10,1... | collective-permute-start | bytes 1081352 | tf_op jit(solution)/shard_map/ppermute | solution.py:830
  18.1 0.1 pad_add_fusion.place
  18.2 4.9 %collective-permute-done.2.from_right = f32[8,88,128]{2,1,0:T(8,128)S(1)} collective-permute-done((f32[8,88,128]{2,1,0:T(8,128)S(1)}, f32[8,88,128]{2,1,0:T(8,128)S(1)}, u32[]{:S(2)}, u32[]{:S(2)}) %collective-permute-start.2) | collective-permute-done | bytes 360480 | tf_op jit(solution)/shard_map/ppermute | solution.py:829
  23.2 0.0 collective-permute-done.3.from_left
  23.2 0.0 copy-start.1
  23.2 0.9 copy-done.1
  24.1 3.5 %shard_map.52 = (f32[5,2,208,128]{3,2,1,0:T(8,128)S(1)}, f32[6,2,112,128]{3,2,1,0:T(8,128)S(1)}, f32[6,2,64,128]{3,2,1,0:T(8,128)S(1)}, f32[3,2,208,128]{3,2,1,0...) custom-call(s32[3]{0:T(128)S(1)} %pad_add_fusion.place, ...), custom_call_target="tpu_custom_call" | custom-call | tf_op jit(solution)/shard_map/pallas_call | solution.py:785
  27.6 0.2 broadcast_in_dim.15
  27.8 30.3 %all_to_all.10 = f32[128,1,768]{2,1,0:T(1,128)S(1)} all-to-all(f32[128,1,768]{2,1,0:T(1,128)S(1)} %broadcast_in_dim.15), channel_id=1, replica_groups=mesh['z'=8,'y'=4,'x'=4,'core'=2] {'z','y','x'}, dimensions={0} | all-to-all | bytes 786432 | tf_op jit(solution)/shard_map/all_to_all | solution.py:802
  58.1 3.0 %collective-permute-start.4 = (f32[768,128]{1,0:T(8,128)S(1)}, f32[768,128]{1,0:T(8,128)S(1)}, u32[]{:S(2)}, u32[]{:S(2)}) collective-permute-start(f32[768,128]{1,0:T(8,128)S(1)} %bitcast.7), channel_id=1, source_target_pairs={{0,1},{1,0},{2,3},{3,2},{4,5},{5,4},{6,7},{7,6},{8,9},{9,8},{10,11... | collective-permute-start | bytes 1179656 | tf_op jit(solution)/shard_map/ppermute | solution.py:804
  61.1 1.3 %collective-permute-done.4.other = f32[768,128]{1,0:T(8,128)S(1)} collective-permute-done((f32[768,128]{1,0:T(8,128)S(1)}, f32[768,128]{1,0:T(8,128)S(1)}, u32[]{:S(2)}, u32[]{:S(2)}) %collective-permute-start.4) | collective-permute-done | bytes 393248 | tf_op jit(solution)/shard_map/ppermute | solution.py:804
  62.4 9.3 %shard_map.53 = (f32[6,6,80,128]{3,2,1,0:T(8,128)S(1)}, f32[6,2,48,128]{3,2,1,0:T(8,128)S(1)}, f32[6,1,32,128]{3,2,1,0:T(8,128)S(1)}, f32[6,1,24,128]{3,2,1,0:T(...) custom-call(s32[3]{0:T(128)S(1)} %pad_add_fusion.place, ...), custom_call_target="tpu_custom_call" | custom-call | tf_op jit(solution)/shard_map/pallas_call | solution.py:785
  71.7 0.1 broadcast_in_dim.17
  71.8 18.1 %all_to_all.11 = f32[128,1,384]{2,1,0:T(1,128)S(1)} all-to-all(f32[128,1,384]{2,1,0:T(1,128)S(1)} %broadcast_in_dim.17), channel_id=1, replica_groups=mesh['z'=8,'y'=4,'x'=4,'core'=2] {'z','y','x'}, dimensions={0} | all-to-all | bytes 393216 | tf_op jit(solution)/shard_map/all_to_all | solution.py:802
  89.9 2.1 %collective-permute-start.5 = (f32[384,128]{1,0:T(8,128)S(1)}, f32[384,128]{1,0:T(8,128)S(1)}, u32[]{:S(2)}, u32[]{:S(2)}) collective-permute-start(f32[384,128]{1,0:T(8,128)S(1)} %bitcast.9), channel_id=1, source_target_pairs={{0,1},{1,0},{2,3},{3,2},{4,5},{5,4},{6,7},{7,6},{8,9},{9,8},{10,11... | collective-permute-start | bytes 589832 | tf_op jit(solution)/shard_map/ppermute | solution.py:804
  92.0 1.1 %collective-permute-done.5.other = f32[384,128]{1,0:T(8,128)S(1)} collective-permute-done((f32[384,128]{1,0:T(8,128)S(1)}, f32[384,128]{1,0:T(8,128)S(1)}, u32[]{:S(2)}, u32[]{:S(2)}) %collective-permute-start.5) | collective-permute-done | bytes 196640 | tf_op jit(solution)/shard_map/ppermute | solution.py:804
  93.1 7.1 %shard_map.54 = (f32[3,64,128]{2,1,0:T(8,128)}, f32[3,64,128]{2,1,0:T(8,128)}) custom-call(s32[3]{0:T(128)S(1)} %pad_add_fusion.place, f32[384,128]{1,0:T(8,128)S(1)} %bitcast.10, f32[384,128]{1,0:T(8,128)S(1)} %collective-permute-done.5.other, f32[5,2,208,128]{3,2,1,0:T(8,128)S(1)} %get-tuple-element.36.m0, f32[6,2,112,128]{3,2,1,0:T(8,128)S(1)} %get-tuple-element.37.m1, ...), custom_call_target="tpu_custom_call" | custom-call | tf_op jit(solution)/shard_map/pallas_call | solution.py:785
Async XLA Ops:
  2.5 12.0 %collective-permute-start = (f32[8,56,128]{2,1,0:T(8,128)}, f32[8,56,128]{2,1,0:T(8,128)S(1)}, u32[]{:S(2)}, u32[]{:S(2)}) collective-permute-start(f32[8,56,128]{2,1,0:T(8,128)} %get-tuple-element.31), channel_id=1, source_target_pairs={{0,32},{32,64},{64,96},{96,128},{128,160},{160,192},{192,224},{224... | collective-permute-start | bytes 688136 | tf_op jit(solution)/shard_map/ppermute | solution.py:824
  5.0 9.5 %collective-permute-start.1 = (f32[8,56,128]{2,1,0:T(8,128)}, f32[8,56,128]{2,1,0:T(8,128)S(1)}, u32[]{:S(2)}, u32[]{:S(2)}) collective-permute-start(f32[8,56,128]{2,1,0:T(8,128)} %get-tuple-element.32), channel_id=1, source_target_pairs={{0,224},{32,0},{64,32},{96,64},{128,96},{160,128},{192,160},{224,1... | collective-permute-start | bytes 688136 | tf_op jit(solution)/shard_map/ppermute | solution.py:825
  14.5 1.0 copy-start
  15.6 7.5 %collective-permute-start.2 = (f32[8,88,128]{2,1,0:T(8,128)S(1)}, f32[8,88,128]{2,1,0:T(8,128)S(1)}, u32[]{:S(2)}, u32[]{:S(2)}) collective-permute-start(f32[8,88,128]{2,1,0:T(8,128)S(1)} %get-tuple-element.33), channel_id=1, source_target_pairs={{0,31},{1,0},{2,1},{3,2},{4,3},{5,4},{6,5},{7,6},{8,7},{9,8},{10,9... | collective-permute-start | bytes 1081352 | tf_op jit(solution)/shard_map/ppermute | solution.py:829
  16.9 6.2 %collective-permute-start.3 = (f32[8,88,128]{2,1,0:T(8,128)S(1)}, f32[8,88,128]{2,1,0:T(8,128)S(1)}, u32[]{:S(2)}, u32[]{:S(2)}) collective-permute-start(f32[8,88,128]{2,1,0:T(8,128)S(1)} %get-tuple-element.34), channel_id=1, source_target_pairs={{0,1},{1,2},{2,3},{3,4},{4,5},{5,6},{6,7},{7,8},{8,9},{9,10},{10,1... | collective-permute-start | bytes 1081352 | tf_op jit(solution)/shard_map/ppermute | solution.py:830
  23.2 1.0 copy-start.1
  58.1 4.3 %collective-permute-start.4 = (f32[768,128]{1,0:T(8,128)S(1)}, f32[768,128]{1,0:T(8,128)S(1)}, u32[]{:S(2)}, u32[]{:S(2)}) collective-permute-start(f32[768,128]{1,0:T(8,128)S(1)} %bitcast.7), channel_id=1, source_target_pairs={{0,1},{1,0},{2,3},{3,2},{4,5},{5,4},{6,7},{7,6},{8,9},{9,8},{10,11... | collective-permute-start | bytes 1179656 | tf_op jit(solution)/shard_map/ppermute | solution.py:804
  89.9 3.2 %collective-permute-start.5 = (f32[384,128]{1,0:T(8,128)S(1)}, f32[384,128]{1,0:T(8,128)S(1)}, u32[]{:S(2)}, u32[]{:S(2)}) collective-permute-start(f32[384,128]{1,0:T(8,128)S(1)} %bitcast.9), channel_id=1, source_target_pairs={{0,1},{1,0},{2,3},{3,2},{4,5},{5,4},{6,7},{7,6},{8,9},{9,8},{10,11... | collective-permute-start | bytes 589832 | tf_op jit(solution)/shard_map/ppermute | solution.py:804

commit v3 on v2

--- a/solution.py
+++ b/solution.py
@@ -52,14 +52,8 @@
     return jnp.where(low, pltpu.roll(x, LANES - width, 1), x)
 
 
-def exact_dot(x, chosen):
-    return lax.dot_general(
-        x,
-        chosen,
-        (((1,), (0,)), ((), ())),
-        precision=lax.Precision.HIGHEST,
-        preferred_element_type=F32,
-    )
+def picked(x, lanes):
+    return jnp.take_along_axis(x, lanes, axis=1, mode="promise_in_bounds")
 
 
 def chunks(low, high, size, body):
@@ -125,40 +119,94 @@
     )
 
 
-def stack_kernel(
-    guidance_in, weight_in, label_in, whole, upper, lower, guidance, weight, label, arrived
-):
+FIELDS = 5
+WEIGHT, LABEL = 3, 4
+UPDOWN_ROWS = FIELDS * REACH + 8
+SIDE_ROWS = FIELDS * 88 + 16
+
+
+def stack_kernel(guidance_in, weight_in, label_in, down, up, guidance, weight_at, label_at, arrived):
     copies = [
         pltpu.make_async_copy(source, target, arrived.at[i])
         for i, (source, target) in enumerate(
-            ((guidance_in, guidance), (weight_in, weight), (label_in, label))
+            ((guidance_in, guidance), (weight_in, weight_at), (label_in, label_at))
         )
     ]
     for copy in copies:
         copy.start()
     for copy in copies:
         copy.wait()
+    weight, label = weight_at[...].astype(F32), label_at[...].astype(F32)
+    row = lax.broadcasted_iota(jnp.int32, (64, LANES), 0)
+    lane = lane_ids(64)
+
+    def edge(turn, axis, inside):
+        matching = jnp.where(pltpu.roll(label, turn, axis) == label, 1.0 / 64.0, SEAM_FACTOR / 64.0)
+        return jnp.where(inside, (weight + pltpu.roll(weight, turn, axis)) * matching, 0.0)
+
+    below, right = edge(63, 0, row < 63), edge(LANES - 1, 1, lane < LANES - 1)
 
     def put(a, x):
-        whole[a] = x
-        upper[a] = x[:REACH]
-        lower[a] = x[64 - REACH :]
-
+        down[REACH * a : REACH * (a + 1), :] = x[64 - REACH :]
+        up[REACH * a : REACH * (a + 1), :] = x[:REACH]
+
+    ends = [guidance[0, c, 63:64, :] for c in range(CHANNELS)]
     for c in range(CHANNELS):
-        put(c, guidance[0, c])
-        put(CHANNELS + c, guidance[1, c])
-    put(6, weight[...].astype(F32))
-    put(7, label[...].astype(F32))
-
-
-def pack_kernel(own, above, below, to_left, to_right):
-    for a in range(8):
-        top = jnp.concatenate([above[a], own[a, :32]], axis=0)
-        bottom = jnp.concatenate([own[a, 32:], below[a]], axis=0)
-        bottom = pltpu.roll(bottom, 64, 1)
-        low = lane_ids(88) < 64
-        to_left[a] = jnp.where(low, top, bottom)
-        to_right[a] = jnp.where(low, bottom, top)
+        first, second = below * guidance[0, c], right * guidance[1, c]
+        put(c, (pltpu.roll(first, 1, 0) - first) + (pltpu.roll(second, 1, 1) - second))
+        last = jnp.broadcast_to(guidance[1, c, :, LANES - 1 :], (64, LANES))
+        ends.append(jnp.sum(jnp.where(row == lane, last, 0.0), axis=0, keepdims=True))
+    put(WEIGHT, weight)
+    put(LABEL, label)
+    ends = jnp.concatenate(ends + [jnp.zeros((2, LANES), F32)], axis=0)
+    down[FIELDS * REACH :, :] = ends
+    up[FIELDS * REACH :, :] = ends
+
+
+def own_kernel(down, up, own, ends):
+    for a in range(FIELDS):
+        own[a, :REACH, :] = up[REACH * a : REACH * (a + 1), :]
+        own[a, REACH:, :] = down[REACH * (a + 1) - (64 - REACH) : REACH * (a + 1), :]
+    ends[...] = up[FIELDS * REACH :, :]
+
+
+def upright(row, first, count):
+    hit = lane_ids(count) == first + lax.broadcasted_iota(jnp.int32, (count, LANES), 0)
+    return jnp.sum(jnp.where(hit, jnp.broadcast_to(row, (count, LANES)), 0.0), axis=1, keepdims=True)
+
+
+def pack_kernel(place, own, ends, above, below, swap, side, edge):
+    first_core = place[2] == 0
+    low = lane_ids(88) < 64
+    base = FIELDS * REACH
+
+    def halves(x):
+        return x[:88], pltpu.roll(x[88:], 64, 1)
+
+    for a in range(FIELDS):
+        at = slice(REACH * a, REACH * (a + 1))
+        whole = jnp.concatenate([above[at, :], own[a], below[at, :]], axis=0)
+        top, bottom = halves(whole)
+        to_left = jnp.where(low, top, bottom)
+        if a < CHANNELS:
+            column = jnp.concatenate(
+                [
+                    upright(above[base + 3 + a : base + 4 + a, :], 64 - REACH, REACH),
+                    upright(ends[3 + a : 4 + a, :], 0, 64),
+                    upright(below[base + 3 + a : base + 4 + a, :], 0, REACH),
+                ],
+                axis=0,
+            )
+            column = jnp.broadcast_to(column, (176, LANES))
+            edge[a] = column
+            top, bottom = halves(jnp.where(lane_ids(176) == 64, column, whole))
+        to_right = jnp.where(low, bottom, top)
+        at = slice(88 * a, 88 * (a + 1))
+        swap[at, :] = jnp.where(first_core, to_right, to_left)
+        side[at, :] = jnp.where(first_core, to_left, to_right)
+    for ref in (swap, side):
+        ref[88 * FIELDS : 88 * FIELDS + 8, :] = above[base:, :]
+        ref[88 * FIELDS + 8 :, :] = ends[...]
 
 
 def local_down(level, field, base, work, maps, next_base, next_maps, first_rows, rest_rows, next_rows):
@@ -184,11 +232,8 @@
 
 
 def own_row(x):
-    lane = lax.broadcasted_iota(jnp.int32, (LANES, LANES), 0)
-    place = lax.broadcasted_iota(jnp.int32, (LANES, LANES), 1)
-    chosen = jnp.where(lane == 8 * (place & 15), 1.0, 0.0).astype(F32)
     count = x.shape[0] // 8
-    spread = exact_dot(x, chosen)
+    spread = picked(x, 8 * (lane_ids(x.shape[0]) & 15))
     rows = []
     keep = (lane_ids(8) >> 4) == lax.broadcasted_iota(jnp.int32, (8, LANES), 0)
     for i in range(count):
@@ -238,25 +283,32 @@
 
 
 def setup_kernel(
-    place, own, above, below, from_right, from_left,
+    place, own, ends, above, below, swapped, sided, border,
     m0, m1, m2, source, f0, g1, f1, g2, f2, message,
     cells, raw0, raw1, raw2, w0, w1, w2,
 ):
-    row_at, col_at = place[0], place[1]
+    row_at, col_at, first_core = place[0], place[1], place[2] == 0
     rows_of = lambda n, low: low + lax.broadcasted_iota(jnp.int32, (n, LANES), 0)
     edge = jnp.zeros((16, LANES), F32)
     not_top, not_bottom = row_at > 0, row_at < 7
-    for a in range(8):
+    low = lane_ids(88) < 64
+    inside = (low & (col_at < 31)) | (~low & (col_at > 0))
+
+    def sides(start, size):
+        one, two = swapped[start : start + size, :], sided[start : start + size, :]
+        return jnp.where(first_core, one, two), jnp.where(first_core, two, one)
+
+    for a in range(FIELDS):
+        at = slice(REACH * a, REACH * (a + 1))
         for h in range(2):
             cells[a, h, 0:16, :] = edge
             cells[a, h, 192:208, :] = edge
-        cells[a, 0, 16:72, :] = jnp.where(not_top, above[a], 0.0)
+        cells[a, 0, 16:72, :] = jnp.where(not_top, above[at, :], 0.0)
         cells[a, 0, 72:136, :] = own[a]
-        cells[a, 0, 136:192, :] = jnp.where(not_bottom, below[a], 0.0)
-        low = lane_ids(88) < 64
-        inside = (low & (col_at < 31)) | (~low & (col_at > 0))
-        top = jnp.where(low, from_right[a], from_left[a])
-        bottom = pltpu.roll(jnp.where(low, from_left[a], from_right[a]), 64, 1)
+        cells[a, 0, 136:192, :] = jnp.where(not_bottom, below[at, :], 0.0)
+        from_right, from_left = sides(88 * a, 88)
+        top = jnp.where(low, from_right, from_left)
+        bottom = pltpu.roll(jnp.where(low, from_left, from_right), 64, 1)
         cells[a, 1, 16:104, :] = jnp.where(inside & (not_top | (rows_of(88, 8) >= 64)), top, 0.0)
         cells[a, 1, 104:192, :] = jnp.where(
             inside & (not_bottom | (rows_of(88, 96) < 128)), bottom, 0.0
@@ -272,17 +324,17 @@
         size = 176
         at = pl.ds(start, size)
         up_at, down_at = pl.ds(start - 1, size), pl.ds(start + 1, size)
-        weights = [cells[6, h, at, :] for h in range(2)]
-        labels = [cells[7, h, at, :] for h in range(2)]
+        weights = [cells[WEIGHT, h, at, :] for h in range(2)]
+        labels = [cells[LABEL, h, at, :] for h in range(2)]
         weight_sides = beside(weights, 1)
         label_sides = beside(labels, 1)
-        coef = []
+        coef, shares = [], []
         for h in range(2):
             near_weights = (
-                cells[6, h, up_at, :], cells[6, h, down_at, :], weight_sides[0][h], weight_sides[1][h],
+                cells[WEIGHT, h, up_at, :], cells[WEIGHT, h, down_at, :], weight_sides[0][h], weight_sides[1][h],
             )
             near_labels = (
-                cells[7, h, up_at, :], cells[7, h, down_at, :], label_sides[0][h], label_sides[1][h],
+                cells[LABEL, h, up_at, :], cells[LABEL, h, down_at, :], label_sides[0][h], label_sides[1][h],
             )
             raw = []
             for m in range(4):
@@ -291,20 +343,39 @@
                 value = jnp.where(weights[h] > 0.0, value, 0.0)
                 raw.append(value)
                 raw0[m, h, at, :] = value
-            scaled, scale, _ = scaled_maps(raw, 1.0)
+            scaled, scale, share = scaled_maps(raw, 1.0)
+            shares.append(share)
             for m in range(4):
                 m0[m, h, at, :] = scaled[m]
             m0[SCALE, h, at, :] = scale
             coef.append(scaled)
         for c in range(CHANNELS):
-            second = [cells[CHANNELS + c, h, at, :] for h in range(2)]
-            left = beside(second, 1)[0]
-            for h in range(2):
-                flux = coef[h][UP] * cells[c, h, up_at, :] - coef[h][DOWN] * cells[c, h, at, :]
-                flux = flux + coef[h][LEFT] * left[h] - coef[h][RIGHT] * second[h]
-                source[c, h, at, :] = flux
+            part = [cells[c, h, at, :] for h in range(2)]
+            own_end = border[c]
+            left_end = pltpu.roll(part[1], 64, 1), pltpu.roll(part[1], 63, 1)
+            first, last = lane_ids(size) == 0, lane_ids(size) == LANES - 1
+            flux = jnp.where(first, coef[0][LEFT] * left_end[0], 0.0)
+            flux = flux - jnp.where(last, coef[0][RIGHT] * own_end, 0.0)
+            source[c, 0, at, :] = shares[0] * part[0] + flux
+            flux = jnp.where(first, coef[1][LEFT] * own_end, 0.0)
+            flux = flux - jnp.where(last, coef[1][RIGHT] * left_end[1], 0.0)
+            source[c, 1, at, :] = shares[1] * part[1] + flux
 
     chunks(8, 184, 176, fine)
+    from_right, from_left = sides(88 * FIELDS, 16)
+    beside_own = jnp.where(lane_ids(16) < 64, from_right, from_left)
+    for first, upper in ((0, 71), (8, 135)):
+        for c in range(CHANNELS):
+            if first == 0:
+                straight = above[FIELDS * REACH + c : FIELDS * REACH + c + 1, :]
+            else:
+                straight = ends[c : c + 1, :]
+            for h, flow in ((0, straight), (1, beside_own[first + c : first + c + 1])):
+                if first == 0:
+                    flow = jnp.where(not_top, flow, 0.0)
+                one, two = pl.ds(upper, 1), pl.ds(upper + 1, 1)
+                source[c, h, one, :] = source[c, h, one, :] - m0[DOWN, h, one, :] * flow
+                source[c, h, two, :] = source[c, h, two, :] + m0[UP, h, two, :] * flow
 
     def coarser(raw, width, start, size, h):
         parts = []
@@ -372,31 +443,26 @@
                 put(f, PAD + 8 * z, group, x)
 
 
-def halving(kind):
-    lane = lax.broadcasted_iota(jnp.int32, (2 * LANES, LANES), 0)
-    place = lax.broadcasted_iota(jnp.int32, (2 * LANES, LANES), 1)
-    if kind == "sum":
-        hit = (lane >> 1) == place
-    elif kind == "low":
-        hit = lane == 2 * place
-    else:
-        hit = lane == 2 * place + 1
-    return jnp.where(hit, 1.0, 0.0).astype(F32)
-
-
-def doubling():
-    place = lax.broadcasted_iota(jnp.int32, (LANES, 2 * LANES), 0)
-    lane = lax.broadcasted_iota(jnp.int32, (LANES, 2 * LANES), 1)
-    return jnp.where((lane >> 1) == place, 1.0, 0.0).astype(F32)
-
-
-def folded(halves, matrix):
-    if len(halves) == 1:
-        return [exact_dot(halves[0], matrix[:LANES])]
-    return [
-        exact_dot(jnp.concatenate(halves[i : i + 2], axis=1), matrix)
-        for i in range(0, len(halves), 2)
-    ]
+def folded(halves, kind):
+    lane = lane_ids(halves[0].shape[0])
+    even = (2 * lane) & (LANES - 1)
+
+    def one(x):
+        if kind == "low":
+            return picked(x, even)
+        if kind == "high":
+            return picked(x, even + 1)
+        return picked(x, even) + picked(x, even + 1)
+
+    parts = [one(x) for x in halves]
+    if len(parts) == 1:
+        parts.append(jnp.zeros_like(parts[0]))
+    return [jnp.where(lane < 64, parts[i], parts[i + 1]) for i in range(0, len(parts), 2)]
+
+
+def doubled(x):
+    lane = lane_ids(x.shape[0])
+    return [picked(x, lane >> 1), picked(x, 64 + (lane >> 1))]
 
 
 WHOLE = {3: (4, 64, 1), 4: (2, 32, 0), 5: (1, 16, 0), 6: (1, 8, 0)}
@@ -435,7 +501,7 @@
             even, odd = even_odd(raw, (m, first + h), PAD, next_rows)
             parts.append(even if m == UP else odd if m == DOWN else even + odd)
         kind = "sum" if m in (UP, DOWN) else "low" if m == LEFT else "high"
-        for h, x in enumerate(folded(parts, halving(kind))):
+        for h, x in enumerate(folded(parts, kind)):
             next_raw[m, next_first + h, PAD : PAD + next_rows, :] = 0.5 * x
 
 
@@ -521,7 +587,7 @@
             even, odd = even_odd(other, (c, first + h), PAD, next_rows)
             parts.append(even + odd)
         summed.append(jnp.concatenate(parts, axis=0))
-    for h, x in enumerate(folded(summed, halving("sum"))):
+    for h, x in enumerate(folded(summed, "sum")):
         inverse = 0.25 * maps[level + 1][INVERSE, next_first + h, PAD : PAD + next_rows, :]
         for c in range(CHANNELS):
             part = x[c * next_rows : (c + 1) * next_rows]
@@ -542,11 +608,11 @@
             for h in range(next_halves)
         ]
     for m, x in enumerate(coarse):
-        wide = exact_dot(x, doubling())
+        wide = doubled(x)
         for i in range(min(halves, 2)):
             h = first + 2 * m + i
             for c in range(CHANNELS):
-                part = wide[c * next_rows : (c + 1) * next_rows, LANES * i : LANES * (i + 1)]
+                part = wide[i][c * next_rows : (c + 1) * next_rows]
                 for offset in range(2):
                     at = pl.ds(PAD + offset, next_rows, stride=2)
                     field[c, h, at, :] = field[c, h, at, :] + part
@@ -565,14 +631,6 @@
     low = lane < 64
     fits = lane + offset < LANES
     return jnp.where(low, jnp.where(fits, here, after), jnp.where(fits, before, here))
-
-
-def spread_matrix():
-    place = lax.broadcasted_iota(jnp.int32, (LANES, 2 * LANES), 0)
-    lane = lax.broadcasted_iota(jnp.int32, (LANES, 2 * LANES), 1)
-    source = lane >> 3
-    source = jnp.where(lane >= 192, source + 96, source)
-    return jnp.where(place == source, 1.0, 0.0).astype(F32)
 
 
 def correct_level_two(place, bases, fields, maps, f2, near_maps, near_base, near_a, near_b):
@@ -588,10 +646,11 @@
     stencil("relax", near_b, near_a, near_base, near_maps, 0, 24, 24, 1, 1)
     stencil("relax", near_a, near_b, near_base, near_maps, 0, 24, 24, 1, 1)
     flat = jnp.concatenate([near_a[c, 0, PAD : PAD + 24, :] for c in range(CHANNELS)], axis=0)
-    wide = exact_dot(flat, spread_matrix())
+    lane = lane_ids(flat.shape[0])
+    wide = [picked(flat, lane >> 3), picked(flat, jnp.where(lane < 64, 16, 112) + (lane >> 3))]
     for c in range(CHANNELS):
         for h in range(2):
-            part = wide[24 * c : 24 * c + 24, LANES * h : LANES * h + LANES]
+            part = wide[h][24 * c : 24 * c + 24]
             for offset in range(2):
                 at = pl.ds(PAD + offset, 24, stride=2)
                 f2[c, h, at, :] = f2[c, h, at, :] + part
@@ -789,6 +848,7 @@
         out_specs=[pl.BlockSpec(memory_space=pltpu.VMEM) for _ in outs],
         scratch_shapes=[pltpu.VMEM(s, F32) for s in scratch],
         compiler_params=pltpu.CompilerParams(vmem_limit_bytes=14 * 1024 * 1024),
+        cost_estimate=pl.CostEstimate(flops=0, bytes_accessed=8_000_000, transcendentals=0),
     )(*args)
 
 
@@ -808,11 +868,11 @@
     place = jnp.stack(
         [lax.axis_index("z"), lax.axis_index(SIDES), lax.axis_index("core")]
     ).astype(jnp.int32)
-    own, upper, lower = pl.pallas_call(
+    down, up = pl.pallas_call(
         stack_kernel,
-        out_shape=[shape(8, 64, LANES), shape(8, REACH, LANES), shape(8, REACH, LANES)],
+        out_shape=[shape(UPDOWN_ROWS, LANES)] * 2,
         in_specs=[pl.BlockSpec(memory_space=pltpu.HBM)] * 3,
-        out_specs=[pl.BlockSpec(memory_space=pltpu.VMEM)] * 3,
+        out_specs=[pl.BlockSpec(memory_space=pltpu.VMEM)] * 2,
         scratch_shapes=[
             pltpu.VMEM((2, CHANNELS, 64, LANES), F32),
             pltpu.VMEM((64, LANES), jnp.int32),
@@ -821,21 +881,26 @@
         ],
         compiler_params=pltpu.CompilerParams(vmem_limit_bytes=58 * 1024 * 1024),
     )(guidance, seam_weight, source_label)
-    above = lax.ppermute(lower, "z", ring(8, 1))
-    below = lax.ppermute(upper, "z", ring(8, -1))
-    to_left, to_right = call(
-        pack_kernel, [(8, 88, LANES)] * 2, [], own, above, below
+    above = lax.ppermute(down, "z", ring(8, 1))
+    below = lax.ppermute(up, "z", ring(8, -1))
+    own, ends = call(own_kernel, [(FIELDS, 64, LANES), (8, LANES)], [], down, up)
+    swap, side, border = call(
+        pack_kernel,
+        [(SIDE_ROWS, LANES)] * 2 + [(CHANNELS, 176, LANES)],
+        [],
+        place, own, ends, above, below,
     )
-    from_right = lax.ppermute(to_left, SIDES, ring(32, -1))
-    from_left = lax.ppermute(to_right, SIDES, ring(32, 1))
+    swapped = lax.ppermute(swap, "core", ring(2, 1))
+    pairs = [(i, min(max(i + 2 * (i % 2) - 1, 0), 31)) for i in range(32)]
+    sided = lax.ppermute(side, SIDES, pairs)
     fields = [field_shape(level, CHANNELS) for level in range(3)]
     maps = [field_shape(0, 5), field_shape(1, 6), field_shape(2, 6)]
     raws = [field_shape(level, 4) for level in range(3)]
     m0, m1, m2, source, f0, g1, f1, g2, f2, message = call(
         setup_kernel,
         maps + [fields[0], fields[0], fields[1], fields[1], fields[2], fields[2], (6, LANES)],
-        [field_shape(0, 8)] + raws + fields,
-        place, own, above, below, from_right, from_left,
+        [field_shape(0, FIELDS)] + raws + fields,
+        place, own, ends, above, below, swapped, sided, border,
     )
     mine, other = gathered(message)
     wholes = [whole_shape(level, CHANNELS) for level in (3, 4, 5) for _ in range(3)]

time: 100 us -> 129 us (1.29)
  Pallas kernels: 21.9 us -> 53.8 us
  waiting for transfers between devices: 12.8 us -> 8.87 us
  blocking collectives: 48.4 us -> 50 us
  starting transfers between devices: 14.1 us -> 12.7 us
    pallas_call x4 -> x5, Pallas kernels: 20.1 us -> 51.9 us  [call(): pl.pallas_call(kernel, out_shape=[shape(*o) for o in outs], in_specs=in_s...]
    ppermute x4, waiting for transfers between devices: 10.4 us -> 6.08 us  [the longest x1 4.34 us: local(): sided = lax.ppermute(side, SIDES, pairs)]
    ppermute x2, starting transfers between devices: 5.05 us -> 1.83 us  [gathered(): return (mine, lax.ppermute(mine, 'core', ring(2, 1)))]
    ppermute x4, starting transfers between devices: 9.06 us -> 10.9 us  [the longest x1 4.03 us: local(): below = lax.ppermute(up, 'z', ring(8, -1))]
    all_to_all x2, blocking collectives: 48.4 us -> 50 us  [gathered(): mine = lax.all_to_all(sent, CHIPS, 0, 0, tiled=True)]
where the time goes in v3:
time: 129 us; the launch traced here: 128 us
  Pallas kernels  53.8 us (42%)
  blocking collectives  50 us (39%)
  starting transfers between devices  12.7 us (10%)
  waiting for transfers between devices  8.87 us (7%)
  local copies, waits for them, and re-layouts  2.16 us (2%)
    pallas_call x5, Pallas kernels, call(): pl.pallas_call(kernel, out_shape=[shape(*o) for o in outs], in_specs=in_s...  51.9 us
    all_to_all x2, blocking collectives, gathered(): mine = lax.all_to_all(sent, CHIPS, 0, 0, tiled=True)  50 us
    ppermute x1, waiting for transfers between devices, local(): sided = lax.ppermute(side, SIDES, pairs)  4.34 us
    ppermute x1, starting transfers between devices, local(): below = lax.ppermute(up, 'z', ring(8, -1))  4.03 us
    ppermute x1, starting transfers between devices, local(): sided = lax.ppermute(side, SIDES, pairs)  3.02 us
    ppermute x2, waiting for transfers between devices, gathered(): return (mine, lax.ppermute(mine, 'core', ring(2, 1)))  2.79 us
  transfers between devices with their start and end apart: 6, of which 4 were waited for; matrix products, arithmetic and copies ran while one was open for 0% of the time, Pallas kernels for 0%

profile of v3, /device:TPU:1, one launch (start us, length us, event | category | flops | bytes accessed | tf_op | source)
XLA Modules:
  0.0 128.3 jit_solution(10696651556514675647)
XLA Ops:
  0.6 1.9 %shard_map.50 = (f32[288,128]{1,0:T(8,128)}, f32[288,128]{1,0:T(8,128)}) custom-call(f32[2,3,64,128]{3,2,1,0:T(8,128)} %guidance_in.1, s32[64,128]{1,0:T(8,128)} %weight_in.1, s32[64,128]{1,0:T(8,128)} %label_in.1), custom_call_target="tpu_custom_call" | custom-call | tf_op jit(solution)/shard_map/pallas_call | solution.py:871
  2.5 2.5 %collective-permute-start = (f32[288,128]{1,0:T(8,128)}, f32[288,128]{1,0:T(8,128)S(1)}, u32[]{:S(2)}, u32[]{:S(2)}) collective-permute-start(f32[288,128]{1,0:T(8,128)} %get-tuple-element.32.down), channel_id=1, source_target_pairs={{0,32},{32,64},{64,96},{96,128},{128,160},{160,192},{192,224},{224... | collective-permute-start | bytes 442376 | tf_op jit(solution)/shard_map/ppermute | solution.py:884
  5.0 4.0 %collective-permute-start.1 = (f32[288,128]{1,0:T(8,128)}, f32[288,128]{1,0:T(8,128)S(1)}, u32[]{:S(2)}, u32[]{:S(2)}) collective-permute-start(f32[288,128]{1,0:T(8,128)} %get-tuple-element.33.up), channel_id=1, source_target_pairs={{0,224},{32,0},{64,32},{96,64},{128,96},{160,128},{192,160},{224,1... | collective-permute-start | bytes 442376 | tf_op jit(solution)/shard_map/ppermute | solution.py:885
  9.1 0.0 copy-start
  9.1 0.9 copy-done
  10.0 0.0 copy-start.1
  10.0 0.9 copy-done.1
  11.0 0.1 pad_add_fusion.place
  11.0 1.7 %collective-permute-done.above = f32[288,128]{1,0:T(8,128)S(1)} collective-permute-done((f32[288,128]{1,0:T(8,128)}, f32[288,128]{1,0:T(8,128)S(1)}, u32[]{:S(2)}, u32[]{:S(2)}) %collective-permute-start) | collective-permute-done | bytes 147488 | tf_op jit(solution)/shard_map/ppermute | solution.py:884
  12.8 0.0 collective-permute-done.1.below
  12.8 1.2 shard_map.52
  14.0 1.3 %collective-permute-start.2 = (f32[456,128]{1,0:T(8,128)S(1)}, f32[456,128]{1,0:T(8,128)S(1)}, u32[]{:S(2)}, u32[]{:S(2)}) collective-permute-start(f32[456,128]{1,0:T(8,128)S(1)} %get-tuple-element.36), channel_id=1, source_target_pairs={{0,1},{1,0},{2,3},{3,2},{4,5},{5,4},{6,7},{7,6},{8,9},{9,8},{10,11... | collective-permute-start | bytes 700424 | tf_op jit(solution)/shard_map/ppermute | solution.py:893
  15.3 3.0 %collective-permute-start.3 = (f32[456,128]{1,0:T(8,128)S(1)}, f32[456,128]{1,0:T(8,128)S(1)}, u32[]{:S(2)}, u32[]{:S(2)}) collective-permute-start(f32[456,128]{1,0:T(8,128)S(1)} %get-tuple-element.37), channel_id=1, source_target_pairs={{0,0},{1,2},{2,1},{3,4},{4,3},{5,6},{6,5},{7,8},{8,7},{9,10},{10,9... | collective-permute-start | bytes 700424 | tf_op jit(solution)/shard_map/ppermute | solution.py:895
  18.3 0.0 collective-permute-done.2.swapped
  18.3 4.3 %collective-permute-done.3.sided = f32[456,128]{1,0:T(8,128)S(1)} collective-permute-done((f32[456,128]{1,0:T(8,128)S(1)}, f32[456,128]{1,0:T(8,128)S(1)}, u32[]{:S(2)}, u32[]{:S(2)}) %collective-permute-start.3) | collective-permute-done | bytes 233504 | tf_op jit(solution)/shard_map/ppermute | solution.py:895
  22.7 3.6 %shard_map.53 = (f32[5,2,208,128]{3,2,1,0:T(8,128)S(1)}, f32[6,2,112,128]{3,2,1,0:T(8,128)S(1)}, f32[6,2,64,128]{3,2,1,0:T(8,128)S(1)}, f32[3,2,208,128]{3,2,1,0...) custom-call(s32[3]{0:T(128)S(1)} %pad_add_fusion.place, ...), custom_call_target="tpu_custom_call" | custom-call | bytes 8000000 | tf_op jit(solution)/shard_map/pallas_call | solution.py:844
  26.3 0.2 broadcast_in_dim.15
  26.5 31.6 %all_to_all.10 = f32[128,1,768]{2,1,0:T(1,128)S(1)} all-to-all(f32[128,1,768]{2,1,0:T(1,128)S(1)} %broadcast_in_dim.15), channel_id=1, replica_groups=mesh['z'=8,'y'=4,'x'=4,'core'=2] {'z','y','x'}, dimensions={0} | all-to-all | bytes 786432 | tf_op jit(solution)/shard_map/all_to_all | solution.py:862
  58.1 0.0 collective-permute-start.4
  58.1 1.7 %collective-permute-done.4.other = f32[768,128]{1,0:T(8,128)S(1)} collective-permute-done((f32[768,128]{1,0:T(8,128)S(1)}, f32[768,128]{1,0:T(8,128)S(1)}, u32[]{:S(2)}, u32[]{:S(2)}) %collective-permute-start.4) | collective-permute-done | bytes 393248 | tf_op jit(solution)/shard_map/ppermute | solution.py:864
  59.9 31.5 %shard_map.54 = (f32[6,6,80,128]{3,2,1,0:T(8,128)S(1)}, f32[6,2,48,128]{3,2,1,0:T(8,128)S(1)}, f32[6,1,32,128]{3,2,1,0:T(8,128)S(1)}, f32[6,1,24,128]{3,2,1,0:T(...) custom-call(s32[3]{0:T(128)S(1)} %pad_add_fusion.place, ...), custom_call_target="tpu_custom_call" | custom-call | bytes 8000000 | tf_op jit(solution)/shard_map/pallas_call | solution.py:844
  91.3 0.1 broadcast_in_dim.17
  91.5 18.4 %all_to_all.11 = f32[128,1,384]{2,1,0:T(1,128)S(1)} all-to-all(f32[128,1,384]{2,1,0:T(1,128)S(1)} %broadcast_in_dim.17), channel_id=1, replica_groups=mesh['z'=8,'y'=4,'x'=4,'core'=2] {'z','y','x'}, dimensions={0} | all-to-all | bytes 393216 | tf_op jit(solution)/shard_map/all_to_all | solution.py:862
  109.8 1.8 %collective-permute-start.5 = (f32[384,128]{1,0:T(8,128)S(1)}, f32[384,128]{1,0:T(8,128)S(1)}, u32[]{:S(2)}, u32[]{:S(2)}) collective-permute-start(f32[384,128]{1,0:T(8,128)S(1)} %bitcast.9), channel_id=1, source_target_pairs={{0,1},{1,0},{2,3},{3,2},{4,5},{5,4},{6,7},{7,6},{8,9},{9,8},{10,11... | collective-permute-start | bytes 589832 | tf_op jit(solution)/shard_map/ppermute | solution.py:864
  111.7 1.1 collective-permute-done.5.other
  112.7 15.6 %shard_map.55 = (f32[3,64,128]{2,1,0:T(8,128)}, f32[3,64,128]{2,1,0:T(8,128)}) custom-call(s32[3]{0:T(128)S(1)} %pad_add_fusion.place, f32[384,128]{1,0:T(8,128)S(1)} %bitcast.10, f32[384,128]{1,0:T(8,128)S(1)} %collective-permute-done.5.other, f32[5,2,208,128]{3,2,1,0:T(8,128)S(1)} %get-tuple-element.40.m0, f32[6,2,112,128]{3,2,1,0:T(8,128)S(1)} %get-tuple-element.41.m1, ...), custom_call_target="tpu_custom_call" | custom-call | bytes 8000000 | tf_op jit(solution)/shard_map/pallas_call | solution.py:844
  (1 shorter events, 0.0 us)
Async XLA Ops:
  2.5 10.3 %collective-permute-start = (f32[288,128]{1,0:T(8,128)}, f32[288,128]{1,0:T(8,128)S(1)}, u32[]{:S(2)}, u32[]{:S(2)}) collective-permute-start(f32[288,128]{1,0:T(8,128)} %get-tuple-element.32.down), channel_id=1, source_target_pairs={{0,32},{32,64},{64,96},{96,128},{128,160},{160,192},{192,224},{224... | collective-permute-start | bytes 442376 | tf_op jit(solution)/shard_map/ppermute | solution.py:884
  5.0 7.7 %collective-permute-start.1 = (f32[288,128]{1,0:T(8,128)}, f32[288,128]{1,0:T(8,128)S(1)}, u32[]{:S(2)}, u32[]{:S(2)}) collective-permute-start(f32[288,128]{1,0:T(8,128)} %get-tuple-element.33.up), channel_id=1, source_target_pairs={{0,224},{32,0},{64,32},{96,64},{128,96},{160,128},{192,160},{224,1... | collective-permute-start | bytes 442376 | tf_op jit(solution)/shard_map/ppermute | solution.py:885
  9.1 0.9 copy-start
  10.0 0.9 copy-start.1
  14.0 4.3 %collective-permute-start.2 = (f32[456,128]{1,0:T(8,128)S(1)}, f32[456,128]{1,0:T(8,128)S(1)}, u32[]{:S(2)}, u32[]{:S(2)}) collective-permute-start(f32[456,128]{1,0:T(8,128)S(1)} %get-tuple-element.36), channel_id=1, source_target_pairs={{0,1},{1,0},{2,3},{3,2},{4,5},{5,4},{6,7},{7,6},{8,9},{9,8},{10,11... | collective-permute-start | bytes 700424 | tf_op jit(solution)/shard_map/ppermute | solution.py:893
  15.3 7.4 %collective-permute-start.3 = (f32[456,128]{1,0:T(8,128)S(1)}, f32[456,128]{1,0:T(8,128)S(1)}, u32[]{:S(2)}, u32[]{:S(2)}) collective-permute-start(f32[456,128]{1,0:T(8,128)S(1)} %get-tuple-element.37), channel_id=1, source_target_pairs={{0,0},{1,2},{2,1},{3,4},{4,3},{5,6},{6,5},{7,8},{8,7},{9,10},{10,9... | collective-permute-start | bytes 700424 | tf_op jit(solution)/shard_map/ppermute | solution.py:895
  58.1 1.7 %collective-permute-start.4 = (f32[768,128]{1,0:T(8,128)S(1)}, f32[768,128]{1,0:T(8,128)S(1)}, u32[]{:S(2)}, u32[]{:S(2)}) collective-permute-start(f32[768,128]{1,0:T(8,128)S(1)} %bitcast.7), channel_id=1, source_target_pairs={{0,1},{1,0},{2,3},{3,2},{4,5},{5,4},{6,7},{7,6},{8,9},{9,8},{10,11... | collective-permute-start | bytes 1179656 | tf_op jit(solution)/shard_map/ppermute | solution.py:864
  109.8 2.9 %collective-permute-start.5 = (f32[384,128]{1,0:T(8,128)S(1)}, f32[384,128]{1,0:T(8,128)S(1)}, u32[]{:S(2)}, u32[]{:S(2)}) collective-permute-start(f32[384,128]{1,0:T(8,128)S(1)} %bitcast.9), channel_id=1, source_target_pairs={{0,1},{1,0},{2,3},{3,2},{4,5},{5,4},{6,7},{7,6},{8,9},{9,8},{10,11... | collective-permute-start | bytes 589832 | tf_op jit(solution)/shard_map/ppermute | solution.py:864

commit v4 on v3

--- a/solution.py
+++ b/solution.py
@@ -171,8 +171,8 @@
 
 
 def upright(row, first, count):
-    hit = lane_ids(count) == first + lax.broadcasted_iota(jnp.int32, (count, LANES), 0)
-    return jnp.sum(jnp.where(hit, jnp.broadcast_to(row, (count, LANES)), 0.0), axis=1, keepdims=True)
+    place = first + lax.broadcasted_iota(jnp.int32, (count, LANES), 0)
+    return picked(jnp.broadcast_to(row, (count, LANES)), place)
 
 
 def pack_kernel(place, own, ends, above, below, swap, side, edge):
@@ -197,7 +197,6 @@
                 ],
                 axis=0,
             )
-            column = jnp.broadcast_to(column, (176, LANES))
             edge[a] = column
             top, bottom = halves(jnp.where(lane_ids(176) == 64, column, whole))
         to_right = jnp.where(low, bottom, top)
@@ -425,22 +424,16 @@
         ordered[f, pl.ds(0, 128, stride=2), :] = jnp.where(core == 0, own, theirs)
         ordered[f, pl.ds(1, 128, stride=2), :] = jnp.where(core == 0, theirs, own)
     sub = lax.broadcasted_iota(jnp.int32, (8, LANES), 0)
-    part = lane_ids(8) >> 4
-
+    part, cell = lane_ids(8) >> 4, lane_ids(8) & 15
+    first = (((sub - part) & 7) << 4) + cell
+    last = (((part - sub) & 7) << 4) + cell
     for z in range(8):
         for f in range(count):
             for group in range(4):
-                x = ordered[f, pl.ds(z * 32 + 8 * group, 8), :]
-                for k in (4, 2, 1):
-                    same = (sub & k) == (part & k)
-                    ahead = pltpu.roll(pltpu.roll(x, 8 - k, 0), 16 * k, 1)
-                    if k == 4:
-                        moved = ahead
-                    else:
-                        behind = pltpu.roll(pltpu.roll(x, k, 0), LANES - 16 * k, 1)
-                        moved = jnp.where((sub & k) == 0, ahead, behind)
-                    x = jnp.where(same, x, moved)
-                put(f, PAD + 8 * z, group, x)
+                x = picked(ordered[f, pl.ds(z * 32 + 8 * group, 8), :], first)
+                for k in (1, 2, 4):
+                    x = jnp.where((part & k) != 0, pltpu.roll(x, 8 - k, 0), x)
+                put(f, PAD + 8 * z, group, picked(x, last))
 
 
 def folded(halves, kind):

time: 129 us -> 96.2 us (0.75)
  Pallas kernels: 53.8 us -> 21.4 us
    pallas_call x5, Pallas kernels: 51.9 us -> 19.5 us  [call(): pl.pallas_call(kernel, out_shape=[shape(*o) for o in outs], in_specs=in_s...]
where the time goes in v4:
time: 96.2 us; the launch traced here: 95.9 us
  blocking collectives  50 us (52%)
  Pallas kernels  21.4 us (22%)
  starting transfers between devices  12.7 us (13%)
  waiting for transfers between devices  8.87 us (9%)
  local copies, waits for them, and re-layouts  2.16 us (2%)
    all_to_all x2, blocking collectives, gathered(): mine = lax.all_to_all(sent, CHIPS, 0, 0, tiled=True)  50 us
    pallas_call x5, Pallas kernels, call(): pl.pallas_call(kernel, out_shape=[shape(*o) for o in outs], in_specs=in_s...  19.5 us
    ppermute x1, waiting for transfers between devices, local(): sided = lax.ppermute(side, SIDES, pairs)  4.34 us
    ppermute x1, starting transfers between devices, local(): below = lax.ppermute(up, 'z', ring(8, -1))  4.03 us
    ppermute x1, starting transfers between devices, local(): sided = lax.ppermute(side, SIDES, pairs)  3.02 us
    ppermute x2, waiting for transfers between devices, gathered(): return (mine, lax.ppermute(mine, 'core', ring(2, 1)))  2.79 us
    ppermute x1, starting transfers between devices, local(): above = lax.ppermute(down, 'z', ring(8, 1))  2.54 us
  transfers between devices with their start and end apart: 6, of which 4 were waited for; matrix products, arithmetic and copies ran while one was open for 0% of the time, Pallas kernels for 0%

profile of v4, /device:TPU:1, one launch (start us, length us, event | category | flops | bytes accessed | tf_op | source)
XLA Modules:
  0.0 95.9 jit_solution(15594070007057298270)
XLA Ops:
  0.6 1.9 %shard_map.50 = (f32[288,128]{1,0:T(8,128)}, f32[288,128]{1,0:T(8,128)}) custom-call(f32[2,3,64,128]{3,2,1,0:T(8,128)} %guidance_in.1, s32[64,128]{1,0:T(8,128)} %weight_in.1, s32[64,128]{1,0:T(8,128)} %label_in.1), custom_call_target="tpu_custom_call" | custom-call | tf_op jit(solution)/shard_map/pallas_call | solution.py:864
  2.5 2.5 %collective-permute-start = (f32[288,128]{1,0:T(8,128)}, f32[288,128]{1,0:T(8,128)S(1)}, u32[]{:S(2)}, u32[]{:S(2)}) collective-permute-start(f32[288,128]{1,0:T(8,128)} %get-tuple-element.32.down), channel_id=1, source_target_pairs={{0,32},{32,64},{64,96},{96,128},{128,160},{160,192},{192,224},{224... | collective-permute-start | bytes 442376 | tf_op jit(solution)/shard_map/ppermute | solution.py:877
  5.0 4.0 %collective-permute-start.1 = (f32[288,128]{1,0:T(8,128)}, f32[288,128]{1,0:T(8,128)S(1)}, u32[]{:S(2)}, u32[]{:S(2)}) collective-permute-start(f32[288,128]{1,0:T(8,128)} %get-tuple-element.33.up), channel_id=1, source_target_pairs={{0,224},{32,0},{64,32},{96,64},{128,96},{160,128},{192,160},{224,1... | collective-permute-start | bytes 442376 | tf_op jit(solution)/shard_map/ppermute | solution.py:878
  9.1 0.0 copy-start
  9.1 0.9 copy-done
  10.0 0.0 copy-start.1
  10.0 0.9 copy-done.1
  11.0 0.1 pad_add_fusion.place
  11.0 1.7 %collective-permute-done.above = f32[288,128]{1,0:T(8,128)S(1)} collective-permute-done((f32[288,128]{1,0:T(8,128)}, f32[288,128]{1,0:T(8,128)S(1)}, u32[]{:S(2)}, u32[]{:S(2)}) %collective-permute-start) | collective-permute-done | bytes 147488 | tf_op jit(solution)/shard_map/ppermute | solution.py:877
  12.8 0.0 collective-permute-done.1.below
  12.8 1.0 %shard_map.52 = (f32[456,128]{1,0:T(8,128)S(1)}, f32[456,128]{1,0:T(8,128)S(1)}, f32[3,176,128]{2,1,0:T(8,128)S(1)}) custom-call(s32[3]{0:T(128)S(1)} %pad_add_fusion.place, f32[5,64,128]{2,1,0:T(8,128)S(1)} %get-tuple-element.34.own, f32[8,128]{1,0:T(8,128)S(1)} %get-tuple-element.35.ends, f32[288,128]{1,0:T(8,128)S(1)} %collective-permute-done.above, ...), custom_call_target="tpu_custom_call" | custom-call | bytes 8000000 | tf_op jit(solution)/shard_map/pallas_call | solution.py:837
  13.8 1.3 %collective-permute-start.2 = (f32[456,128]{1,0:T(8,128)S(1)}, f32[456,128]{1,0:T(8,128)S(1)}, u32[]{:S(2)}, u32[]{:S(2)}) collective-permute-start(f32[456,128]{1,0:T(8,128)S(1)} %get-tuple-element.36), channel_id=1, source_target_pairs={{0,1},{1,0},{2,3},{3,2},{4,5},{5,4},{6,7},{7,6},{8,9},{9,8},{10,11... | collective-permute-start | bytes 700424 | tf_op jit(solution)/shard_map/ppermute | solution.py:886
  15.1 3.0 %collective-permute-start.3 = (f32[456,128]{1,0:T(8,128)S(1)}, f32[456,128]{1,0:T(8,128)S(1)}, u32[]{:S(2)}, u32[]{:S(2)}) collective-permute-start(f32[456,128]{1,0:T(8,128)S(1)} %get-tuple-element.37), channel_id=1, source_target_pairs={{0,0},{1,2},{2,1},{3,4},{4,3},{5,6},{6,5},{7,8},{8,7},{9,10},{10,9... | collective-permute-start | bytes 700424 | tf_op jit(solution)/shard_map/ppermute | solution.py:888
  18.1 0.0 collective-permute-done.2.swapped
  18.1 4.3 %collective-permute-done.3.sided = f32[456,128]{1,0:T(8,128)S(1)} collective-permute-done((f32[456,128]{1,0:T(8,128)S(1)}, f32[456,128]{1,0:T(8,128)S(1)}, u32[]{:S(2)}, u32[]{:S(2)}) %collective-permute-start.3) | collective-permute-done | bytes 233504 | tf_op jit(solution)/shard_map/ppermute | solution.py:888
  22.5 3.6 %shard_map.53 = (f32[5,2,208,128]{3,2,1,0:T(8,128)S(1)}, f32[6,2,112,128]{3,2,1,0:T(8,128)S(1)}, f32[6,2,64,128]{3,2,1,0:T(8,128)S(1)}, f32[3,2,208,128]{3,2,1,0...) custom-call(s32[3]{0:T(128)S(1)} %pad_add_fusion.place, ...), custom_call_target="tpu_custom_call" | custom-call | bytes 8000000 | tf_op jit(solution)/shard_map/pallas_call | solution.py:837
  26.1 0.2 broadcast_in_dim.15
  26.3 31.6 %all_to_all.10 = f32[128,1,768]{2,1,0:T(1,128)S(1)} all-to-all(f32[128,1,768]{2,1,0:T(1,128)S(1)} %broadcast_in_dim.15), channel_id=1, replica_groups=mesh['z'=8,'y'=4,'x'=4,'core'=2] {'z','y','x'}, dimensions={0} | all-to-all | bytes 786432 | tf_op jit(solution)/shard_map/all_to_all | solution.py:855
  57.9 0.0 collective-permute-start.4
  57.9 1.7 %collective-permute-done.4.other = f32[768,128]{1,0:T(8,128)S(1)} collective-permute-done((f32[768,128]{1,0:T(8,128)S(1)}, f32[768,128]{1,0:T(8,128)S(1)}, u32[]{:S(2)}, u32[]{:S(2)}) %collective-permute-start.4) | collective-permute-done | bytes 393248 | tf_op jit(solution)/shard_map/ppermute | solution.py:857
  59.7 8.8 %shard_map.54 = (f32[6,6,80,128]{3,2,1,0:T(8,128)S(1)}, f32[6,2,48,128]{3,2,1,0:T(8,128)S(1)}, f32[6,1,32,128]{3,2,1,0:T(8,128)S(1)}, f32[6,1,24,128]{3,2,1,0:T(...) custom-call(s32[3]{0:T(128)S(1)} %pad_add_fusion.place, ...), custom_call_target="tpu_custom_call" | custom-call | bytes 8000000 | tf_op jit(solution)/shard_map/pallas_call | solution.py:837
  68.4 0.1 broadcast_in_dim.17
  68.5 18.4 %all_to_all.11 = f32[128,1,384]{2,1,0:T(1,128)S(1)} all-to-all(f32[128,1,384]{2,1,0:T(1,128)S(1)} %broadcast_in_dim.17), channel_id=1, replica_groups=mesh['z'=8,'y'=4,'x'=4,'core'=2] {'z','y','x'}, dimensions={0} | all-to-all | bytes 393216 | tf_op jit(solution)/shard_map/all_to_all | solution.py:855
  86.9 1.8 %collective-permute-start.5 = (f32[384,128]{1,0:T(8,128)S(1)}, f32[384,128]{1,0:T(8,128)S(1)}, u32[]{:S(2)}, u32[]{:S(2)}) collective-permute-start(f32[384,128]{1,0:T(8,128)S(1)} %bitcast.9), channel_id=1, source_target_pairs={{0,1},{1,0},{2,3},{3,2},{4,5},{5,4},{6,7},{7,6},{8,9},{9,8},{10,11... | collective-permute-start | bytes 589832 | tf_op jit(solution)/shard_map/ppermute | solution.py:857
  88.7 1.1 %collective-permute-done.5.other = f32[384,128]{1,0:T(8,128)S(1)} collective-permute-done((f32[384,128]{1,0:T(8,128)S(1)}, f32[384,128]{1,0:T(8,128)S(1)}, u32[]{:S(2)}, u32[]{:S(2)}) %collective-permute-start.5) | collective-permute-done | bytes 196640 | tf_op jit(solution)/shard_map/ppermute | solution.py:857
  89.8 6.1 %shard_map.55 = (f32[3,64,128]{2,1,0:T(8,128)}, f32[3,64,128]{2,1,0:T(8,128)}) custom-call(s32[3]{0:T(128)S(1)} %pad_add_fusion.place, f32[384,128]{1,0:T(8,128)S(1)} %bitcast.10, f32[384,128]{1,0:T(8,128)S(1)} %collective-permute-done.5.other, f32[5,2,208,128]{3,2,1,0:T(8,128)S(1)} %get-tuple-element.40.m0, f32[6,2,112,128]{3,2,1,0:T(8,128)S(1)} %get-tuple-element.41.m1, ...), custom_call_target="tpu_custom_call" | custom-call | bytes 8000000 | tf_op jit(solution)/shard_map/pallas_call | solution.py:837
  (1 shorter events, 0.0 us)
Async XLA Ops:
  2.5 10.3 %collective-permute-start = (f32[288,128]{1,0:T(8,128)}, f32[288,128]{1,0:T(8,128)S(1)}, u32[]{:S(2)}, u32[]{:S(2)}) collective-permute-start(f32[288,128]{1,0:T(8,128)} %get-tuple-element.32.down), channel_id=1, source_target_pairs={{0,32},{32,64},{64,96},{96,128},{128,160},{160,192},{192,224},{224... | collective-permute-start | bytes 442376 | tf_op jit(solution)/shard_map/ppermute | solution.py:877
  5.0 7.7 %collective-permute-start.1 = (f32[288,128]{1,0:T(8,128)}, f32[288,128]{1,0:T(8,128)S(1)}, u32[]{:S(2)}, u32[]{:S(2)}) collective-permute-start(f32[288,128]{1,0:T(8,128)} %get-tuple-element.33.up), channel_id=1, source_target_pairs={{0,224},{32,0},{64,32},{96,64},{128,96},{160,128},{192,160},{224,1... | collective-permute-start | bytes 442376 | tf_op jit(solution)/shard_map/ppermute | solution.py:878
  9.1 0.9 copy-start
  10.0 0.9 copy-start.1
  13.8 4.3 %collective-permute-start.2 = (f32[456,128]{1,0:T(8,128)S(1)}, f32[456,128]{1,0:T(8,128)S(1)}, u32[]{:S(2)}, u32[]{:S(2)}) collective-permute-start(f32[456,128]{1,0:T(8,128)S(1)} %get-tuple-element.36), channel_id=1, source_target_pairs={{0,1},{1,0},{2,3},{3,2},{4,5},{5,4},{6,7},{7,6},{8,9},{9,8},{10,11... | collective-permute-start | bytes 700424 | tf_op jit(solution)/shard_map/ppermute | solution.py:886
  15.1 7.4 %collective-permute-start.3 = (f32[456,128]{1,0:T(8,128)S(1)}, f32[456,128]{1,0:T(8,128)S(1)}, u32[]{:S(2)}, u32[]{:S(2)}) collective-permute-start(f32[456,128]{1,0:T(8,128)S(1)} %get-tuple-element.37), channel_id=1, source_target_pairs={{0,0},{1,2},{2,1},{3,4},{4,3},{5,6},{6,5},{7,8},{8,7},{9,10},{10,9... | collective-permute-start | bytes 700424 | tf_op jit(solution)/shard_map/ppermute | solution.py:888
  57.9 1.7 %collective-permute-start.4 = (f32[768,128]{1,0:T(8,128)S(1)}, f32[768,128]{1,0:T(8,128)S(1)}, u32[]{:S(2)}, u32[]{:S(2)}) collective-permute-start(f32[768,128]{1,0:T(8,128)S(1)} %bitcast.7), channel_id=1, source_target_pairs={{0,1},{1,0},{2,3},{3,2},{4,5},{5,4},{6,7},{7,6},{8,9},{9,8},{10,11... | collective-permute-start | bytes 1179656 | tf_op jit(solution)/shard_map/ppermute | solution.py:857
  86.9 2.9 %collective-permute-start.5 = (f32[384,128]{1,0:T(8,128)S(1)}, f32[384,128]{1,0:T(8,128)S(1)}, u32[]{:S(2)}, u32[]{:S(2)}) collective-permute-start(f32[384,128]{1,0:T(8,128)S(1)} %bitcast.9), channel_id=1, source_target_pairs={{0,1},{1,0},{2,3},{3,2},{4,5},{5,4},{6,7},{7,6},{8,9},{9,8},{10,11... | collective-permute-start | bytes 589832 | tf_op jit(solution)/shard_map/ppermute | solution.py:857

commit v5 on v4

--- a/solution.py
+++ b/solution.py
@@ -175,8 +175,14 @@
     return picked(jnp.broadcast_to(row, (count, LANES)), place)
 
 
-def pack_kernel(place, own, ends, above, below, swap, side, edge):
-    first_core = place[2] == 0
+def whereabouts():
+    core = lax.axis_index("core")
+    chip = lax.axis_index("y") * 4 + lax.axis_index("x")
+    return lax.axis_index("z"), 2 * chip + core, core
+
+
+def pack_kernel(own, ends, above, below, swap, side, edge):
+    first_core = whereabouts()[2] == 0
     low = lane_ids(88) < 64
     base = FIELDS * REACH
 
@@ -282,11 +288,12 @@
 
 
 def setup_kernel(
-    place, own, ends, above, below, swapped, sided, border,
+    own, ends, above, below, swapped, sided, border,
     m0, m1, m2, source, f0, g1, f1, g2, f2, message,
     cells, raw0, raw1, raw2, w0, w1, w2,
 ):
-    row_at, col_at, first_core = place[0], place[1], place[2] == 0
+    row_at, col_at, core = whereabouts()
+    first_core = core == 0
     rows_of = lambda n, low: low + lax.broadcasted_iota(jnp.int32, (n, LANES), 0)
     edge = jnp.zeros((16, LANES), F32)
     not_top, not_bottom = row_at > 0, row_at < 7
@@ -704,11 +711,12 @@
 
 
 def middle_kernel(
-    place, mine, other, m0, m1, m2, source, f0, g1, f1, g2, f2,
+    mine, other, m0, m1, m2, source, f0, g1, f1, g2, f2,
     m3, m4, m5, m6, product, solution, n0, h0, k1, h1, k2, h2, message,
     ordered, raw3, raw4, raw5, raw6, b3, v3, o3, b4, v4, o4, b5, v5, o5, b6,
     w0, w1, w2, near_maps, near_base, near_a, near_b,
 ):
+    place = whereabouts()
     for ref in (m3, raw3, b3, v3, o3):
         rows = ref.shape[2]
         clear(ref, (0, PAD), (rows - PAD, rows))
@@ -775,11 +783,12 @@
 
 
 def last_kernel(
-    place, mine, other, m0, m1, m2, source, m3, m4, m5, m6, product, before, n0, f0, k1, f1, k2, f2,
+    mine, other, m0, m1, m2, source, m3, m4, m5, m6, product, before, n0, f0, k1, f1, k2, f2,
     solution, residual,
     ordered, b3, v3, o3, b4, v4, o4, b5, v5, o5, b6,
     h0, h1, h2, w0, w1, w2, near_maps, near_base, near_a, near_b,
 ):
+    place = whereabouts()
     for ref in (b3, v3, o3):
         rows = ref.shape[2]
         clear(ref, (0, PAD), (rows - PAD, rows))
@@ -832,8 +841,6 @@
 
 def call(kernel, outs, scratch, *args):
     in_specs = [pl.BlockSpec(memory_space=pltpu.VMEM) for _ in args]
-    if args[0].dtype == jnp.int32 and args[0].ndim == 1:
-        in_specs[0] = pl.BlockSpec(memory_space=pltpu.SMEM)
     return pl.pallas_call(
         kernel,
         out_shape=[shape(*o) for o in outs],
@@ -858,12 +865,9 @@
 
 
 def local(guidance, seam_weight, source_label):
-    place = jnp.stack(
-        [lax.axis_index("z"), lax.axis_index(SIDES), lax.axis_index("core")]
-    ).astype(jnp.int32)
     down, up = pl.pallas_call(
         stack_kernel,
-        out_shape=[shape(UPDOWN_ROWS, LANES)] * 2,
+        out_shape=[pltpu.VMEM((UPDOWN_ROWS, LANES), F32)] * 2,
         in_specs=[pl.BlockSpec(memory_space=pltpu.HBM)] * 3,
         out_specs=[pl.BlockSpec(memory_space=pltpu.VMEM)] * 2,
         scratch_shapes=[
@@ -881,7 +885,7 @@
         pack_kernel,
         [(SIDE_ROWS, LANES)] * 2 + [(CHANNELS, 176, LANES)],
         [],
-        place, own, ends, above, below,
+        own, ends, above, below,
     )
     swapped = lax.ppermute(swap, "core", ring(2, 1))
     pairs = [(i, min(max(i + 2 * (i % 2) - 1, 0), 31)) for i in range(32)]
@@ -893,7 +897,7 @@
         setup_kernel,
         maps + [fields[0], fields[0], fields[1], fields[1], fields[2], fields[2], (6, LANES)],
         [field_shape(0, FIELDS)] + raws + fields,
-        place, own, ends, above, below, swapped, sided, border,
+        own, ends, above, below, swapped, sided, border,
     )
     mine, other = gathered(message)
     wholes = [whole_shape(level, CHANNELS) for level in (3, 4, 5) for _ in range(3)]
@@ -905,14 +909,14 @@
         + [(len(DIAMOND), 8, LANES)] + [fields[0]] * 3 + [fields[1]] * 2 + [fields[2]] * 2 + [(CHANNELS, LANES)],
         [(6, 256, LANES)] + [whole_shape(level, 4) for level in (3, 4, 5, 6)]
         + wholes + fields + near,
-        place, mine, other, m0, m1, m2, source, f0, g1, f1, g2, f2,
+        mine, other, m0, m1, m2, source, f0, g1, f1, g2, f2,
     )
     mine, other = gathered(message)
     outs = call(
         last_kernel,
         [(CHANNELS, 64, LANES)] * 2,
         [(CHANNELS, 256, LANES)] + wholes + fields + fields + near,
-        place, mine, other, m0, m1, m2, source, m3, m4, m5, m6, product,
+        mine, other, m0, m1, m2, source, m3, m4, m5, m6, product,
         solution, n0, h0, k1, h1, k2, h2,
     )
     return tuple(outs)

time: 96.2 us -> 92.2 us (0.958)
  Pallas kernels: 21.4 us -> 17.7 us
  local copies, waits for them, and re-layouts: 2.16 us -> 0.31 us
  waiting for transfers between devices: 8.87 us -> 10.6 us
    pallas_call x5, Pallas kernels: 19.5 us -> 16.6 us  [call(): pl.pallas_call(kernel, out_shape=[shape(*o) for o in outs], in_specs=in_s...]
    unnamed x4 -> x0, local copies, waits for them, and re-layouts: 1.85 us -> none
    ppermute x1, waiting for transfers between devices: 1.74 us -> 3.47 us  [local(): above = lax.ppermute(down, 'z', ring(8, 1))]
where the time goes in v5:
time: 92.2 us; the launch traced here: 92 us
  blocking collectives  50 us (54%)
  Pallas kernels  17.7 us (19%)
  starting transfers between devices  12.7 us (14%)
  waiting for transfers between devices  10.6 us (11%)
    all_to_all x2, blocking collectives, gathered(): mine = lax.all_to_all(sent, CHIPS, 0, 0, tiled=True)  50 us
    pallas_call x5, Pallas kernels, call(): pl.pallas_call(kernel, out_shape=[shape(*o) for o in outs], in_specs=in_s...  16.6 us
    ppermute x1, waiting for transfers between devices, local(): sided = lax.ppermute(side, SIDES, pairs)  4.34 us
    ppermute x1, starting transfers between devices, local(): below = lax.ppermute(up, 'z', ring(8, -1))  4.03 us
    ppermute x1, waiting for transfers between devices, local(): above = lax.ppermute(down, 'z', ring(8, 1))  3.47 us
    ppermute x1, starting transfers between devices, local(): sided = lax.ppermute(side, SIDES, pairs)  3.02 us
    ppermute x2, waiting for transfers between devices, gathered(): return (mine, lax.ppermute(mine, 'core', ring(2, 1)))  2.79 us
    ppermute x1, starting transfers between devices, local(): above = lax.ppermute(down, 'z', ring(8, 1))  2.54 us
  transfers between devices with their start and end apart: 6, of which 4 were waited for; matrix products, arithmetic and copies ran while one was open for 0% of the time, Pallas kernels for 0%

profile of v5, /device:TPU:1, one launch (start us, length us, event | category | flops | bytes accessed | tf_op | source)
XLA Modules:
  0.0 92.0 jit_solution(5871619831802471195)
XLA Ops:
  0.6 1.1 %shard_map.50 = (f32[288,128]{1,0:T(8,128)S(1)}, f32[288,128]{1,0:T(8,128)S(1)}) custom-call(f32[2,3,64,128]{3,2,1,0:T(8,128)} %guidance_in.1, s32[64,128]{1,0:T(8,128)} %weight_in.1, s32[64,128]{1,0:T(8,128)} %label_in.1), custom_call_target="tpu_custom_call" | custom-call | tf_op jit(solution)/shard_map/pallas_call | solution.py:868
  1.8 2.5 %collective-permute-start = (f32[288,128]{1,0:T(8,128)S(1)}, f32[288,128]{1,0:T(8,128)S(1)}, u32[]{:S(2)}, u32[]{:S(2)}) collective-permute-start(f32[288,128]{1,0:T(8,128)S(1)} %get-tuple-element.32.down), channel_id=1, source_target_pairs={{0,32},{32,64},{64,96},{96,128},{128,160},{160,192},{192,224},{224... | collective-permute-start | bytes 442376 | tf_op jit(solution)/shard_map/ppermute | solution.py:881
  4.3 4.0 %collective-permute-start.1 = (f32[288,128]{1,0:T(8,128)S(1)}, f32[288,128]{1,0:T(8,128)S(1)}, u32[]{:S(2)}, u32[]{:S(2)}) collective-permute-start(f32[288,128]{1,0:T(8,128)S(1)} %get-tuple-element.33.up), channel_id=1, source_target_pairs={{0,224},{32,0},{64,32},{96,64},{128,96},{160,128},{192,160},{224,1... | collective-permute-start | bytes 442376 | tf_op jit(solution)/shard_map/ppermute | solution.py:882
  8.4 3.5 %collective-permute-done.above = f32[288,128]{1,0:T(8,128)S(1)} collective-permute-done((f32[288,128]{1,0:T(8,128)S(1)}, f32[288,128]{1,0:T(8,128)S(1)}, u32[]{:S(2)}, u32[]{:S(2)}) %collective-permute-start) | collective-permute-done | bytes 147488 | tf_op jit(solution)/shard_map/ppermute | solution.py:881
  11.8 0.0 collective-permute-done.1.below
  11.8 0.5 shard_map.52
  12.3 1.3 %collective-permute-start.2 = (f32[456,128]{1,0:T(8,128)S(1)}, f32[456,128]{1,0:T(8,128)S(1)}, u32[]{:S(2)}, u32[]{:S(2)}) collective-permute-start(f32[456,128]{1,0:T(8,128)S(1)} %get-tuple-element.36), channel_id=1, source_target_pairs={{0,1},{1,0},{2,3},{3,2},{4,5},{5,4},{6,7},{7,6},{8,9},{9,8},{10,11... | collective-permute-start | bytes 700424 | tf_op jit(solution)/shard_map/ppermute | solution.py:890
  13.6 3.0 %collective-permute-start.3 = (f32[456,128]{1,0:T(8,128)S(1)}, f32[456,128]{1,0:T(8,128)S(1)}, u32[]{:S(2)}, u32[]{:S(2)}) collective-permute-start(f32[456,128]{1,0:T(8,128)S(1)} %get-tuple-element.37), channel_id=1, source_target_pairs={{0,0},{1,2},{2,1},{3,4},{4,3},{5,6},{6,5},{7,8},{8,7},{9,10},{10,9... | collective-permute-start | bytes 700424 | tf_op jit(solution)/shard_map/ppermute | solution.py:892
  16.6 0.0 collective-permute-done.2.swapped
  16.7 4.3 %collective-permute-done.3.sided = f32[456,128]{1,0:T(8,128)S(1)} collective-permute-done((f32[456,128]{1,0:T(8,128)S(1)}, f32[456,128]{1,0:T(8,128)S(1)}, u32[]{:S(2)}, u32[]{:S(2)}) %collective-permute-start.3) | collective-permute-done | bytes 233504 | tf_op jit(solution)/shard_map/ppermute | solution.py:892
  21.0 3.0 %shard_map.53 = (f32[5,2,208,128]{3,2,1,0:T(8,128)S(1)}, f32[6,2,112,128]{3,2,1,0:T(8,128)S(1)}, f32[6,2,64,128]{3,2,1,0:T(8,128)S(1)}, f32[3,2,208,128]{3,2,1,0...) custom-call(f32[5,64,128]{2,1,0:T(8,128)S(1)} %get-tuple-element.34., ...), custom_call_target="tpu_custom_call" | custom-call | bytes 8000000 | tf_op jit(solution)/shard_map/pallas_call | solution.py:844
  24.0 0.2 broadcast_in_dim.15
  24.2 31.6 %all_to_all.10 = f32[128,1,768]{2,1,0:T(1,128)S(1)} all-to-all(f32[128,1,768]{2,1,0:T(1,128)S(1)} %broadcast_in_dim.15), channel_id=1, replica_groups=mesh['z'=8,'y'=4,'x'=4,'core'=2] {'z','y','x'}, dimensions={0} | all-to-all | bytes 786432 | tf_op jit(solution)/shard_map/all_to_all | solution.py:862
  55.8 0.0 collective-permute-start.4
  55.8 1.7 %collective-permute-done.4.other = f32[768,128]{1,0:T(8,128)S(1)} collective-permute-done((f32[768,128]{1,0:T(8,128)S(1)}, f32[768,128]{1,0:T(8,128)S(1)}, u32[]{:S(2)}, u32[]{:S(2)}) %collective-permute-start.4) | collective-permute-done | bytes 393248 | tf_op jit(solution)/shard_map/ppermute | solution.py:864
  57.5 7.7 %shard_map.54 = (f32[6,6,80,128]{3,2,1,0:T(8,128)S(1)}, f32[6,2,48,128]{3,2,1,0:T(8,128)S(1)}, f32[6,1,32,128]{3,2,1,0:T(8,128)S(1)}, f32[6,1,24,128]{3,2,1,0:T(...) custom-call(f32[768,128]{1,0:T(8,128)S(1)} %bitcast.5, ...), custom_call_target="tpu_custom_call" | custom-call | bytes 8000000 | tf_op jit(solution)/shard_map/pallas_call | solution.py:844
  65.3 0.1 broadcast_in_dim.17
  65.4 18.4 %all_to_all.11 = f32[128,1,384]{2,1,0:T(1,128)S(1)} all-to-all(f32[128,1,384]{2,1,0:T(1,128)S(1)} %broadcast_in_dim.17), channel_id=1, replica_groups=mesh['z'=8,'y'=4,'x'=4,'core'=2] {'z','y','x'}, dimensions={0} | all-to-all | bytes 393216 | tf_op jit(solution)/shard_map/all_to_all | solution.py:862
  83.8 1.8 %collective-permute-start.5 = (f32[384,128]{1,0:T(8,128)S(1)}, f32[384,128]{1,0:T(8,128)S(1)}, u32[]{:S(2)}, u32[]{:S(2)}) collective-permute-start(f32[384,128]{1,0:T(8,128)S(1)} %bitcast.6), channel_id=1, source_target_pairs={{0,1},{1,0},{2,3},{3,2},{4,5},{5,4},{6,7},{7,6},{8,9},{9,8},{10,11... | collective-permute-start | bytes 589832 | tf_op jit(solution)/shard_map/ppermute | solution.py:864
  85.6 1.1 %collective-permute-done.5.other = f32[384,128]{1,0:T(8,128)S(1)} collective-permute-done((f32[384,128]{1,0:T(8,128)S(1)}, f32[384,128]{1,0:T(8,128)S(1)}, u32[]{:S(2)}, u32[]{:S(2)}) %collective-permute-start.5) | collective-permute-done | bytes 196640 | tf_op jit(solution)/shard_map/ppermute | solution.py:864
  86.7 5.4 %shard_map.55 = (f32[3,64,128]{2,1,0:T(8,128)}, f32[3,64,128]{2,1,0:T(8,128)}) custom-call(f32[384,128]{1,0:T(8,128)S(1)} %bitcast.7, f32[384,128]{1,0:T(8,128)S(1)} %collective-permute-done.5.other, f32[5,2,208,128]{3,2,1,0:T(8,128)S(1)} %get-tuple-element.40.m0, f32[6,2,112,128]{3,2,1,0:T(8,128)S(1)} %get-tuple-element.41.m1, ...), custom_call_target="tpu_custom_call" | custom-call | bytes 8000000 | tf_op jit(solution)/shard_map/pallas_call | solution.py:844
  (1 shorter events, 0.0 us)
Async XLA Ops:
  1.8 10.1 %collective-permute-start = (f32[288,128]{1,0:T(8,128)S(1)}, f32[288,128]{1,0:T(8,128)S(1)}, u32[]{:S(2)}, u32[]{:S(2)}) collective-permute-start(f32[288,128]{1,0:T(8,128)S(1)} %get-tuple-element.32.down), channel_id=1, source_target_pairs={{0,32},{32,64},{64,96},{96,128},{128,160},{160,192},{192,224},{224... | collective-permute-start | bytes 442376 | tf_op jit(solution)/shard_map/ppermute | solution.py:881
  4.3 7.5 %collective-permute-start.1 = (f32[288,128]{1,0:T(8,128)S(1)}, f32[288,128]{1,0:T(8,128)S(1)}, u32[]{:S(2)}, u32[]{:S(2)}) collective-permute-start(f32[288,128]{1,0:T(8,128)S(1)} %get-tuple-element.33.up), channel_id=1, source_target_pairs={{0,224},{32,0},{64,32},{96,64},{128,96},{160,128},{192,160},{224,1... | collective-permute-start | bytes 442376 | tf_op jit(solution)/shard_map/ppermute | solution.py:882
  12.3 4.3 %collective-permute-start.2 = (f32[456,128]{1,0:T(8,128)S(1)}, f32[456,128]{1,0:T(8,128)S(1)}, u32[]{:S(2)}, u32[]{:S(2)}) collective-permute-start(f32[456,128]{1,0:T(8,128)S(1)} %get-tuple-element.36), channel_id=1, source_target_pairs={{0,1},{1,0},{2,3},{3,2},{4,5},{5,4},{6,7},{7,6},{8,9},{9,8},{10,11... | collective-permute-start | bytes 700424 | tf_op jit(solution)/shard_map/ppermute | solution.py:890
  13.6 7.4 %collective-permute-start.3 = (f32[456,128]{1,0:T(8,128)S(1)}, f32[456,128]{1,0:T(8,128)S(1)}, u32[]{:S(2)}, u32[]{:S(2)}) collective-permute-start(f32[456,128]{1,0:T(8,128)S(1)} %get-tuple-element.37), channel_id=1, source_target_pairs={{0,0},{1,2},{2,1},{3,4},{4,3},{5,6},{6,5},{7,8},{8,7},{9,10},{10,9... | collective-permute-start | bytes 700424 | tf_op jit(solution)/shard_map/ppermute | solution.py:892
  55.8 1.7 %collective-permute-start.4 = (f32[768,128]{1,0:T(8,128)S(1)}, f32[768,128]{1,0:T(8,128)S(1)}, u32[]{:S(2)}, u32[]{:S(2)}) collective-permute-start(f32[768,128]{1,0:T(8,128)S(1)} %bitcast.4), channel_id=1, source_target_pairs={{0,1},{1,0},{2,3},{3,2},{4,5},{5,4},{6,7},{7,6},{8,9},{9,8},{10,11... | collective-permute-start | bytes 1179656 | tf_op jit(solution)/shard_map/ppermute | solution.py:864
  83.8 2.9 %collective-permute-start.5 = (f32[384,128]{1,0:T(8,128)S(1)}, f32[384,128]{1,0:T(8,128)S(1)}, u32[]{:S(2)}, u32[]{:S(2)}) collective-permute-start(f32[384,128]{1,0:T(8,128)S(1)} %bitcast.6), channel_id=1, source_target_pairs={{0,1},{1,0},{2,3},{3,2},{4,5},{5,4},{6,7},{7,6},{8,9},{9,8},{10,11... | collective-permute-start | bytes 589832 | tf_op jit(solution)/shard_map/ppermute | solution.py:864

commit v6 on v5

--- a/solution.py
+++ b/solution.py
@@ -247,6 +247,12 @@
     return rows
 
 
+def repeat(rows, message):
+    block = jnp.concatenate(rows * (24 // len(rows)), axis=0)
+    for i in range(message.shape[0] // 24):
+        message[24 * i : 24 * i + 24, :] = block
+
+
 def down_levels(fields, bases, work, maps, ranges):
     for level in range(3):
         local_down(
@@ -278,6 +284,8 @@
 )
 FIRST_UP = ((32, 160, 128), (8, 88, 80), (0, 48, 48))
 LATER_UP = ((56, 136, 80), (24, 72, 48), (8, 40, 32))
+FIRST_SPANS = ((8, 88, 80), (0, 48, 48))
+LATER_SPANS = ((24, 72, 48), (8, 40, 32))
 
 
 def clear(ref, *bounds):
@@ -319,13 +327,6 @@
         cells[a, 1, 104:192, :] = jnp.where(
             inside & (not_bottom | (rows_of(88, 96) < 128)), bottom, 0.0
         )
-    for ref in (m0, raw0, source, f0, w0):
-        clear(ref, (0, 16), (192, 208))
-    for ref, rows in ((m1, 96), (raw1, 96), (g1, 96), (f1, 96), (w1, 96)):
-        clear(ref, (0, 8), (rows + 8, rows + 16))
-    for ref, rows in ((m2, 48), (raw2, 48), (g2, 48), (f2, 48), (w2, 48)):
-        clear(ref, (0, 8), (rows + 8, rows + 16))
-
     def fine(start):
         size = 176
         at = pl.ds(start, size)
@@ -418,9 +419,7 @@
     cell = lane_ids(8) >> 3
     turned = pltpu.roll(pltpu.roll(rightward, LANES - 8, 1), 7, 0)
     ends = jnp.where(row == 7, downward, jnp.where(cell == 15, rightward, turned))
-    rows = own_row(jnp.concatenate(tiles + [upward, leftward, ends], axis=0))
-    for i in range(6):
-        message[i : i + 1, :] = rows[i]
+    repeat(own_row(jnp.concatenate(tiles + [upward, leftward, ends], axis=0)), message)
 
 
 def unpack(place, mine, other, count, stride, ordered, put):
@@ -633,7 +632,9 @@
     return jnp.where(low, jnp.where(fits, here, after), jnp.where(fits, before, here))
 
 
-def correct_level_two(place, bases, fields, maps, f2, near_maps, near_base, near_a, near_b):
+def correct_level_two(
+    place, bases, fields, maps, f2, target, near_maps, near_base, near_a, near_b
+):
     for m in range(4):
         near_maps[m, 0, PAD : PAD + 24, :] = window(maps[3], m, place)
     edge = jnp.zeros((PAD, LANES), F32)
@@ -653,30 +654,30 @@
             part = wide[h][24 * c : 24 * c + 24]
             for offset in range(2):
                 at = pl.ds(PAD + offset, 24, stride=2)
-                f2[c, h, at, :] = f2[c, h, at, :] + part
-
-
-def add_rows(field, coarse, low, high, size):
+                target[c, h, at, :] = f2[c, h, at, :] + part
+
+
+def add_rows(target, field, coarse, low, high, size):
     def body(start):
         for c in range(CHANNELS):
             for h in range(2):
                 part = coarse[c, h, pl.ds(start, size), :]
                 for offset in range(2):
                     at = pl.ds(2 * start - PAD + offset, size, stride=2)
-                    field[c, h, at, :] = field[c, h, at, :] + part
+                    target[c, h, at, :] = field[c, h, at, :] + part
 
     chunks(low, high, size, body)
 
 
-def up_levels(ranges, fields, bases, works, maps, extra):
+def up_levels(ranges, spans, before, fields, bases, works, maps, extra):
     low, high, size = ranges[2]
     stencil("relax", works[2], fields[2], bases[2], maps[2], low, high, size, 4)
     stencil("relax", fields[2], works[2], bases[2], maps[2], low, high, size, 4)
-    add_rows(fields[1], fields[2], 0, 48, 48)
+    add_rows(fields[1], before[1], fields[2], *spans[1])
     low, high, size = ranges[1]
     stencil("relax", works[1], fields[1], bases[1], maps[1], low, high, size, 2)
     stencil("relax", fields[1], works[1], bases[1], maps[1], low, high, size, 2)
-    add_rows(fields[0], fields[1], 0, 96, 96)
+    add_rows(fields[0], before[0], fields[1], *spans[0])
     low, high, size = ranges[0]
     stencil("relax", works[0], fields[0], bases[0], maps[0], low, high, size, 1)
     if extra is None:
@@ -685,13 +686,6 @@
         stencil(
             "relax_add", fields[0], works[0], bases[0], maps[0], low, high, size, 1, extra=extra
         )
-
-
-def copy_field(source, target):
-    count, halves, rows, _ = source.shape
-    for c in range(count):
-        for h in range(halves):
-            target[c, h] = source[c, h]
 
 
 def complete_maps(raw):
@@ -717,7 +711,7 @@
     w0, w1, w2, near_maps, near_base, near_a, near_b,
 ):
     place = whereabouts()
-    for ref in (m3, raw3, b3, v3, o3):
+    for ref in (m3, b3, v3):
         rows = ref.shape[2]
         clear(ref, (0, PAD), (rows - PAD, rows))
         for index in range(ref.shape[0]):
@@ -726,9 +720,6 @@
     for ref in (b4, v4, o4, b5, v5, o5):
         rows = ref.shape[2]
         clear(ref, (0, PAD), (rows - PAD, rows))
-    for ref in (w0, w1, w2, n0):
-        rows = ref.shape[2]
-        clear(ref, (0, rows))
 
     def put(f, start, group, tile):
         if f < CHANNELS:
@@ -751,22 +742,16 @@
         3, {3: b3, 4: b4, 5: b5, 6: b6}, {3: v3, 4: v4, 5: v5}, {3: o3, 4: o4, 5: o5}, maps,
         product,
     )
-    copy_field(f0, solution)
-    copy_field(f1, h1)
-    copy_field(f2, h2)
     correct_level_two(
-        place, {3: b3}, {3: v3}, maps, h2, near_maps, near_base, near_a, near_b
+        place, {3: b3}, {3: v3}, maps, f2, h2, near_maps, near_base, near_a, near_b
     )
     local_maps = (m0, m1, m2)
-    up_levels(FIRST_UP, (solution, h1, h2), (source, g1, g2), (w0, w1, w2), local_maps, None)
+    up_levels(
+        FIRST_UP, FIRST_SPANS, (f0, f1), (solution, h1, h2), (source, g1, g2), (w0, w1, w2), local_maps, None,
+    )
     stencil("difference", n0, solution, source, m0, 32, 160, 128, 1)
-    for ref in (h0, k1, k2):
-        rows = ref.shape[2]
-        clear(ref, (0, rows))
     tiles = down_levels((h0, h1, h2), (n0, k1, k2), (w0, w1, w2), local_maps, LATER_DOWN)
-    rows = own_row(jnp.concatenate(tiles, axis=0))
-    for i in range(CHANNELS):
-        message[i : i + 1, :] = rows[i]
+    repeat(own_row(jnp.concatenate(tiles, axis=0)), message)
 
 
 def scale_base(base, maps):
@@ -789,7 +774,7 @@
     h0, h1, h2, w0, w1, w2, near_maps, near_base, near_a, near_b,
 ):
     place = whereabouts()
-    for ref in (b3, v3, o3):
+    for ref in (b3, v3):
         rows = ref.shape[2]
         clear(ref, (0, PAD), (rows - PAD, rows))
         for index in range(ref.shape[0]):
@@ -798,9 +783,6 @@
     for ref in (b4, v4, o4, b5, v5, o5):
         rows = ref.shape[2]
         clear(ref, (0, PAD), (rows - PAD, rows))
-    for ref in (w0, w1, w2):
-        rows = ref.shape[2]
-        clear(ref, (0, rows))
 
     def put(f, start, group, tile):
         b3[f, 1 + group, pl.ds(start, 8), :] = tile
@@ -812,14 +794,13 @@
         3, {3: b3, 4: b4, 5: b5, 6: b6}, {3: v3, 4: v4, 5: v5}, {3: o3, 4: o4, 5: o5}, maps,
         product,
     )
-    copy_field(f0, h0)
-    copy_field(f1, h1)
-    copy_field(f2, h2)
     correct_level_two(
-        place, {3: b3}, {3: v3}, maps, h2, near_maps, near_base, near_a, near_b
+        place, {3: b3}, {3: v3}, maps, f2, h2, near_maps, near_base, near_a, near_b
     )
     local_maps = (m0, m1, m2)
-    up_levels(LATER_UP, (h0, h1, h2), (n0, k1, k2), (w0, w1, w2), local_maps, before)
+    up_levels(
+        LATER_UP, LATER_SPANS, (f0, f1), (h0, h1, h2), (n0, k1, k2), (w0, w1, w2), local_maps, before,
+    )
     stencil("final", w0, h0, source, m0, 64, 128, 64, 1)
     for c in range(CHANNELS):
         solution[c] = h0[c, 0, PAD + 64 : PAD + 128, :]
@@ -857,10 +838,8 @@
 
 
 def gathered(message):
-    rows = message.shape[0]
-    sent = jnp.broadcast_to(message.reshape(1, 1, rows * LANES), (128, 1, rows * LANES))
-    mine = lax.all_to_all(sent, CHIPS, 0, 0, tiled=True)
-    mine = mine.reshape(128 * rows, LANES)
+    mine = lax.all_to_all(message.reshape(128, 1, -1), CHIPS, 0, 0, tiled=True)
+    mine = mine.reshape(message.shape)
     return mine, lax.ppermute(mine, "core", ring(2, 1))
 
 
@@ -895,7 +874,7 @@
     raws = [field_shape(level, 4) for level in range(3)]
     m0, m1, m2, source, f0, g1, f1, g2, f2, message = call(
         setup_kernel,
-        maps + [fields[0], fields[0], fields[1], fields[1], fields[2], fields[2], (6, LANES)],
+        maps + [fields[0], fields[0], fields[1], fields[1], fields[2], fields[2], (6 * 128, LANES)],
         [field_shape(0, FIELDS)] + raws + fields,
         own, ends, above, below, swapped, sided, border,
     )
@@ -906,7 +885,7 @@
     m3, m4, m5, m6, product, solution, n0, h0, k1, h1, k2, h2, message = call(
         middle_kernel,
         [whole_shape(level, 6) for level in (3, 4, 5, 6)]
-        + [(len(DIAMOND), 8, LANES)] + [fields[0]] * 3 + [fields[1]] * 2 + [fields[2]] * 2 + [(CHANNELS, LANES)],
+        + [(len(DIAMOND), 8, LANES)] + [fields[0]] * 3 + [fields[1]] * 2 + [fields[2]] * 2 + [(CHANNELS * 128, LANES)],
         [(6, 256, LANES)] + [whole_shape(level, 4) for level in (3, 4, 5, 6)]
         + wholes + fields + near,
         mine, other, m0, m1, m2, source, f0, g1, f1, g2, f2,

time: 92.2 us -> 92.6 us (level)
  no operation moved by 1% of the time
where the time goes in v6:
time: 92.6 us; the launch traced here: 92.4 us
  blocking collectives  50 us (54%)
  Pallas kernels  18.4 us (20%)
  starting transfers between devices  12.7 us (14%)
  waiting for transfers between devices  10.6 us (11%)
    all_to_all x2, blocking collectives, gathered(): mine = lax.all_to_all(message.reshape(128, 1, -1), CHIPS, 0, 0, tiled=True)  50 us
    pallas_call x5, Pallas kernels, call(): pl.pallas_call(kernel, out_shape=[shape(*o) for o in outs], in_specs=in_s...  17.2 us
    ppermute x1, waiting for transfers between devices, local(): sided = lax.ppermute(side, SIDES, pairs)  4.34 us
    ppermute x1, starting transfers between devices, local(): below = lax.ppermute(up, 'z', ring(8, -1))  4.03 us
    ppermute x1, waiting for transfers between devices, local(): above = lax.ppermute(down, 'z', ring(8, 1))  3.47 us
    ppermute x1, starting transfers between devices, local(): sided = lax.ppermute(side, SIDES, pairs)  3.02 us
    ppermute x2, waiting for transfers between devices, gathered(): return (mine, lax.ppermute(mine, 'core', ring(2, 1)))  2.79 us
    ppermute x1, starting transfers between devices, local(): above = lax.ppermute(down, 'z', ring(8, 1))  2.54 us
  transfers between devices with their start and end apart: 6, of which 4 were waited for; matrix products, arithmetic and copies ran while one was open for 0% of the time, Pallas kernels for 0%

profile of v6, /device:TPU:1, one launch (start us, length us, event | category | flops | bytes accessed | tf_op | source)
XLA Modules:
  0.0 92.4 jit_solution(5206611294442056555)
XLA Ops:
  0.6 1.1 %shard_map.50 = (f32[288,128]{1,0:T(8,128)S(1)}, f32[288,128]{1,0:T(8,128)S(1)}) custom-call(f32[2,3,64,128]{3,2,1,0:T(8,128)} %guidance_in.1, s32[64,128]{1,0:T(8,128)} %weight_in.1, s32[64,128]{1,0:T(8,128)} %label_in.1), custom_call_target="tpu_custom_call" | custom-call | tf_op jit(solution)/shard_map/pallas_call | solution.py:847
  1.8 2.5 %collective-permute-start = (f32[288,128]{1,0:T(8,128)S(1)}, f32[288,128]{1,0:T(8,128)S(1)}, u32[]{:S(2)}, u32[]{:S(2)}) collective-permute-start(f32[288,128]{1,0:T(8,128)S(1)} %get-tuple-element.32.down), channel_id=1, source_target_pairs={{0,32},{32,64},{64,96},{96,128},{128,160},{160,192},{192,224},{224... | collective-permute-start | bytes 442376 | tf_op jit(solution)/shard_map/ppermute | solution.py:860
  4.3 4.0 %collective-permute-start.1 = (f32[288,128]{1,0:T(8,128)S(1)}, f32[288,128]{1,0:T(8,128)S(1)}, u32[]{:S(2)}, u32[]{:S(2)}) collective-permute-start(f32[288,128]{1,0:T(8,128)S(1)} %get-tuple-element.33.up), channel_id=1, source_target_pairs={{0,224},{32,0},{64,32},{96,64},{128,96},{160,128},{192,160},{224,1... | collective-permute-start | bytes 442376 | tf_op jit(solution)/shard_map/ppermute | solution.py:861
  8.4 3.5 %collective-permute-done.above = f32[288,128]{1,0:T(8,128)S(1)} collective-permute-done((f32[288,128]{1,0:T(8,128)S(1)}, f32[288,128]{1,0:T(8,128)S(1)}, u32[]{:S(2)}, u32[]{:S(2)}) %collective-permute-start) | collective-permute-done | bytes 147488 | tf_op jit(solution)/shard_map/ppermute | solution.py:860
  11.8 0.0 collective-permute-done.1.below
  11.8 0.5 shard_map.52
  12.3 1.3 %collective-permute-start.2 = (f32[456,128]{1,0:T(8,128)S(1)}, f32[456,128]{1,0:T(8,128)S(1)}, u32[]{:S(2)}, u32[]{:S(2)}) collective-permute-start(f32[456,128]{1,0:T(8,128)S(1)} %get-tuple-element.36), channel_id=1, source_target_pairs={{0,1},{1,0},{2,3},{3,2},{4,5},{5,4},{6,7},{7,6},{8,9},{9,8},{10,11... | collective-permute-start | bytes 700424 | tf_op jit(solution)/shard_map/ppermute | solution.py:869
  13.6 3.0 %collective-permute-start.3 = (f32[456,128]{1,0:T(8,128)S(1)}, f32[456,128]{1,0:T(8,128)S(1)}, u32[]{:S(2)}, u32[]{:S(2)}) collective-permute-start(f32[456,128]{1,0:T(8,128)S(1)} %get-tuple-element.37), channel_id=1, source_target_pairs={{0,0},{1,2},{2,1},{3,4},{4,3},{5,6},{6,5},{7,8},{8,7},{9,10},{10,9... | collective-permute-start | bytes 700424 | tf_op jit(solution)/shard_map/ppermute | solution.py:871
  16.6 0.0 collective-permute-done.2.swapped
  16.7 4.3 %collective-permute-done.3.sided = f32[456,128]{1,0:T(8,128)S(1)} collective-permute-done((f32[456,128]{1,0:T(8,128)S(1)}, f32[456,128]{1,0:T(8,128)S(1)}, u32[]{:S(2)}, u32[]{:S(2)}) %collective-permute-start.3) | collective-permute-done | bytes 233504 | tf_op jit(solution)/shard_map/ppermute | solution.py:871
  21.0 3.1 %shard_map.53 = (f32[5,2,208,128]{3,2,1,0:T(8,128)S(1)}, f32[6,2,112,128]{3,2,1,0:T(8,128)S(1)}, f32[6,2,64,128]{3,2,1,0:T(8,128)S(1)}, f32[3,2,208,128]{3,2,1,0...) custom-call(f32[5,64,128]{2,1,0:T(8,128)S(1)} %get-tuple-element.34., ...), custom_call_target="tpu_custom_call" | custom-call | bytes 8000000 | tf_op jit(solution)/shard_map/pallas_call | solution.py:825
  24.1 31.6 %all_to_all.10 = f32[128,1,768]{2,1,0:T(1,128)S(1)} all-to-all(f32[128,1,768]{2,1,0:T(1,128)S(1)} %bitcast.8), channel_id=1, replica_groups=mesh['z'=8,'y'=4,'x'=4,'core'=2] {'z','y','x'}, dimensions={0} | all-to-all | bytes 786432 | tf_op jit(solution)/shard_map/all_to_all | solution.py:841
  55.7 0.0 collective-permute-start.4
  55.8 1.7 %collective-permute-done.4.other = f32[768,128]{1,0:T(8,128)S(1)} collective-permute-done((f32[768,128]{1,0:T(8,128)S(1)}, f32[768,128]{1,0:T(8,128)S(1)}, u32[]{:S(2)}, u32[]{:S(2)}) %collective-permute-start.4) | collective-permute-done | bytes 393248 | tf_op jit(solution)/shard_map/ppermute | solution.py:843
  57.5 8.1 %shard_map.54 = (f32[6,6,80,128]{3,2,1,0:T(8,128)S(1)}, f32[6,2,48,128]{3,2,1,0:T(8,128)S(1)}, f32[6,1,32,128]{3,2,1,0:T(8,128)S(1)}, f32[6,1,24,128]{3,2,1,0:T(...) custom-call(f32[768,128]{1,0:T(8,128)S(1)} %bitcast.5, ...), custom_call_target="tpu_custom_call" | custom-call | bytes 8000000 | tf_op jit(solution)/shard_map/pallas_call | solution.py:825
  65.6 18.4 %all_to_all.11 = f32[128,1,384]{2,1,0:T(1,128)S(1)} all-to-all(f32[128,1,384]{2,1,0:T(1,128)S(1)} %bitcast.9), channel_id=1, replica_groups=mesh['z'=8,'y'=4,'x'=4,'core'=2] {'z','y','x'}, dimensions={0} | all-to-all | bytes 393216 | tf_op jit(solution)/shard_map/all_to_all | solution.py:841
  84.0 1.8 %collective-permute-start.5 = (f32[384,128]{1,0:T(8,128)S(1)}, f32[384,128]{1,0:T(8,128)S(1)}, u32[]{:S(2)}, u32[]{:S(2)}) collective-permute-start(f32[384,128]{1,0:T(8,128)S(1)} %bitcast.6), channel_id=1, source_target_pairs={{0,1},{1,0},{2,3},{3,2},{4,5},{5,4},{6,7},{7,6},{8,9},{9,8},{10,11... | collective-permute-start | bytes 589832 | tf_op jit(solution)/shard_map/ppermute | solution.py:843
  85.8 1.1 %collective-permute-done.5.other = f32[384,128]{1,0:T(8,128)S(1)} collective-permute-done((f32[384,128]{1,0:T(8,128)S(1)}, f32[384,128]{1,0:T(8,128)S(1)}, u32[]{:S(2)}, u32[]{:S(2)}) %collective-permute-start.5) | collective-permute-done | bytes 196640 | tf_op jit(solution)/shard_map/ppermute | solution.py:843
  86.9 5.5 %shard_map.55 = (f32[3,64,128]{2,1,0:T(8,128)}, f32[3,64,128]{2,1,0:T(8,128)}) custom-call(f32[384,128]{1,0:T(8,128)S(1)} %bitcast.7, f32[384,128]{1,0:T(8,128)S(1)} %collective-permute-done.5.other, f32[5,2,208,128]{3,2,1,0:T(8,128)S(1)} %get-tuple-element.40.m0, f32[6,2,112,128]{3,2,1,0:T(8,128)S(1)} %get-tuple-element.41.m1, ...), custom_call_target="tpu_custom_call" | custom-call | bytes 8000000 | tf_op jit(solution)/shard_map/pallas_call | solution.py:825
  (1 shorter events, 0.0 us)
Async XLA Ops:
  1.8 10.1 %collective-permute-start = (f32[288,128]{1,0:T(8,128)S(1)}, f32[288,128]{1,0:T(8,128)S(1)}, u32[]{:S(2)}, u32[]{:S(2)}) collective-permute-start(f32[288,128]{1,0:T(8,128)S(1)} %get-tuple-element.32.down), channel_id=1, source_target_pairs={{0,32},{32,64},{64,96},{96,128},{128,160},{160,192},{192,224},{224... | collective-permute-start | bytes 442376 | tf_op jit(solution)/shard_map/ppermute | solution.py:860
  4.3 7.5 %collective-permute-start.1 = (f32[288,128]{1,0:T(8,128)S(1)}, f32[288,128]{1,0:T(8,128)S(1)}, u32[]{:S(2)}, u32[]{:S(2)}) collective-permute-start(f32[288,128]{1,0:T(8,128)S(1)} %get-tuple-element.33.up), channel_id=1, source_target_pairs={{0,224},{32,0},{64,32},{96,64},{128,96},{160,128},{192,160},{224,1... | collective-permute-start | bytes 442376 | tf_op jit(solution)/shard_map/ppermute | solution.py:861
  12.3 4.3 %collective-permute-start.2 = (f32[456,128]{1,0:T(8,128)S(1)}, f32[456,128]{1,0:T(8,128)S(1)}, u32[]{:S(2)}, u32[]{:S(2)}) collective-permute-start(f32[456,128]{1,0:T(8,128)S(1)} %get-tuple-element.36), channel_id=1, source_target_pairs={{0,1},{1,0},{2,3},{3,2},{4,5},{5,4},{6,7},{7,6},{8,9},{9,8},{10,11... | collective-permute-start | bytes 700424 | tf_op jit(solution)/shard_map/ppermute | solution.py:869
  13.6 7.4 %collective-permute-start.3 = (f32[456,128]{1,0:T(8,128)S(1)}, f32[456,128]{1,0:T(8,128)S(1)}, u32[]{:S(2)}, u32[]{:S(2)}) collective-permute-start(f32[456,128]{1,0:T(8,128)S(1)} %get-tuple-element.37), channel_id=1, source_target_pairs={{0,0},{1,2},{2,1},{3,4},{4,3},{5,6},{6,5},{7,8},{8,7},{9,10},{10,9... | collective-permute-start | bytes 700424 | tf_op jit(solution)/shard_map/ppermute | solution.py:871
  55.7 1.7 %collective-permute-start.4 = (f32[768,128]{1,0:T(8,128)S(1)}, f32[768,128]{1,0:T(8,128)S(1)}, u32[]{:S(2)}, u32[]{:S(2)}) collective-permute-start(f32[768,128]{1,0:T(8,128)S(1)} %bitcast.4), channel_id=1, source_target_pairs={{0,1},{1,0},{2,3},{3,2},{4,5},{5,4},{6,7},{7,6},{8,9},{9,8},{10,11... | collective-permute-start | bytes 1179656 | tf_op jit(solution)/shard_map/ppermute | solution.py:843
  84.0 2.9 %collective-permute-start.5 = (f32[384,128]{1,0:T(8,128)S(1)}, f32[384,128]{1,0:T(8,128)S(1)}, u32[]{:S(2)}, u32[]{:S(2)}) collective-permute-start(f32[384,128]{1,0:T(8,128)S(1)} %bitcast.6), channel_id=1, source_target_pairs={{0,1},{1,0},{2,3},{3,2},{4,5},{5,4},{6,7},{7,6},{8,9},{9,8},{10,11... | collective-permute-start | bytes 589832 | tf_op jit(solution)/shard_map/ppermute | solution.py:843

commit v7 on v6

--- a/solution.py
+++ b/solution.py
@@ -16,6 +16,7 @@
 SIDES = ("y", "x", "core")
 CHIPS = ("z", "y", "x")
 LOCAL_ROWS = (192, 96, 48)
+STEP, STEP_R, STEP_F, STEP_C, STEP_A, STEP_W = 8, 16, 16, 16, 8, 16
 UP, DOWN, LEFT, RIGHT, SCALE, INVERSE = range(6)
 
 
@@ -56,22 +57,13 @@
     return jnp.take_along_axis(x, lanes, axis=1, mode="promise_in_bounds")
 
 
-def chunks(low, high, size, body):
-    count = (high - low) // size
-    assert count * size == high - low
-
-    def step(i, carry):
-        body(pl.multiple_of(PAD + low + i * size, 8))
-        return carry
-
-    if count == 1:
-        body(PAD + low)
-    else:
-        lax.fori_loop(0, count, step, 0)
+def chunks(low, high, step, body):
+    for start in range(low, high, step):
+        body(PAD + start, min(step, high - start))
 
 
 def stencil(mode, target, field, base, maps, low, high, size, width=1, halves=2, first=0, extra=None):
-    def body(start):
+    def body(start, size):
         at = pl.ds(start, size)
         span = range(first, first + halves)
         coef = [[maps[m, h, at, :] for h in span] for m in range(4)]
@@ -102,7 +94,7 @@
                     result = maps[SCALE, h, at, :] * (base[c, h, at, :] + total)
                 target[c, h, at, :] = result
 
-    chunks(low, high, size, body)
+    chunks(low, high, STEP, body)
 
 
 def scaled_maps(raw, factor):
@@ -225,7 +217,7 @@
 
     low, high, size = next_rows
 
-    def body(start):
+    def body(start, size):
         at = pl.ds(start, size)
         for h in range(2):
             inverse = 0.25 * next_maps[INVERSE, h, at, :]
@@ -233,7 +225,7 @@
                 even, odd = even_odd(work, (c, h), 2 * start - PAD, size)
                 next_base[c, h, at, :] = pair_sum(even + odd, width) * inverse
 
-    chunks(low, high, size, body)
+    chunks(low, high, STEP_R, body)
 
 
 def own_row(x):
@@ -327,8 +319,7 @@
         cells[a, 1, 104:192, :] = jnp.where(
             inside & (not_bottom | (rows_of(88, 96) < 128)), bottom, 0.0
         )
-    def fine(start):
-        size = 176
+    def fine(start, size):
         at = pl.ds(start, size)
         up_at, down_at = pl.ds(start - 1, size), pl.ds(start + 1, size)
         weights = [cells[WEIGHT, h, at, :] for h in range(2)]
@@ -358,7 +349,7 @@
             coef.append(scaled)
         for c in range(CHANNELS):
             part = [cells[c, h, at, :] for h in range(2)]
-            own_end = border[c]
+            own_end = border[c, start - PAD - 8 : start - PAD - 8 + size, :]
             left_end = pltpu.roll(part[1], 64, 1), pltpu.roll(part[1], 63, 1)
             first, last = lane_ids(size) == 0, lane_ids(size) == LANES - 1
             flux = jnp.where(first, coef[0][LEFT] * left_end[0], 0.0)
@@ -368,7 +359,7 @@
             flux = flux - jnp.where(last, coef[1][RIGHT] * left_end[1], 0.0)
             source[c, 1, at, :] = shares[1] * part[1] + flux
 
-    chunks(8, 184, 176, fine)
+    chunks(8, 184, STEP_F, fine)
     from_right, from_left = sides(88 * FIELDS, 16)
     beside_own = jnp.where(lane_ids(16) < 64, from_right, from_left)
     for first, upper in ((0, 71), (8, 135)):
@@ -400,8 +391,7 @@
 
     for level, fine_raw, raw, maps, rows in ((1, raw0, raw1, m1, 96), (2, raw1, raw2, m2, 48)):
 
-        def coarse(start, level=level, fine_raw=fine_raw, raw=raw, maps=maps, rows=rows):
-            size = rows
+        def coarse(start, size, level=level, fine_raw=fine_raw, raw=raw, maps=maps):
             at = pl.ds(start, size)
             for h in range(2):
                 parts = coarser(fine_raw, 2 ** (level - 1), 2 * start - PAD, size, h)
@@ -412,7 +402,7 @@
                 maps[SCALE, h, at, :] = scale
                 maps[INVERSE, h, at, :] = inverse
 
-        chunks(0, rows, rows, coarse)
+        chunks(0, rows, STEP_C, coarse)
     tiles = down_levels((f0, f1, f2), (source, g1, g2), (w0, w1, w2), (m0, m1, m2), FIRST_DOWN)
     upward, downward, leftward, rightward = coarser(raw2, 4, PAD + 16, 8, 0)
     row = lax.broadcasted_iota(jnp.int32, (8, LANES), 0)
@@ -469,9 +459,8 @@
 
 def whole_maps(level, raw, maps):
     halves, rows, first = WHOLE[level]
-    size = rows
-
-    def body(start):
+
+    def body(start, size):
         at = pl.ds(start, size)
         lane = lane_ids(size)
         for i in range(halves):
@@ -488,7 +477,7 @@
             maps[SCALE, first + i, at, :] = scale
             maps[INVERSE, first + i, at, :] = inverse
 
-    chunks(0, rows, size, body)
+    chunks(0, rows, STEP_W, body)
 
 
 def coarsen_whole(level, raw, next_raw):
@@ -658,7 +647,7 @@
 
 
 def add_rows(target, field, coarse, low, high, size):
-    def body(start):
+    def body(start, size):
         for c in range(CHANNELS):
             for h in range(2):
                 part = coarse[c, h, pl.ds(start, size), :]
@@ -666,7 +655,7 @@
                     at = pl.ds(2 * start - PAD + offset, size, stride=2)
                     target[c, h, at, :] = field[c, h, at, :] + part
 
-    chunks(low, high, size, body)
+    chunks(low, high, STEP_A, body)
 
 
 def up_levels(ranges, spans, before, fields, bases, works, maps, extra):
@@ -757,14 +746,14 @@
 def scale_base(base, maps):
     halves, rows, first = WHOLE[3]
 
-    def body(start):
-        at = pl.ds(start, rows)
+    def body(start, size):
+        at = pl.ds(start, size)
         for i in range(halves):
             inverse = maps[INVERSE, first + i, at, :]
             for c in range(CHANNELS):
                 base[c, first + i, at, :] = base[c, first + i, at, :] * inverse
 
-    chunks(0, rows, rows, body)
+    chunks(0, rows, STEP_W, body)
 
 
 def last_kernel(

time: 92.6 us -> 90.4 us (0.976)
  Pallas kernels: 18.4 us -> 16.2 us
    pallas_call x5, Pallas kernels: 17.2 us -> 15 us  [call(): pl.pallas_call(kernel, out_shape=[shape(*o) for o in outs], in_specs=in_s...]
where the time goes in v7:
time: 90.4 us; the launch traced here: 90.2 us
  blocking collectives  50 us (55%)
  Pallas kernels  16.2 us (18%)
  starting transfers between devices  12.7 us (14%)
  waiting for transfers between devices  10.6 us (12%)
    all_to_all x2, blocking collectives, gathered(): mine = lax.all_to_all(message.reshape(128, 1, -1), CHIPS, 0, 0, tiled=True)  50 us
    pallas_call x5, Pallas kernels, call(): pl.pallas_call(kernel, out_shape=[shape(*o) for o in outs], in_specs=in_s...  15 us
    ppermute x1, waiting for transfers between devices, local(): sided = lax.ppermute(side, SIDES, pairs)  4.34 us
    ppermute x1, starting transfers between devices, local(): below = lax.ppermute(up, 'z', ring(8, -1))  4.03 us
    ppermute x1, waiting for transfers between devices, local(): above = lax.ppermute(down, 'z', ring(8, 1))  3.47 us
    ppermute x1, starting transfers between devices, local(): sided = lax.ppermute(side, SIDES, pairs)  3.02 us
    ppermute x2, waiting for transfers between devices, gathered(): return (mine, lax.ppermute(mine, 'core', ring(2, 1)))  2.79 us
    ppermute x1, starting transfers between devices, local(): above = lax.ppermute(down, 'z', ring(8, 1))  2.54 us
  transfers between devices with their start and end apart: 6, of which 4 were waited for; matrix products, arithmetic and copies ran while one was open for 0% of the time, Pallas kernels for 0%

profile of v7, /device:TPU:1, one launch (start us, length us, event | category | flops | bytes accessed | tf_op | source)
XLA Modules:
  0.0 90.2 jit_solution(2556166660654677694)
XLA Ops:
  0.6 1.1 %shard_map.50 = (f32[288,128]{1,0:T(8,128)S(1)}, f32[288,128]{1,0:T(8,128)S(1)}) custom-call(f32[2,3,64,128]{3,2,1,0:T(8,128)} %guidance_in.1, s32[64,128]{1,0:T(8,128)} %weight_in.1, s32[64,128]{1,0:T(8,128)} %label_in.1), custom_call_target="tpu_custom_call" | custom-call | tf_op jit(solution)/shard_map/pallas_call | solution.py:836
  1.8 2.5 %collective-permute-start = (f32[288,128]{1,0:T(8,128)S(1)}, f32[288,128]{1,0:T(8,128)S(1)}, u32[]{:S(2)}, u32[]{:S(2)}) collective-permute-start(f32[288,128]{1,0:T(8,128)S(1)} %get-tuple-element.32.down), channel_id=1, source_target_pairs={{0,32},{32,64},{64,96},{96,128},{128,160},{160,192},{192,224},{224... | collective-permute-start | bytes 442376 | tf_op jit(solution)/shard_map/ppermute | solution.py:849
  4.3 4.0 %collective-permute-start.1 = (f32[288,128]{1,0:T(8,128)S(1)}, f32[288,128]{1,0:T(8,128)S(1)}, u32[]{:S(2)}, u32[]{:S(2)}) collective-permute-start(f32[288,128]{1,0:T(8,128)S(1)} %get-tuple-element.33.up), channel_id=1, source_target_pairs={{0,224},{32,0},{64,32},{96,64},{128,96},{160,128},{192,160},{224,1... | collective-permute-start | bytes 442376 | tf_op jit(solution)/shard_map/ppermute | solution.py:850
  8.4 3.5 %collective-permute-done.above = f32[288,128]{1,0:T(8,128)S(1)} collective-permute-done((f32[288,128]{1,0:T(8,128)S(1)}, f32[288,128]{1,0:T(8,128)S(1)}, u32[]{:S(2)}, u32[]{:S(2)}) %collective-permute-start) | collective-permute-done | bytes 147488 | tf_op jit(solution)/shard_map/ppermute | solution.py:849
  11.8 0.0 collective-permute-done.1.below
  11.8 0.5 shard_map.52
  12.3 1.3 %collective-permute-start.2 = (f32[456,128]{1,0:T(8,128)S(1)}, f32[456,128]{1,0:T(8,128)S(1)}, u32[]{:S(2)}, u32[]{:S(2)}) collective-permute-start(f32[456,128]{1,0:T(8,128)S(1)} %get-tuple-element.36), channel_id=1, source_target_pairs={{0,1},{1,0},{2,3},{3,2},{4,5},{5,4},{6,7},{7,6},{8,9},{9,8},{10,11... | collective-permute-start | bytes 700424 | tf_op jit(solution)/shard_map/ppermute | solution.py:858
  13.6 3.0 %collective-permute-start.3 = (f32[456,128]{1,0:T(8,128)S(1)}, f32[456,128]{1,0:T(8,128)S(1)}, u32[]{:S(2)}, u32[]{:S(2)}) collective-permute-start(f32[456,128]{1,0:T(8,128)S(1)} %get-tuple-element.37), channel_id=1, source_target_pairs={{0,0},{1,2},{2,1},{3,4},{4,3},{5,6},{6,5},{7,8},{8,7},{9,10},{10,9... | collective-permute-start | bytes 700424 | tf_op jit(solution)/shard_map/ppermute | solution.py:860
  16.6 0.0 collective-permute-done.2.swapped
  16.7 4.3 %collective-permute-done.3.sided = f32[456,128]{1,0:T(8,128)S(1)} collective-permute-done((f32[456,128]{1,0:T(8,128)S(1)}, f32[456,128]{1,0:T(8,128)S(1)}, u32[]{:S(2)}, u32[]{:S(2)}) %collective-permute-start.3) | collective-permute-done | bytes 233504 | tf_op jit(solution)/shard_map/ppermute | solution.py:860
  21.0 2.3 %shard_map.53 = (f32[5,2,208,128]{3,2,1,0:T(8,128)S(1)}, f32[6,2,112,128]{3,2,1,0:T(8,128)S(1)}, f32[6,2,64,128]{3,2,1,0:T(8,128)S(1)}, f32[3,2,208,128]{3,2,1,0...) custom-call(f32[5,64,128]{2,1,0:T(8,128)S(1)} %get-tuple-element.34., ...), custom_call_target="tpu_custom_call" | custom-call | bytes 8000000 | tf_op jit(solution)/shard_map/pallas_call | solution.py:814
  23.3 31.6 %all_to_all.10 = f32[128,1,768]{2,1,0:T(1,128)S(1)} all-to-all(f32[128,1,768]{2,1,0:T(1,128)S(1)} %bitcast.8), channel_id=1, replica_groups=mesh['z'=8,'y'=4,'x'=4,'core'=2] {'z','y','x'}, dimensions={0} | all-to-all | bytes 786432 | tf_op jit(solution)/shard_map/all_to_all | solution.py:830
  54.9 0.0 collective-permute-start.4
  54.9 1.7 %collective-permute-done.4.other = f32[768,128]{1,0:T(8,128)S(1)} collective-permute-done((f32[768,128]{1,0:T(8,128)S(1)}, f32[768,128]{1,0:T(8,128)S(1)}, u32[]{:S(2)}, u32[]{:S(2)}) %collective-permute-start.4) | collective-permute-done | bytes 393248 | tf_op jit(solution)/shard_map/ppermute | solution.py:832
  56.6 7.2 %shard_map.54 = (f32[6,6,80,128]{3,2,1,0:T(8,128)S(1)}, f32[6,2,48,128]{3,2,1,0:T(8,128)S(1)}, f32[6,1,32,128]{3,2,1,0:T(8,128)S(1)}, f32[6,1,24,128]{3,2,1,0:T(...) custom-call(f32[768,128]{1,0:T(8,128)S(1)} %bitcast.5, ...), custom_call_target="tpu_custom_call" | custom-call | bytes 8000000 | tf_op jit(solution)/shard_map/pallas_call | solution.py:814
  63.8 18.4 %all_to_all.11 = f32[128,1,384]{2,1,0:T(1,128)S(1)} all-to-all(f32[128,1,384]{2,1,0:T(1,128)S(1)} %bitcast.9), channel_id=1, replica_groups=mesh['z'=8,'y'=4,'x'=4,'core'=2] {'z','y','x'}, dimensions={0} | all-to-all | bytes 393216 | tf_op jit(solution)/shard_map/all_to_all | solution.py:830
  82.2 1.8 %collective-permute-start.5 = (f32[384,128]{1,0:T(8,128)S(1)}, f32[384,128]{1,0:T(8,128)S(1)}, u32[]{:S(2)}, u32[]{:S(2)}) collective-permute-start(f32[384,128]{1,0:T(8,128)S(1)} %bitcast.6), channel_id=1, source_target_pairs={{0,1},{1,0},{2,3},{3,2},{4,5},{5,4},{6,7},{7,6},{8,9},{9,8},{10,11... | collective-permute-start | bytes 589832 | tf_op jit(solution)/shard_map/ppermute | solution.py:832
  84.0 1.1 %collective-permute-done.5.other = f32[384,128]{1,0:T(8,128)S(1)} collective-permute-done((f32[384,128]{1,0:T(8,128)S(1)}, f32[384,128]{1,0:T(8,128)S(1)}, u32[]{:S(2)}, u32[]{:S(2)}) %collective-permute-start.5) | collective-permute-done | bytes 196640 | tf_op jit(solution)/shard_map/ppermute | solution.py:832
  85.1 5.1 %shard_map.55 = (f32[3,64,128]{2,1,0:T(8,128)}, f32[3,64,128]{2,1,0:T(8,128)}) custom-call(f32[384,128]{1,0:T(8,128)S(1)} %bitcast.7, f32[384,128]{1,0:T(8,128)S(1)} %collective-permute-done.5.other, f32[5,2,208,128]{3,2,1,0:T(8,128)S(1)} %get-tuple-element.40.m0, f32[6,2,112,128]{3,2,1,0:T(8,128)S(1)} %get-tuple-element.41.m1, ...), custom_call_target="tpu_custom_call" | custom-call | bytes 8000000 | tf_op jit(solution)/shard_map/pallas_call | solution.py:814
  (1 shorter events, 0.0 us)
Async XLA Ops:
  1.8 10.1 %collective-permute-start = (f32[288,128]{1,0:T(8,128)S(1)}, f32[288,128]{1,0:T(8,128)S(1)}, u32[]{:S(2)}, u32[]{:S(2)}) collective-permute-start(f32[288,128]{1,0:T(8,128)S(1)} %get-tuple-element.32.down), channel_id=1, source_target_pairs={{0,32},{32,64},{64,96},{96,128},{128,160},{160,192},{192,224},{224... | collective-permute-start | bytes 442376 | tf_op jit(solution)/shard_map/ppermute | solution.py:849
  4.3 7.5 %collective-permute-start.1 = (f32[288,128]{1,0:T(8,128)S(1)}, f32[288,128]{1,0:T(8,128)S(1)}, u32[]{:S(2)}, u32[]{:S(2)}) collective-permute-start(f32[288,128]{1,0:T(8,128)S(1)} %get-tuple-element.33.up), channel_id=1, source_target_pairs={{0,224},{32,0},{64,32},{96,64},{128,96},{160,128},{192,160},{224,1... | collective-permute-start | bytes 442376 | tf_op jit(solution)/shard_map/ppermute | solution.py:850
  12.3 4.3 %collective-permute-start.2 = (f32[456,128]{1,0:T(8,128)S(1)}, f32[456,128]{1,0:T(8,128)S(1)}, u32[]{:S(2)}, u32[]{:S(2)}) collective-permute-start(f32[456,128]{1,0:T(8,128)S(1)} %get-tuple-element.36), channel_id=1, source_target_pairs={{0,1},{1,0},{2,3},{3,2},{4,5},{5,4},{6,7},{7,6},{8,9},{9,8},{10,11... | collective-permute-start | bytes 700424 | tf_op jit(solution)/shard_map/ppermute | solution.py:858
  13.6 7.4 %collective-permute-start.3 = (f32[456,128]{1,0:T(8,128)S(1)}, f32[456,128]{1,0:T(8,128)S(1)}, u32[]{:S(2)}, u32[]{:S(2)}) collective-permute-start(f32[456,128]{1,0:T(8,128)S(1)} %get-tuple-element.37), channel_id=1, source_target_pairs={{0,0},{1,2},{2,1},{3,4},{4,3},{5,6},{6,5},{7,8},{8,7},{9,10},{10,9... | collective-permute-start | bytes 700424 | tf_op jit(solution)/shard_map/ppermute | solution.py:860
  54.9 1.7 %collective-permute-start.4 = (f32[768,128]{1,0:T(8,128)S(1)}, f32[768,128]{1,0:T(8,128)S(1)}, u32[]{:S(2)}, u32[]{:S(2)}) collective-permute-start(f32[768,128]{1,0:T(8,128)S(1)} %bitcast.4), channel_id=1, source_target_pairs={{0,1},{1,0},{2,3},{3,2},{4,5},{5,4},{6,7},{7,6},{8,9},{9,8},{10,11... | collective-permute-start | bytes 1179656 | tf_op jit(solution)/shard_map/ppermute | solution.py:832
  82.2 2.9 %collective-permute-start.5 = (f32[384,128]{1,0:T(8,128)S(1)}, f32[384,128]{1,0:T(8,128)S(1)}, u32[]{:S(2)}, u32[]{:S(2)}) collective-permute-start(f32[384,128]{1,0:T(8,128)S(1)} %bitcast.6), channel_id=1, source_target_pairs={{0,1},{1,0},{2,3},{3,2},{4,5},{5,4},{6,7},{7,6},{8,9},{9,8},{10,11... | collective-permute-start | bytes 589832 | tf_op jit(solution)/shard_map/ppermute | solution.py:832

commit v8 on v7

--- a/solution.py
+++ b/solution.py
@@ -14,7 +14,7 @@
 LANES = 128
 REACH = 56
 SIDES = ("y", "x", "core")
-CHIPS = ("z", "y", "x")
+CHIPS = ("y", "x", "z")
 LOCAL_ROWS = (192, 96, 48)
 STEP, STEP_R, STEP_F, STEP_C, STEP_A, STEP_W = 8, 16, 16, 16, 8, 16
 UP, DOWN, LEFT, RIGHT, SCALE, INVERSE = range(6)
@@ -415,10 +415,11 @@
 def unpack(place, mine, other, count, stride, ordered, put):
     core = place[2]
     for f in range(count):
-        own = mine[pl.ds(f, 128, stride=stride), :]
-        theirs = other[pl.ds(f, 128, stride=stride), :]
-        ordered[f, pl.ds(0, 128, stride=2), :] = jnp.where(core == 0, own, theirs)
-        ordered[f, pl.ds(1, 128, stride=2), :] = jnp.where(core == 0, theirs, own)
+        for z in range(8):
+            at = pl.ds(f + stride * z, 16, stride=8 * stride)
+            own, theirs = mine[at, :], other[at, :]
+            ordered[f, pl.ds(32 * z, 16, stride=2), :] = jnp.where(core == 0, own, theirs)
+            ordered[f, pl.ds(32 * z + 1, 16, stride=2), :] = jnp.where(core == 0, theirs, own)
     sub = lax.broadcasted_iota(jnp.int32, (8, LANES), 0)
     part, cell = lane_ids(8) >> 4, lane_ids(8) & 15
     first = (((sub - part) & 7) << 4) + cell
@@ -467,11 +468,12 @@
             scaled, scale, inverse = scaled_maps(
                 [raw[m, first + i, at, :] for m in range(4)], 0.5**level
             )
+            breadth = 64 if level == 6 else LANES
             if i == 0:
-                scaled[LEFT] = jnp.where(lane == 0, 0.0, scaled[LEFT])
+                scaled[LEFT] = jnp.where((lane & (breadth - 1)) == 0, 0.0, scaled[LEFT])
             if i == halves - 1:
-                last = 63 if level == 6 else LANES - 1
-                scaled[RIGHT] = jnp.where(lane == last, 0.0, scaled[RIGHT])
+                at_last = (lane & (breadth - 1)) == breadth - 1
+                scaled[RIGHT] = jnp.where(at_last, 0.0, scaled[RIGHT])
             for m in range(4):
                 maps[m, first + i, at, :] = scaled[m]
             maps[SCALE, first + i, at, :] = scale
@@ -489,6 +491,8 @@
             even, odd = even_odd(raw, (m, first + h), PAD, next_rows)
             parts.append(even if m == UP else odd if m == DOWN else even + odd)
         kind = "sum" if m in (UP, DOWN) else "low" if m == LEFT else "high"
+        if level == 5:
+            parts = parts * 2
         for h, x in enumerate(folded(parts, kind)):
             next_raw[m, next_first + h, PAD : PAD + next_rows, :] = 0.5 * x
 
@@ -531,7 +535,7 @@
 
 def coarse_solve(base, maps, product):
     sweep = one_sweep(maps)
-    right_side = [base[c, 0, PAD : PAD + 8, :] for c in range(CHANNELS)]
+    right_side = [base[i, 0, PAD : PAD + 8, :] for i in range(2)]
     first = right_side
     for _ in range(3):
         first = [
@@ -541,19 +545,19 @@
     values = first
     for _ in range(COARSE_SWEEPS // 4 - 1):
         lanes = [[moved(v, 0, b) for b in range(-4, 5)] for v in values]
-        totals = [list() for _ in range(CHANNELS)]
+        totals = [list() for _ in values]
         for a in range(-4, 5):
-            sums = [None] * CHANNELS
+            sums = [None] * len(values)
             for i, at in enumerate(DIAMOND):
                 if at[0] == a:
                     coef = product[i]
-                    for c in range(CHANNELS):
+                    for c in range(len(values)):
                         term = coef * lanes[c][at[1] + 4]
                         sums[c] = term if sums[c] is None else sums[c] + term
-            for c in range(CHANNELS):
+            for c in range(len(values)):
                 totals[c].append(moved(sums[c], a, 0))
         values = []
-        for c in range(CHANNELS):
+        for c in range(len(first)):
             t = totals[c]
             even = (t[0] + t[1]) + (t[2] + t[3])
             odd = (t[5] + t[6]) + (t[7] + t[8])
@@ -575,14 +579,20 @@
             even, odd = even_odd(other, (c, first + h), PAD, next_rows)
             parts.append(even + odd)
         summed.append(jnp.concatenate(parts, axis=0))
-    for h, x in enumerate(folded(summed, "sum")):
+    if level == 5:
+        parts = [summed[0][c * next_rows : (c + 1) * next_rows] for c in range(CHANNELS)]
+        inverse = 0.25 * maps[6][INVERSE, 0, PAD : PAD + next_rows, :]
+        for i, group in enumerate((parts[:2], parts[2:])):
+            bases[6][i, 0, PAD : PAD + next_rows, :] = folded(group, "sum")[0] * inverse
+        summed = []
+    for h, x in enumerate(folded(summed, "sum") if summed else []):
         inverse = 0.25 * maps[level + 1][INVERSE, next_first + h, PAD : PAD + next_rows, :]
         for c in range(CHANNELS):
             part = x[c * next_rows : (c + 1) * next_rows]
             bases[level + 1][c, next_first + h, PAD : PAD + next_rows, :] = part * inverse
     if level == 5:
-        coarse = coarse_solve(bases[6], maps[6], product)
-        coarse = [jnp.concatenate(coarse, axis=0)]
+        both, third = coarse_solve(bases[6], maps[6], product)
+        coarse = [None]
     else:
         whole_cycle(level + 1, bases, fields, others, maps, product)
         coarse = [
@@ -596,7 +606,10 @@
             for h in range(next_halves)
         ]
     for m, x in enumerate(coarse):
-        wide = doubled(x)
+        if x is None:
+            wide = [jnp.concatenate(doubled(both) + doubled(third)[:1], axis=0)]
+        else:
+            wide = doubled(x)
         for i in range(min(halves, 2)):
             h = first + 2 * m + i
             for c in range(CHANNELS):
@@ -624,8 +637,9 @@
 def correct_level_two(
     place, bases, fields, maps, f2, target, near_maps, near_base, near_a, near_b
 ):
-    for m in range(4):
-        near_maps[m, 0, PAD : PAD + 24, :] = window(maps[3], m, place)
+    if maps is not None:
+        for m in range(4):
+            near_maps[m, 0, PAD : PAD + 24, :] = window(maps[3], m, place)
     edge = jnp.zeros((PAD, LANES), F32)
     for c in range(CHANNELS):
         near_base[c, 0, PAD : PAD + 24, :] = window(bases[3], c, place)
@@ -695,9 +709,9 @@
 
 def middle_kernel(
     mine, other, m0, m1, m2, source, f0, g1, f1, g2, f2,
-    m3, m4, m5, m6, product, solution, n0, h0, k1, h1, k2, h2, message,
+    m3, m4, m5, m6, product, near_maps, solution, n0, h0, k1, h1, k2, h2, message,
     ordered, raw3, raw4, raw5, raw6, b3, v3, o3, b4, v4, o4, b5, v5, o5, b6,
-    w0, w1, w2, near_maps, near_base, near_a, near_b,
+    w0, w1, w2, near_base, near_a, near_b,
 ):
     place = whereabouts()
     for ref in (m3, b3, v3):
@@ -757,10 +771,10 @@
 
 
 def last_kernel(
-    mine, other, m0, m1, m2, source, m3, m4, m5, m6, product, before, n0, f0, k1, f1, k2, f2,
+    mine, other, m0, m1, m2, source, m3, m4, m5, m6, product, near_maps, before, n0, f0, k1, f1, k2, f2,
     solution, residual,
     ordered, b3, v3, o3, b4, v4, o4, b5, v5, o5, b6,
-    h0, h1, h2, w0, w1, w2, near_maps, near_base, near_a, near_b,
+    h0, h1, h2, w0, w1, w2, near_base, near_a, near_b, left,
 ):
     place = whereabouts()
     for ref in (b3, v3):
@@ -784,16 +798,22 @@
         product,
     )
     correct_level_two(
-        place, {3: b3}, {3: v3}, maps, f2, h2, near_maps, near_base, near_a, near_b
+        place, {3: b3}, {3: v3}, None, f2, h2, near_maps, near_base, near_a, near_b
     )
     local_maps = (m0, m1, m2)
     up_levels(
         LATER_UP, LATER_SPANS, (f0, f1), (h0, h1, h2), (n0, k1, k2), (w0, w1, w2), local_maps, before,
     )
+    own = pl.ds(PAD + 64, 64)
+    copies = [
+        pltpu.make_async_copy(field.at[:, 0, own, :], target, left.at[i])
+        for i, (field, target) in enumerate(((h0, solution), (w0, residual)))
+    ]
+    copies[0].start()
     stencil("final", w0, h0, source, m0, 64, 128, 64, 1)
-    for c in range(CHANNELS):
-        solution[c] = h0[c, 0, PAD + 64 : PAD + 128, :]
-        residual[c] = w0[c, 0, PAD + 64 : PAD + 128, :]
+    copies[1].start()
+    for copy in copies:
+        copy.wait()
 
 
 def shape(*dims):
@@ -809,14 +829,14 @@
     return (count, halves + 2 * first, rows + 2 * PAD, LANES)
 
 
-def call(kernel, outs, scratch, *args):
+def call(kernel, outs, scratch, *args, out_space=pltpu.VMEM, semaphores=()):
     in_specs = [pl.BlockSpec(memory_space=pltpu.VMEM) for _ in args]
     return pl.pallas_call(
         kernel,
         out_shape=[shape(*o) for o in outs],
         in_specs=in_specs,
-        out_specs=[pl.BlockSpec(memory_space=pltpu.VMEM) for _ in outs],
-        scratch_shapes=[pltpu.VMEM(s, F32) for s in scratch],
+        out_specs=[pl.BlockSpec(memory_space=out_space) for _ in outs],
+        scratch_shapes=[pltpu.VMEM(s, F32) for s in scratch] + list(semaphores),
         compiler_params=pltpu.CompilerParams(vmem_limit_bytes=14 * 1024 * 1024),
         cost_estimate=pl.CostEstimate(flops=0, bytes_accessed=8_000_000, transcendentals=0),
     )(*args)
@@ -870,11 +890,11 @@
     mine, other = gathered(message)
     wholes = [whole_shape(level, CHANNELS) for level in (3, 4, 5) for _ in range(3)]
     wholes = wholes + [whole_shape(6, CHANNELS)]
-    near = [(4, 1, 40, LANES)] + [(CHANNELS, 1, 40, LANES)] * 3
-    m3, m4, m5, m6, product, solution, n0, h0, k1, h1, k2, h2, message = call(
+    near = [(CHANNELS, 1, 40, LANES)] * 3
+    m3, m4, m5, m6, product, near_maps, solution, n0, h0, k1, h1, k2, h2, message = call(
         middle_kernel,
         [whole_shape(level, 6) for level in (3, 4, 5, 6)]
-        + [(len(DIAMOND), 8, LANES)] + [fields[0]] * 3 + [fields[1]] * 2 + [fields[2]] * 2 + [(CHANNELS * 128, LANES)],
+        + [(len(DIAMOND), 8, LANES), (4, 1, 40, LANES)] + [fields[0]] * 3 + [fields[1]] * 2 + [fields[2]] * 2 + [(CHANNELS * 128, LANES)],
         [(6, 256, LANES)] + [whole_shape(level, 4) for level in (3, 4, 5, 6)]
         + wholes + fields + near,
         mine, other, m0, m1, m2, source, f0, g1, f1, g2, f2,
@@ -884,8 +904,9 @@
         last_kernel,
         [(CHANNELS, 64, LANES)] * 2,
         [(CHANNELS, 256, LANES)] + wholes + fields + fields + near,
-        mine, other, m0, m1, m2, source, m3, m4, m5, m6, product,
+        mine, other, m0, m1, m2, source, m3, m4, m5, m6, product, near_maps,
         solution, n0, h0, k1, h1, k2, h2,
+        out_space=pltpu.HBM, semaphores=[pltpu.SemaphoreType.DMA((2,))],
     )
     return tuple(outs)
 

time: 90.4 us -> 90.6 us (level)
  no operation moved by 1% of the time
where the time goes in v8:
time: 90.6 us; the launch traced here: 90.4 us
  blocking collectives  50.3 us (56%)
  Pallas kernels  16.3 us (18%)
  starting transfers between devices  12.3 us (14%)
  waiting for transfers between devices  10.6 us (12%)
    all_to_all x2, blocking collectives, gathered(): mine = lax.all_to_all(message.reshape(128, 1, -1), CHIPS, 0, 0, tiled=True)  50.3 us
    pallas_call x5, Pallas kernels, call(): pl.pallas_call(kernel, out_shape=[shape(*o) for o in outs], in_specs=in_s...  15.1 us
    ppermute x1, waiting for transfers between devices, local(): sided = lax.ppermute(side, SIDES, pairs)  4.34 us
    ppermute x1, starting transfers between devices, local(): below = lax.ppermute(up, 'z', ring(8, -1))  4.03 us
    ppermute x1, waiting for transfers between devices, local(): above = lax.ppermute(down, 'z', ring(8, 1))  3.47 us
    ppermute x1, starting transfers between devices, local(): sided = lax.ppermute(side, SIDES, pairs)  3.02 us
    ppermute x2, waiting for transfers between devices, gathered(): return (mine, lax.ppermute(mine, 'core', ring(2, 1)))  2.79 us
    ppermute x1, starting transfers between devices, local(): above = lax.ppermute(down, 'z', ring(8, 1))  2.54 us
  transfers between devices with their start and end apart: 6, of which 4 were waited for; matrix products, arithmetic and copies ran while one was open for 0% of the time, Pallas kernels for 0%

profile of v8, /device:TPU:1, one launch (start us, length us, event | category | flops | bytes accessed | tf_op | source)
XLA Modules:
  0.0 90.4 jit_solution(2070473980156295214)
XLA Ops:
  0.6 1.1 %shard_map.50 = (f32[288,128]{1,0:T(8,128)S(1)}, f32[288,128]{1,0:T(8,128)S(1)}) custom-call(f32[2,3,64,128]{3,2,1,0:T(8,128)} %guidance_in.1, s32[64,128]{1,0:T(8,128)} %weight_in.1, s32[64,128]{1,0:T(8,128)} %label_in.1), custom_call_target="tpu_custom_call" | custom-call | tf_op jit(solution)/shard_map/pallas_call | solution.py:856
  1.8 2.5 %collective-permute-start = (f32[288,128]{1,0:T(8,128)S(1)}, f32[288,128]{1,0:T(8,128)S(1)}, u32[]{:S(2)}, u32[]{:S(2)}) collective-permute-start(f32[288,128]{1,0:T(8,128)S(1)} %get-tuple-element.33.down), channel_id=1, source_target_pairs={{0,32},{32,64},{64,96},{96,128},{128,160},{160,192},{192,224},{224... | collective-permute-start | bytes 442376 | tf_op jit(solution)/shard_map/ppermute | solution.py:869
  4.3 4.0 %collective-permute-start.1 = (f32[288,128]{1,0:T(8,128)S(1)}, f32[288,128]{1,0:T(8,128)S(1)}, u32[]{:S(2)}, u32[]{:S(2)}) collective-permute-start(f32[288,128]{1,0:T(8,128)S(1)} %get-tuple-element.34.up), channel_id=1, source_target_pairs={{0,224},{32,0},{64,32},{96,64},{128,96},{160,128},{192,160},{224,1... | collective-permute-start | bytes 442376 | tf_op jit(solution)/shard_map/ppermute | solution.py:870
  8.4 3.5 %collective-permute-done.above = f32[288,128]{1,0:T(8,128)S(1)} collective-permute-done((f32[288,128]{1,0:T(8,128)S(1)}, f32[288,128]{1,0:T(8,128)S(1)}, u32[]{:S(2)}, u32[]{:S(2)}) %collective-permute-start) | collective-permute-done | bytes 147488 | tf_op jit(solution)/shard_map/ppermute | solution.py:869
  11.8 0.0 collective-permute-done.1.below
  11.8 0.5 shard_map.52
  12.3 1.3 %collective-permute-start.2 = (f32[456,128]{1,0:T(8,128)S(1)}, f32[456,128]{1,0:T(8,128)S(1)}, u32[]{:S(2)}, u32[]{:S(2)}) collective-permute-start(f32[456,128]{1,0:T(8,128)S(1)} %get-tuple-element.37), channel_id=1, source_target_pairs={{0,1},{1,0},{2,3},{3,2},{4,5},{5,4},{6,7},{7,6},{8,9},{9,8},{10,11... | collective-permute-start | bytes 700424 | tf_op jit(solution)/shard_map/ppermute | solution.py:878
  13.6 3.0 %collective-permute-start.3 = (f32[456,128]{1,0:T(8,128)S(1)}, f32[456,128]{1,0:T(8,128)S(1)}, u32[]{:S(2)}, u32[]{:S(2)}) collective-permute-start(f32[456,128]{1,0:T(8,128)S(1)} %get-tuple-element.38), channel_id=1, source_target_pairs={{0,0},{1,2},{2,1},{3,4},{4,3},{5,6},{6,5},{7,8},{8,7},{9,10},{10,9... | collective-permute-start | bytes 700424 | tf_op jit(solution)/shard_map/ppermute | solution.py:880
  16.6 0.0 collective-permute-done.2.swapped
  16.7 4.3 %collective-permute-done.3.sided = f32[456,128]{1,0:T(8,128)S(1)} collective-permute-done((f32[456,128]{1,0:T(8,128)S(1)}, f32[456,128]{1,0:T(8,128)S(1)}, u32[]{:S(2)}, u32[]{:S(2)}) %collective-permute-start.3) | collective-permute-done | bytes 233504 | tf_op jit(solution)/shard_map/ppermute | solution.py:880
  21.0 2.3 %shard_map.53 = (f32[5,2,208,128]{3,2,1,0:T(8,128)S(1)}, f32[6,2,112,128]{3,2,1,0:T(8,128)S(1)}, f32[6,2,64,128]{3,2,1,0:T(8,128)S(1)}, f32[3,2,208,128]{3,2,1,0...) custom-call(f32[5,64,128]{2,1,0:T(8,128)S(1)} %get-tuple-element.35., ...), custom_call_target="tpu_custom_call" | custom-call | bytes 8000000 | tf_op jit(solution)/shard_map/pallas_call | solution.py:834
  23.3 31.6 %all_to_all.10 = f32[128,1,768]{2,1,0:T(1,128)S(1)} all-to-all(f32[128,1,768]{2,1,0:T(1,128)S(1)} %bitcast.8), channel_id=1, replica_groups=mesh['z'=8,'y'=4,'x'=4,'core'=2] {'y','x','z'}, dimensions={0} | all-to-all | bytes 786432 | tf_op jit(solution)/shard_map/all_to_all | solution.py:850
  54.9 0.0 collective-permute-start.4
  54.9 1.7 %collective-permute-done.4.other = f32[768,128]{1,0:T(8,128)S(1)} collective-permute-done((f32[768,128]{1,0:T(8,128)S(1)}, f32[768,128]{1,0:T(8,128)S(1)}, u32[]{:S(2)}, u32[]{:S(2)}) %collective-permute-start.4) | collective-permute-done | bytes 393248 | tf_op jit(solution)/shard_map/ppermute | solution.py:852
  56.6 7.2 %shard_map.54 = (f32[6,6,80,128]{3,2,1,0:T(8,128)S(1)}, f32[6,2,48,128]{3,2,1,0:T(8,128)S(1)}, f32[6,1,32,128]{3,2,1,0:T(8,128)S(1)}, f32[6,1,24,128]{3,2,1,0:T(...) custom-call(f32[768,128]{1,0:T(8,128)S(1)} %bitcast.5, ...), custom_call_target="tpu_custom_call" | custom-call | bytes 8000000 | tf_op jit(solution)/shard_map/pallas_call | solution.py:834
  63.8 18.8 %all_to_all.11 = f32[128,1,384]{2,1,0:T(1,128)S(1)} all-to-all(f32[128,1,384]{2,1,0:T(1,128)S(1)} %bitcast.9), channel_id=1, replica_groups=mesh['z'=8,'y'=4,'x'=4,'core'=2] {'y','x','z'}, dimensions={0} | all-to-all | bytes 393216 | tf_op jit(solution)/shard_map/all_to_all | solution.py:850
  82.5 1.4 %collective-permute-start.5 = (f32[384,128]{1,0:T(8,128)S(1)}, f32[384,128]{1,0:T(8,128)S(1)}, u32[]{:S(2)}, u32[]{:S(2)}) collective-permute-start(f32[384,128]{1,0:T(8,128)S(1)} %bitcast.6), channel_id=1, source_target_pairs={{0,1},{1,0},{2,3},{3,2},{4,5},{5,4},{6,7},{7,6},{8,9},{9,8},{10,11... | collective-permute-start | bytes 589832 | tf_op jit(solution)/shard_map/ppermute | solution.py:852
  83.9 1.1 %collective-permute-done.5.other = f32[384,128]{1,0:T(8,128)S(1)} collective-permute-done((f32[384,128]{1,0:T(8,128)S(1)}, f32[384,128]{1,0:T(8,128)S(1)}, u32[]{:S(2)}, u32[]{:S(2)}) %collective-permute-start.5) | collective-permute-done | bytes 196640 | tf_op jit(solution)/shard_map/ppermute | solution.py:852
  85.0 5.2 %shard_map.55 = (f32[3,64,128]{2,1,0:T(8,128)}, f32[3,64,128]{2,1,0:T(8,128)}) custom-call(f32[384,128]{1,0:T(8,128)S(1)} %bitcast.7, f32[384,128]{1,0:T(8,128)S(1)} %collective-permute-done.5.other, f32[5,2,208,128]{3,2,1,0:T(8,128)S(1)} %get-tuple-element.41.m0, f32[6,2,112,128]{3,2,1,0:T(8,128)S(1)} %get-tuple-element.42.m1, ...), custom_call_target="tpu_custom_call" | custom-call | bytes 8000000 | tf_op jit(solution)/shard_map/pallas_call | solution.py:834
  (1 shorter events, 0.0 us)
Async XLA Ops:
  1.8 10.1 %collective-permute-start = (f32[288,128]{1,0:T(8,128)S(1)}, f32[288,128]{1,0:T(8,128)S(1)}, u32[]{:S(2)}, u32[]{:S(2)}) collective-permute-start(f32[288,128]{1,0:T(8,128)S(1)} %get-tuple-element.33.down), channel_id=1, source_target_pairs={{0,32},{32,64},{64,96},{96,128},{128,160},{160,192},{192,224},{224... | collective-permute-start | bytes 442376 | tf_op jit(solution)/shard_map/ppermute | solution.py:869
  4.3 7.5 %collective-permute-start.1 = (f32[288,128]{1,0:T(8,128)S(1)}, f32[288,128]{1,0:T(8,128)S(1)}, u32[]{:S(2)}, u32[]{:S(2)}) collective-permute-start(f32[288,128]{1,0:T(8,128)S(1)} %get-tuple-element.34.up), channel_id=1, source_target_pairs={{0,224},{32,0},{64,32},{96,64},{128,96},{160,128},{192,160},{224,1... | collective-permute-start | bytes 442376 | tf_op jit(solution)/shard_map/ppermute | solution.py:870
  12.3 4.3 %collective-permute-start.2 = (f32[456,128]{1,0:T(8,128)S(1)}, f32[456,128]{1,0:T(8,128)S(1)}, u32[]{:S(2)}, u32[]{:S(2)}) collective-permute-start(f32[456,128]{1,0:T(8,128)S(1)} %get-tuple-element.37), channel_id=1, source_target_pairs={{0,1},{1,0},{2,3},{3,2},{4,5},{5,4},{6,7},{7,6},{8,9},{9,8},{10,11... | collective-permute-start | bytes 700424 | tf_op jit(solution)/shard_map/ppermute | solution.py:878
  13.6 7.4 %collective-permute-start.3 = (f32[456,128]{1,0:T(8,128)S(1)}, f32[456,128]{1,0:T(8,128)S(1)}, u32[]{:S(2)}, u32[]{:S(2)}) collective-permute-start(f32[456,128]{1,0:T(8,128)S(1)} %get-tuple-element.38), channel_id=1, source_target_pairs={{0,0},{1,2},{2,1},{3,4},{4,3},{5,6},{6,5},{7,8},{8,7},{9,10},{10,9... | collective-permute-start | bytes 700424 | tf_op jit(solution)/shard_map/ppermute | solution.py:880
  54.9 1.7 %collective-permute-start.4 = (f32[768,128]{1,0:T(8,128)S(1)}, f32[768,128]{1,0:T(8,128)S(1)}, u32[]{:S(2)}, u32[]{:S(2)}) collective-permute-start(f32[768,128]{1,0:T(8,128)S(1)} %bitcast.4), channel_id=1, source_target_pairs={{0,1},{1,0},{2,3},{3,2},{4,5},{5,4},{6,7},{7,6},{8,9},{9,8},{10,11... | collective-permute-start | bytes 1179656 | tf_op jit(solution)/shard_map/ppermute | solution.py:852
  82.5 2.5 %collective-permute-start.5 = (f32[384,128]{1,0:T(8,128)S(1)}, f32[384,128]{1,0:T(8,128)S(1)}, u32[]{:S(2)}, u32[]{:S(2)}) collective-permute-start(f32[384,128]{1,0:T(8,128)S(1)} %bitcast.6), channel_id=1, source_target_pairs={{0,1},{1,0},{2,3},{3,2},{4,5},{5,4},{6,7},{7,6},{8,9},{9,8},{10,11... | collective-permute-start | bytes 589832 | tf_op jit(solution)/shard_map/ppermute | solution.py:852

commit v9 on v8

--- a/solution.py
+++ b/solution.py
@@ -72,7 +72,7 @@
             above = [field[c, h, pl.ds(start - 1, size), :] for h in span]
             below = [field[c, h, pl.ds(start + 1, size), :] for h in span]
             left, right = beside(here, width)
-            for i, h in enumerate(span):
+            for i, h in enumerate(span[:1] if mode == "final" else span):
                 near = (above[i], below[i], left[i], right[i])
                 if mode in ("difference", "scaled_difference", "final"):
                     near = [n - here[i] for n in near]
@@ -266,17 +266,17 @@
 
 FIRST_DOWN = (
     ((8, 184, 176), (8, 184, 176), (0, 96, 96)),
-    ((0, 96, 96), (0, 96, 96), (0, 48, 48)),
-    ((0, 48, 48), (0, 48, 48), None),
+    ((0, 96, 96), (8, 88, 80), (0, 48, 48)),
+    ((0, 48, 48), (16, 32, 16), None),
 )
 LATER_DOWN = (
-    ((32, 160, 128), (32, 160, 128), (16, 80, 64)),
+    ((32, 160, 128), (40, 152, 112), (16, 80, 64)),
     ((16, 80, 64), (16, 80, 64), (8, 40, 32)),
-    ((8, 40, 32), (8, 40, 32), None),
+    ((8, 40, 32), (16, 32, 16), None),
 )
-FIRST_UP = ((32, 160, 128), (8, 88, 80), (0, 48, 48))
+FIRST_UP = ((32, 160, 128), (16, 80, 64), (0, 48, 48))
 LATER_UP = ((56, 136, 80), (24, 72, 48), (8, 40, 32))
-FIRST_SPANS = ((8, 88, 80), (0, 48, 48))
+FIRST_SPANS = ((16, 80, 64), (0, 48, 48))
 LATER_SPANS = ((24, 72, 48), (8, 40, 32))
 
 

time: 90.6 us -> 90.6 us (level)
  no operation moved by 1% of the time
where the time goes in v9:
time: 90.6 us; the launch traced here: 90.4 us
  blocking collectives  50.5 us (56%)
  Pallas kernels  16.2 us (18%)
  starting transfers between devices  12.3 us (14%)
  waiting for transfers between devices  10.6 us (12%)
    all_to_all x2, blocking collectives, gathered(): mine = lax.all_to_all(message.reshape(128, 1, -1), CHIPS, 0, 0, tiled=True)  50.5 us
    pallas_call x5, Pallas kernels, call(): pl.pallas_call(kernel, out_shape=[shape(*o) for o in outs], in_specs=in_s...  15 us
    ppermute x1, waiting for transfers between devices, local(): sided = lax.ppermute(side, SIDES, pairs)  4.34 us
    ppermute x1, starting transfers between devices, local(): below = lax.ppermute(up, 'z', ring(8, -1))  4.03 us
    ppermute x1, waiting for transfers between devices, local(): above = lax.ppermute(down, 'z', ring(8, 1))  3.47 us
    ppermute x1, starting transfers between devices, local(): sided = lax.ppermute(side, SIDES, pairs)  3.02 us
    ppermute x2, waiting for transfers between devices, gathered(): return (mine, lax.ppermute(mine, 'core', ring(2, 1)))  2.79 us
    ppermute x1, starting transfers between devices, local(): above = lax.ppermute(down, 'z', ring(8, 1))  2.54 us
  transfers between devices with their start and end apart: 6, of which 4 were waited for; matrix products, arithmetic and copies ran while one was open for 0% of the time, Pallas kernels for 0%

profile of v9, /device:TPU:1, one launch (start us, length us, event | category | flops | bytes accessed | tf_op | source)
XLA Modules:
  0.0 90.4 jit_solution(3413308831651944591)
XLA Ops:
  0.6 1.1 %shard_map.50 = (f32[288,128]{1,0:T(8,128)S(1)}, f32[288,128]{1,0:T(8,128)S(1)}) custom-call(f32[2,3,64,128]{3,2,1,0:T(8,128)} %guidance_in.1, s32[64,128]{1,0:T(8,128)} %weight_in.1, s32[64,128]{1,0:T(8,128)} %label_in.1), custom_call_target="tpu_custom_call" | custom-call | tf_op jit(solution)/shard_map/pallas_call | solution.py:856
  1.8 2.5 %collective-permute-start = (f32[288,128]{1,0:T(8,128)S(1)}, f32[288,128]{1,0:T(8,128)S(1)}, u32[]{:S(2)}, u32[]{:S(2)}) collective-permute-start(f32[288,128]{1,0:T(8,128)S(1)} %get-tuple-element.33.down), channel_id=1, source_target_pairs={{0,32},{32,64},{64,96},{96,128},{128,160},{160,192},{192,224},{224... | collective-permute-start | bytes 442376 | tf_op jit(solution)/shard_map/ppermute | solution.py:869
  4.3 4.0 %collective-permute-start.1 = (f32[288,128]{1,0:T(8,128)S(1)}, f32[288,128]{1,0:T(8,128)S(1)}, u32[]{:S(2)}, u32[]{:S(2)}) collective-permute-start(f32[288,128]{1,0:T(8,128)S(1)} %get-tuple-element.34.up), channel_id=1, source_target_pairs={{0,224},{32,0},{64,32},{96,64},{128,96},{160,128},{192,160},{224,1... | collective-permute-start | bytes 442376 | tf_op jit(solution)/shard_map/ppermute | solution.py:870
  8.4 3.5 %collective-permute-done.above = f32[288,128]{1,0:T(8,128)S(1)} collective-permute-done((f32[288,128]{1,0:T(8,128)S(1)}, f32[288,128]{1,0:T(8,128)S(1)}, u32[]{:S(2)}, u32[]{:S(2)}) %collective-permute-start) | collective-permute-done | bytes 147488 | tf_op jit(solution)/shard_map/ppermute | solution.py:869
  11.8 0.0 collective-permute-done.1.below
  11.8 0.5 shard_map.52
  12.3 1.3 %collective-permute-start.2 = (f32[456,128]{1,0:T(8,128)S(1)}, f32[456,128]{1,0:T(8,128)S(1)}, u32[]{:S(2)}, u32[]{:S(2)}) collective-permute-start(f32[456,128]{1,0:T(8,128)S(1)} %get-tuple-element.37), channel_id=1, source_target_pairs={{0,1},{1,0},{2,3},{3,2},{4,5},{5,4},{6,7},{7,6},{8,9},{9,8},{10,11... | collective-permute-start | bytes 700424 | tf_op jit(solution)/shard_map/ppermute | solution.py:878
  13.6 3.0 %collective-permute-start.3 = (f32[456,128]{1,0:T(8,128)S(1)}, f32[456,128]{1,0:T(8,128)S(1)}, u32[]{:S(2)}, u32[]{:S(2)}) collective-permute-start(f32[456,128]{1,0:T(8,128)S(1)} %get-tuple-element.38), channel_id=1, source_target_pairs={{0,0},{1,2},{2,1},{3,4},{4,3},{5,6},{6,5},{7,8},{8,7},{9,10},{10,9... | collective-permute-start | bytes 700424 | tf_op jit(solution)/shard_map/ppermute | solution.py:880
  16.6 0.0 collective-permute-done.2.swapped
  16.7 4.3 %collective-permute-done.3.sided = f32[456,128]{1,0:T(8,128)S(1)} collective-permute-done((f32[456,128]{1,0:T(8,128)S(1)}, f32[456,128]{1,0:T(8,128)S(1)}, u32[]{:S(2)}, u32[]{:S(2)}) %collective-permute-start.3) | collective-permute-done | bytes 233504 | tf_op jit(solution)/shard_map/ppermute | solution.py:880
  21.0 2.3 %shard_map.53 = (f32[5,2,208,128]{3,2,1,0:T(8,128)S(1)}, f32[6,2,112,128]{3,2,1,0:T(8,128)S(1)}, f32[6,2,64,128]{3,2,1,0:T(8,128)S(1)}, f32[3,2,208,128]{3,2,1,0...) custom-call(f32[5,64,128]{2,1,0:T(8,128)S(1)} %get-tuple-element.35., ...), custom_call_target="tpu_custom_call" | custom-call | bytes 8000000 | tf_op jit(solution)/shard_map/pallas_call | solution.py:834
  23.3 31.6 %all_to_all.10 = f32[128,1,768]{2,1,0:T(1,128)S(1)} all-to-all(f32[128,1,768]{2,1,0:T(1,128)S(1)} %bitcast.8), channel_id=1, replica_groups=mesh['z'=8,'y'=4,'x'=4,'core'=2] {'y','x','z'}, dimensions={0} | all-to-all | bytes 786432 | tf_op jit(solution)/shard_map/all_to_all | solution.py:850
  54.9 0.0 collective-permute-start.4
  54.9 1.7 %collective-permute-done.4.other = f32[768,128]{1,0:T(8,128)S(1)} collective-permute-done((f32[768,128]{1,0:T(8,128)S(1)}, f32[768,128]{1,0:T(8,128)S(1)}, u32[]{:S(2)}, u32[]{:S(2)}) %collective-permute-start.4) | collective-permute-done | bytes 393248 | tf_op jit(solution)/shard_map/ppermute | solution.py:852
  56.6 7.1 %shard_map.54 = (f32[6,6,80,128]{3,2,1,0:T(8,128)S(1)}, f32[6,2,48,128]{3,2,1,0:T(8,128)S(1)}, f32[6,1,32,128]{3,2,1,0:T(8,128)S(1)}, f32[6,1,24,128]{3,2,1,0:T(...) custom-call(f32[768,128]{1,0:T(8,128)S(1)} %bitcast.5, ...), custom_call_target="tpu_custom_call" | custom-call | bytes 8000000 | tf_op jit(solution)/shard_map/pallas_call | solution.py:834
  63.7 18.9 %all_to_all.11 = f32[128,1,384]{2,1,0:T(1,128)S(1)} all-to-all(f32[128,1,384]{2,1,0:T(1,128)S(1)} %bitcast.9), channel_id=1, replica_groups=mesh['z'=8,'y'=4,'x'=4,'core'=2] {'y','x','z'}, dimensions={0} | all-to-all | bytes 393216 | tf_op jit(solution)/shard_map/all_to_all | solution.py:850
  82.6 1.4 %collective-permute-start.5 = (f32[384,128]{1,0:T(8,128)S(1)}, f32[384,128]{1,0:T(8,128)S(1)}, u32[]{:S(2)}, u32[]{:S(2)}) collective-permute-start(f32[384,128]{1,0:T(8,128)S(1)} %bitcast.6), channel_id=1, source_target_pairs={{0,1},{1,0},{2,3},{3,2},{4,5},{5,4},{6,7},{7,6},{8,9},{9,8},{10,11... | collective-permute-start | bytes 589832 | tf_op jit(solution)/shard_map/ppermute | solution.py:852
  84.0 1.1 %collective-permute-done.5.other = f32[384,128]{1,0:T(8,128)S(1)} collective-permute-done((f32[384,128]{1,0:T(8,128)S(1)}, f32[384,128]{1,0:T(8,128)S(1)}, u32[]{:S(2)}, u32[]{:S(2)}) %collective-permute-start.5) | collective-permute-done | bytes 196640 | tf_op jit(solution)/shard_map/ppermute | solution.py:852
  85.1 5.2 %shard_map.55 = (f32[3,64,128]{2,1,0:T(8,128)}, f32[3,64,128]{2,1,0:T(8,128)}) custom-call(f32[384,128]{1,0:T(8,128)S(1)} %bitcast.7, f32[384,128]{1,0:T(8,128)S(1)} %collective-permute-done.5.other, f32[5,2,208,128]{3,2,1,0:T(8,128)S(1)} %get-tuple-element.41.m0, f32[6,2,112,128]{3,2,1,0:T(8,128)S(1)} %get-tuple-element.42.m1, ...), custom_call_target="tpu_custom_call" | custom-call | bytes 8000000 | tf_op jit(solution)/shard_map/pallas_call | solution.py:834
  (1 shorter events, 0.0 us)
Async XLA Ops:
  1.8 10.1 %collective-permute-start = (f32[288,128]{1,0:T(8,128)S(1)}, f32[288,128]{1,0:T(8,128)S(1)}, u32[]{:S(2)}, u32[]{:S(2)}) collective-permute-start(f32[288,128]{1,0:T(8,128)S(1)} %get-tuple-element.33.down), channel_id=1, source_target_pairs={{0,32},{32,64},{64,96},{96,128},{128,160},{160,192},{192,224},{224... | collective-permute-start | bytes 442376 | tf_op jit(solution)/shard_map/ppermute | solution.py:869
  4.3 7.5 %collective-permute-start.1 = (f32[288,128]{1,0:T(8,128)S(1)}, f32[288,128]{1,0:T(8,128)S(1)}, u32[]{:S(2)}, u32[]{:S(2)}) collective-permute-start(f32[288,128]{1,0:T(8,128)S(1)} %get-tuple-element.34.up), channel_id=1, source_target_pairs={{0,224},{32,0},{64,32},{96,64},{128,96},{160,128},{192,160},{224,1... | collective-permute-start | bytes 442376 | tf_op jit(solution)/shard_map/ppermute | solution.py:870
  12.3 4.3 %collective-permute-start.2 = (f32[456,128]{1,0:T(8,128)S(1)}, f32[456,128]{1,0:T(8,128)S(1)}, u32[]{:S(2)}, u32[]{:S(2)}) collective-permute-start(f32[456,128]{1,0:T(8,128)S(1)} %get-tuple-element.37), channel_id=1, source_target_pairs={{0,1},{1,0},{2,3},{3,2},{4,5},{5,4},{6,7},{7,6},{8,9},{9,8},{10,11... | collective-permute-start | bytes 700424 | tf_op jit(solution)/shard_map/ppermute | solution.py:878
  13.6 7.4 %collective-permute-start.3 = (f32[456,128]{1,0:T(8,128)S(1)}, f32[456,128]{1,0:T(8,128)S(1)}, u32[]{:S(2)}, u32[]{:S(2)}) collective-permute-start(f32[456,128]{1,0:T(8,128)S(1)} %get-tuple-element.38), channel_id=1, source_target_pairs={{0,0},{1,2},{2,1},{3,4},{4,3},{5,6},{6,5},{7,8},{8,7},{9,10},{10,9... | collective-permute-start | bytes 700424 | tf_op jit(solution)/shard_map/ppermute | solution.py:880
  54.9 1.7 %collective-permute-start.4 = (f32[768,128]{1,0:T(8,128)S(1)}, f32[768,128]{1,0:T(8,128)S(1)}, u32[]{:S(2)}, u32[]{:S(2)}) collective-permute-start(f32[768,128]{1,0:T(8,128)S(1)} %bitcast.4), channel_id=1, source_target_pairs={{0,1},{1,0},{2,3},{3,2},{4,5},{5,4},{6,7},{7,6},{8,9},{9,8},{10,11... | collective-permute-start | bytes 1179656 | tf_op jit(solution)/shard_map/ppermute | solution.py:852
  82.6 2.5 %collective-permute-start.5 = (f32[384,128]{1,0:T(8,128)S(1)}, f32[384,128]{1,0:T(8,128)S(1)}, u32[]{:S(2)}, u32[]{:S(2)}) collective-permute-start(f32[384,128]{1,0:T(8,128)S(1)} %bitcast.6), channel_id=1, source_target_pairs={{0,1},{1,0},{2,3},{3,2},{4,5},{5,4},{6,7},{7,6},{8,9},{9,8},{10,11... | collective-permute-start | bytes 589832 | tf_op jit(solution)/shard_map/ppermute | solution.py:852
